TPU v7x, 512 devices: a whole 4x4x16 slice. The times are simulated.
512 devices in a mesh: rep: 4 (over y), ctx: 16 (over x, z_hi, core), tp: 8 (over z_lo).
Axes of the slice: x: 4, y: 4, z: 16 (z_hi: 2, z_lo: 8; z = z_hi * 8 + z_lo), core: 2. Of those that a mesh axis runs over, the one named last changes fastest.
Arguments:
- queries: bfloat16 [8, 512, 8192], P('rep', 'ctx', 'tp'), parts along dimension 0, may hold values from -200 to 200
- cache_keys: bfloat16 [8, 16384, 1024], P('rep', 'ctx', 'tp'), parts along dimension 0, may hold values from -8.1 to 8.1
- stored_values: bfloat16 [8, 16384, 1024], P('rep', 'ctx', 'tp'), parts along dimension 0, may hold values from -6 to 6
- rotated_new_keys: bfloat16 [8, 512, 1024], P('rep', 'ctx', 'tp'), parts along dimension 0, may hold values from -6 to 6
- incoming_values: bfloat16 [8, 512, 1024], P('rep', 'ctx', 'tp'), parts along dimension 0, may hold values from -6 to 6
- lengths: int32 [8], P('rep'), parts along dimension 0, may hold values from 8192 to 16384, as said below
- positions: int32 [8, 512], P('rep', 'ctx'), parts along dimension 0, may hold values from 8192 to 16895, as said below
Outputs:
- attended: bfloat16 [8, 512, 8192], P('rep', 'ctx', 'tp'), parts along dimension 0
There are 4 independent parts, one for each index of `rep`. A program takes and returns all parts, laid end to end along the dimension named above; each array names one. Nothing has to cross between parts.
Inputs may be any that keep to these rules, and one draw needn't show every extreme that they name: `lengths`: one session of each part has all 16384 slots used. `positions`: along each session nondecreasing, the first equal to that session's entry of lengths, each next one equal or one more; a session with all 16384 slots used rises by one at every token.
All inputs are finite; a program needn't handle non-finite values.
Results may differ from a plain program's by a relative error of at most 0.0075.
Values may be sent and summed in bfloat16 or wider, within the bound.
No kernel may reach another device: no remote copies, remote signals or barrier semaphores. Data moves between devices by JAX's collectives and lax.ppermute only.
A program may use at most 64 MiB of HBM per device.

v0:
```python
import jax
import jax.numpy as jnp
from jax import lax
from jax.sharding import PartitionSpec as P

HEAD_SIZE = 128


NEG = -1e30


def shifted(block, axis, distance):
    devices = range(lax.axis_size(axis))
    route = [((i - distance) % len(devices), i) for i in devices]
    return lax.ppermute(block, axis, route)


def partial_attend(block, joined_keys, values, mask):
    session_index, rows, width = block.shape
    kv_heads = joined_keys.shape[2] // HEAD_SIZE
    query_group = width // (kv_heads * HEAD_SIZE)
    query_view = block.reshape(session_index, rows, kv_heads, query_group, HEAD_SIZE)
    key_view = joined_keys.reshape(session_index, joined_keys.shape[1], kv_heads, HEAD_SIZE)
    value_view = values.reshape(session_index, values.shape[1], kv_heads, HEAD_SIZE)
    scores = jnp.einsum(
        "sqhgd,skhd->sqhgk", query_view, key_view, preferred_element_type=jnp.float32
    )
    scores = scores * (1.0 / HEAD_SIZE**0.5)
    top = jnp.max(jnp.where(mask, scores, NEG), axis=-1)
    weights = jnp.where(mask, jnp.exp(scores - top[..., None]), 0.0)
    total = jnp.sum(weights, axis=-1)
    summed = jnp.einsum(
        "sqhgk,skhd->sqhgd",
        weights.astype(jnp.bfloat16),
        value_view,
        preferred_element_type=jnp.float32,
    )
    return (
        summed.reshape(session_index, rows, width),
        top.reshape(session_index, rows, kv_heads * query_group),
        total.reshape(session_index, rows, kv_heads * query_group),
    )


def scale_heads(summed, factor):
    shaped = summed.reshape(factor.shape + (summed.shape[-1] // factor.shape[-1],))
    return (shaped * factor[..., None]).reshape(summed.shape)


def combine(first, second):
    top = jnp.maximum(first[1], second[1])
    left = jnp.exp(first[1] - top)
    right = jnp.exp(second[1] - top)
    summed = scale_heads(first[0], left) + scale_heads(second[0], right)
    return (summed, top, first[2] * left + second[2] * right)


def per_device(
    queries, cache_keys, stored_values, rotated_new_keys, incoming_values, lengths, positions
):
    member = lax.axis_index("ctx")
    count = lax.axis_size("ctx")
    cache_len = cache_keys.shape[1]
    slots = member * cache_len + jnp.arange(cache_len, dtype=jnp.int32)
    cache_mask = (slots[None, :] < lengths[:, None])[:, None, None, None, :]

    def cache_part(block):
        return partial_attend(block, cache_keys, stored_values, cache_mask)

    session_index, rows, width = queries.shape
    head_cols = width // HEAD_SIZE
    start_state = (
        jnp.zeros((session_index, rows, width), jnp.float32),
        jnp.full((session_index, rows, head_cols), NEG, jnp.float32),
        jnp.zeros((session_index, rows, head_cols), jnp.float32),
    )
    piece_keys = lax.all_gather(rotated_new_keys, "ctx", axis=1, tiled=True)
    piece_values = lax.all_gather(incoming_values, "ctx", axis=1, tiled=True)
    piece_pos = lax.all_gather(positions, "ctx", axis=1, tiled=True)
    mask = (piece_pos[:, None, :] <= positions[:, :, None])[:, :, None, None, :]
    fresh = combine(start_state, partial_attend(queries, piece_keys, piece_values, mask))

    def carry_partial(state):
        return shifted((state[0], state[1], state[2]), "ctx", 1)

    def visit(step, state):
        block, carried = state
        block = shifted(block, "ctx", 1)
        carried = carry_partial(carried)
        return (block, combine(carried, cache_part(block)))

    block, carried = lax.fori_loop(1, count, visit, (queries, cache_part(queries)))
    gathered = carry_partial(carried)
    summed, top, total = combine(gathered, fresh)
    return scale_heads(summed, 1.0 / total).astype(jnp.bfloat16)


def solution(mesh):
    in_specs = (
        P("rep", "ctx", "tp"),
        P("rep", "ctx", "tp"),
        P("rep", "ctx", "tp"),
        P("rep", "ctx", "tp"),
        P("rep", "ctx", "tp"),
        P("rep"),
        P("rep", "ctx"),
    )
    out_specs = P("rep", "ctx", "tp")
    return jax.shard_map(
        per_device, mesh=mesh, in_specs=in_specs, out_specs=out_specs, check_vma=False
    )
```

profile of v0, /device:TPU:169, one launch (start us, length us, event | category | flops | bytes accessed | tf_op | source)
XLA Modules:
  0.0 670.7 jit_solution(15545717015487295101)
XLA Ops:
  4.1 519.7 %while.17 = (s32[]{:T(128)}, bf16[2,32,1024]{2,1,0:T(8,128)(2,1)S(1)}, f32[2,32,1024]{2,1,0:T(8,128)S(1)}, f32[2,32,8]{1,2,0:T(8,128)S(1)}, f32[2,32,8]{1,2,0:T(...) while((s32[]{:T(128)}, ...), condition=%wide.region_5.6_spmd.clone, body=%wide.region_2.0_spmd.clone.sunk | while | flops 274403328 | bytes 13566221 | solution.py:92
  4.1 10.4 %collective-permute-start.1 = (f32[2,32,8]{1,2,0:T(8,128)S(1)}, f32[2,32,8]{1,2,0:T(8,128)S(1)}, u32[]{:S(2)}, u32[]{:S(2)}) collective-permute-start(f32[2,32,8]{1,2,0:T(8,128)S(1)} %get-tuple-element.193), channel_id=1, source_target_pairs={{120,0},{0,8},{8,16},{16,24},{24,32},{32,40},{40,48},{48,56},{56,6... | collective-permute-start | bytes 6152 | tf_op jit(solution)/shard_map/while/body/eval_jaxpr/ppermute | solution.py:15
  16.5 5.6 collective-permute-start
  26.6 7.3 %collective-permute-done.3 = f32[2,32,1024]{2,1,0:T(8,128)S(1)} collective-permute-done((f32[2,32,1024]{2,1,0:T(8,128)S(1)}, f32[2,32,1024]{2,1,0:T(8,128)S(1)}, u32[]{:S(2)}, u32[]{:S(2)}) %collective-permute-start.3) | collective-permute-done | bytes 262176 | tf_op jit(solution)/shard_map/while/body/eval_jaxpr/ppermute | solution.py:15
  34.0 13.3 %collective-permute-start.1 = (f32[2,32,8]{1,2,0:T(8,128)S(1)}, f32[2,32,8]{1,2,0:T(8,128)S(1)}, u32[]{:S(2)}, u32[]{:S(2)}) collective-permute-start(f32[2,32,8]{1,2,0:T(8,128)S(1)} %get-tuple-element.193), channel_id=1, source_target_pairs={{120,0},{0,8},{8,16},{16,24},{24,32},{32,40},{40,48},{48,56},{56,6... | collective-permute-start | bytes 6152 | tf_op jit(solution)/shard_map/while/body/eval_jaxpr/ppermute | solution.py:15
  49.2 13.1 %collective-permute-start = (bf16[2,32,1024]{2,1,0:T(8,128)(2,1)S(1)}, bf16[2,32,1024]{2,1,0:T(8,128)(2,1)S(1)}, u32[]{:S(2)}, u32[]{:S(2)}) collective-permute-start(bf16[2,32,1024]{2,1,0:T(8,128)(2,1)S(1)} %get-tuple-element.190), channel_id=1, source_target_pairs={{120,0},{0,8},{8,16},{16,24},{24,32},{32,40},{40,48},{48,56},{56,6... | collective-permute-start | bytes 393224 | tf_op jit(solution)/shard_map/while/body/eval_jaxpr/ppermute | solution.py:15
  66.9 4.9 collective-permute-done.3
  71.9 13.2 %collective-permute-start.1 = (f32[2,32,8]{1,2,0:T(8,128)S(1)}, f32[2,32,8]{1,2,0:T(8,128)S(1)}, u32[]{:S(2)}, u32[]{:S(2)}) collective-permute-start(f32[2,32,8]{1,2,0:T(8,128)S(1)} %get-tuple-element.193), channel_id=1, source_target_pairs={{120,0},{0,8},{8,16},{16,24},{24,32},{32,40},{40,48},{48,56},{56,6... | collective-permute-start | bytes 6152 | tf_op jit(solution)/shard_map/while/body/eval_jaxpr/ppermute | solution.py:15
  87.0 3.5 collective-permute-start
  92.5 3.3 collective-permute-done
  98.7 13.1 %collective-permute-start.1 = (f32[2,32,8]{1,2,0:T(8,128)S(1)}, f32[2,32,8]{1,2,0:T(8,128)S(1)}, u32[]{:S(2)}, u32[]{:S(2)}) collective-permute-start(f32[2,32,8]{1,2,0:T(8,128)S(1)} %get-tuple-element.193), channel_id=1, source_target_pairs={{120,0},{0,8},{8,16},{16,24},{24,32},{32,40},{40,48},{48,56},{56,6... | collective-permute-start | bytes 6152 | tf_op jit(solution)/shard_map/while/body/eval_jaxpr/ppermute | solution.py:15
  113.8 13.0 %collective-permute-start = (bf16[2,32,1024]{2,1,0:T(8,128)(2,1)S(1)}, bf16[2,32,1024]{2,1,0:T(8,128)(2,1)S(1)}, u32[]{:S(2)}, u32[]{:S(2)}) collective-permute-start(bf16[2,32,1024]{2,1,0:T(8,128)(2,1)S(1)} %get-tuple-element.190), channel_id=1, source_target_pairs={{120,0},{0,8},{8,16},{16,24},{24,32},{32,40},{40,48},{48,56},{56,6... | collective-permute-start | bytes 393224 | tf_op jit(solution)/shard_map/while/body/eval_jaxpr/ppermute | solution.py:15
  132.9 14.6 %collective-permute-start.1 = (f32[2,32,8]{1,2,0:T(8,128)S(1)}, f32[2,32,8]{1,2,0:T(8,128)S(1)}, u32[]{:S(2)}, u32[]{:S(2)}) collective-permute-start(f32[2,32,8]{1,2,0:T(8,128)S(1)} %get-tuple-element.193), channel_id=1, source_target_pairs={{120,0},{0,8},{8,16},{16,24},{24,32},{32,40},{40,48},{48,56},{56,6... | collective-permute-start | bytes 6152 | tf_op jit(solution)/shard_map/while/body/eval_jaxpr/ppermute | solution.py:15
  149.4 10.1 %collective-permute-start = (bf16[2,32,1024]{2,1,0:T(8,128)(2,1)S(1)}, bf16[2,32,1024]{2,1,0:T(8,128)(2,1)S(1)}, u32[]{:S(2)}, u32[]{:S(2)}) collective-permute-start(bf16[2,32,1024]{2,1,0:T(8,128)(2,1)S(1)} %get-tuple-element.190), channel_id=1, source_target_pairs={{120,0},{0,8},{8,16},{16,24},{24,32},{32,40},{40,48},{48,56},{56,6... | collective-permute-start | bytes 393224 | tf_op jit(solution)/shard_map/while/body/eval_jaxpr/ppermute | solution.py:15
  159.5 3.3 collective-permute-start.3
  166.3 13.3 %collective-permute-start.1 = (f32[2,32,8]{1,2,0:T(8,128)S(1)}, f32[2,32,8]{1,2,0:T(8,128)S(1)}, u32[]{:S(2)}, u32[]{:S(2)}) collective-permute-start(f32[2,32,8]{1,2,0:T(8,128)S(1)} %get-tuple-element.193), channel_id=1, source_target_pairs={{120,0},{0,8},{8,16},{16,24},{24,32},{32,40},{40,48},{48,56},{56,6... | collective-permute-start | bytes 6152 | tf_op jit(solution)/shard_map/while/body/eval_jaxpr/ppermute | solution.py:15
  179.6 7.5 %collective-permute-start.2 = (f32[2,32,8]{1,2,0:T(8,128)S(1)}, f32[2,32,8]{1,2,0:T(8,128)S(1)}, u32[]{:S(2)}, u32[]{:S(2)}) collective-permute-start(f32[2,32,8]{1,2,0:T(8,128)S(1)} %get-tuple-element.192), channel_id=1, source_target_pairs={{120,0},{0,8},{8,16},{16,24},{24,32},{32,40},{40,48},{48,56},{56,6... | collective-permute-start | bytes 6152 | tf_op jit(solution)/shard_map/while/body/eval_jaxpr/ppermute | solution.py:15
  187.2 14.1 %collective-permute-start = (bf16[2,32,1024]{2,1,0:T(8,128)(2,1)S(1)}, bf16[2,32,1024]{2,1,0:T(8,128)(2,1)S(1)}, u32[]{:S(2)}, u32[]{:S(2)}) collective-permute-start(bf16[2,32,1024]{2,1,0:T(8,128)(2,1)S(1)} %get-tuple-element.190), channel_id=1, source_target_pairs={{120,0},{0,8},{8,16},{16,24},{24,32},{32,40},{40,48},{48,56},{56,6... | collective-permute-start | bytes 393224 | tf_op jit(solution)/shard_map/while/body/eval_jaxpr/ppermute | solution.py:15
  206.7 13.8 %collective-permute-start.1 = (f32[2,32,8]{1,2,0:T(8,128)S(1)}, f32[2,32,8]{1,2,0:T(8,128)S(1)}, u32[]{:S(2)}, u32[]{:S(2)}) collective-permute-start(f32[2,32,8]{1,2,0:T(8,128)S(1)} %get-tuple-element.193), channel_id=1, source_target_pairs={{120,0},{0,8},{8,16},{16,24},{24,32},{32,40},{40,48},{48,56},{56,6... | collective-permute-start | bytes 6152 | tf_op jit(solution)/shard_map/while/body/eval_jaxpr/ppermute | solution.py:15
  222.4 10.6 %collective-permute-start = (bf16[2,32,1024]{2,1,0:T(8,128)(2,1)S(1)}, bf16[2,32,1024]{2,1,0:T(8,128)(2,1)S(1)}, u32[]{:S(2)}, u32[]{:S(2)}) collective-permute-start(bf16[2,32,1024]{2,1,0:T(8,128)(2,1)S(1)} %get-tuple-element.190), channel_id=1, source_target_pairs={{120,0},{0,8},{8,16},{16,24},{24,32},{32,40},{40,48},{48,56},{56,6... | collective-permute-start | bytes 393224 | tf_op jit(solution)/shard_map/while/body/eval_jaxpr/ppermute | solution.py:15
  239.0 13.2 %collective-permute-start.1 = (f32[2,32,8]{1,2,0:T(8,128)S(1)}, f32[2,32,8]{1,2,0:T(8,128)S(1)}, u32[]{:S(2)}, u32[]{:S(2)}) collective-permute-start(f32[2,32,8]{1,2,0:T(8,128)S(1)} %get-tuple-element.193), channel_id=1, source_target_pairs={{120,0},{0,8},{8,16},{16,24},{24,32},{32,40},{40,48},{48,56},{56,6... | collective-permute-start | bytes 6152 | tf_op jit(solution)/shard_map/while/body/eval_jaxpr/ppermute | solution.py:15
  252.1 10.0 %collective-permute-start.2 = (f32[2,32,8]{1,2,0:T(8,128)S(1)}, f32[2,32,8]{1,2,0:T(8,128)S(1)}, u32[]{:S(2)}, u32[]{:S(2)}) collective-permute-start(f32[2,32,8]{1,2,0:T(8,128)S(1)} %get-tuple-element.192), channel_id=1, source_target_pairs={{120,0},{0,8},{8,16},{16,24},{24,32},{32,40},{40,48},{48,56},{56,6... | collective-permute-start | bytes 6152 | tf_op jit(solution)/shard_map/while/body/eval_jaxpr/ppermute | solution.py:15
  262.1 14.0 %collective-permute-start = (bf16[2,32,1024]{2,1,0:T(8,128)(2,1)S(1)}, bf16[2,32,1024]{2,1,0:T(8,128)(2,1)S(1)}, u32[]{:S(2)}, u32[]{:S(2)}) collective-permute-start(bf16[2,32,1024]{2,1,0:T(8,128)(2,1)S(1)} %get-tuple-element.190), channel_id=1, source_target_pairs={{120,0},{0,8},{8,16},{16,24},{24,32},{32,40},{40,48},{48,56},{56,6... | collective-permute-start | bytes 393224 | tf_op jit(solution)/shard_map/while/body/eval_jaxpr/ppermute | solution.py:15
  280.7 6.7 %collective-permute-done.3 = f32[2,32,1024]{2,1,0:T(8,128)S(1)} collective-permute-done((f32[2,32,1024]{2,1,0:T(8,128)S(1)}, f32[2,32,1024]{2,1,0:T(8,128)S(1)}, u32[]{:S(2)}, u32[]{:S(2)}) %collective-permute-start.3) | collective-permute-done | bytes 262176 | tf_op jit(solution)/shard_map/while/body/eval_jaxpr/ppermute | solution.py:15
  287.5 13.1 %collective-permute-start.1 = (f32[2,32,8]{1,2,0:T(8,128)S(1)}, f32[2,32,8]{1,2,0:T(8,128)S(1)}, u32[]{:S(2)}, u32[]{:S(2)}) collective-permute-start(f32[2,32,8]{1,2,0:T(8,128)S(1)} %get-tuple-element.193), channel_id=1, source_target_pairs={{120,0},{0,8},{8,16},{16,24},{24,32},{32,40},{40,48},{48,56},{56,6... | collective-permute-start | bytes 6152 | tf_op jit(solution)/shard_map/while/body/eval_jaxpr/ppermute | solution.py:15
  302.6 5.6 collective-permute-start
  310.2 3.9 collective-permute-done
  317.1 13.2 %collective-permute-start.1 = (f32[2,32,8]{1,2,0:T(8,128)S(1)}, f32[2,32,8]{1,2,0:T(8,128)S(1)}, u32[]{:S(2)}, u32[]{:S(2)}) collective-permute-start(f32[2,32,8]{1,2,0:T(8,128)S(1)} %get-tuple-element.193), channel_id=1, source_target_pairs={{120,0},{0,8},{8,16},{16,24},{24,32},{32,40},{40,48},{48,56},{56,6... | collective-permute-start | bytes 6152 | tf_op jit(solution)/shard_map/while/body/eval_jaxpr/ppermute | solution.py:15
  332.2 12.9 %collective-permute-start = (bf16[2,32,1024]{2,1,0:T(8,128)(2,1)S(1)}, bf16[2,32,1024]{2,1,0:T(8,128)(2,1)S(1)}, u32[]{:S(2)}, u32[]{:S(2)}) collective-permute-start(bf16[2,32,1024]{2,1,0:T(8,128)(2,1)S(1)} %get-tuple-element.190), channel_id=1, source_target_pairs={{120,0},{0,8},{8,16},{16,24},{24,32},{32,40},{40,48},{48,56},{56,6... | collective-permute-start | bytes 393224 | tf_op jit(solution)/shard_map/while/body/eval_jaxpr/ppermute | solution.py:15
  349.7 3.2 collective-permute-done.3
  352.9 13.1 %collective-permute-start.1 = (f32[2,32,8]{1,2,0:T(8,128)S(1)}, f32[2,32,8]{1,2,0:T(8,128)S(1)}, u32[]{:S(2)}, u32[]{:S(2)}) collective-permute-start(f32[2,32,8]{1,2,0:T(8,128)S(1)} %get-tuple-element.193), channel_id=1, source_target_pairs={{120,0},{0,8},{8,16},{16,24},{24,32},{32,40},{40,48},{48,56},{56,6... | collective-permute-start | bytes 6152 | tf_op jit(solution)/shard_map/while/body/eval_jaxpr/ppermute | solution.py:15
  368.0 4.4 collective-permute-start
  378.4 13.3 %collective-permute-start.1 = (f32[2,32,8]{1,2,0:T(8,128)S(1)}, f32[2,32,8]{1,2,0:T(8,128)S(1)}, u32[]{:S(2)}, u32[]{:S(2)}) collective-permute-start(f32[2,32,8]{1,2,0:T(8,128)S(1)} %get-tuple-element.193), channel_id=1, source_target_pairs={{120,0},{0,8},{8,16},{16,24},{24,32},{32,40},{40,48},{48,56},{56,6... | collective-permute-start | bytes 6152 | tf_op jit(solution)/shard_map/while/body/eval_jaxpr/ppermute | solution.py:15
  393.7 10.2 %collective-permute-start = (bf16[2,32,1024]{2,1,0:T(8,128)(2,1)S(1)}, bf16[2,32,1024]{2,1,0:T(8,128)(2,1)S(1)}, u32[]{:S(2)}, u32[]{:S(2)}) collective-permute-start(bf16[2,32,1024]{2,1,0:T(8,128)(2,1)S(1)} %get-tuple-element.190), channel_id=1, source_target_pairs={{120,0},{0,8},{8,16},{16,24},{24,32},{32,40},{40,48},{48,56},{56,6... | collective-permute-start | bytes 393224 | tf_op jit(solution)/shard_map/while/body/eval_jaxpr/ppermute | solution.py:15
  408.5 4.2 collective-permute-done.3
  412.8 13.3 %collective-permute-start.1 = (f32[2,32,8]{1,2,0:T(8,128)S(1)}, f32[2,32,8]{1,2,0:T(8,128)S(1)}, u32[]{:S(2)}, u32[]{:S(2)}) collective-permute-start(f32[2,32,8]{1,2,0:T(8,128)S(1)} %get-tuple-element.193), channel_id=1, source_target_pairs={{120,0},{0,8},{8,16},{16,24},{24,32},{32,40},{40,48},{48,56},{56,6... | collective-permute-start | bytes 6152 | tf_op jit(solution)/shard_map/while/body/eval_jaxpr/ppermute | solution.py:15
  428.0 12.7 %collective-permute-start = (bf16[2,32,1024]{2,1,0:T(8,128)(2,1)S(1)}, bf16[2,32,1024]{2,1,0:T(8,128)(2,1)S(1)}, u32[]{:S(2)}, u32[]{:S(2)}) collective-permute-start(bf16[2,32,1024]{2,1,0:T(8,128)(2,1)S(1)} %get-tuple-element.190), channel_id=1, source_target_pairs={{120,0},{0,8},{8,16},{16,24},{24,32},{32,40},{40,48},{48,56},{56,6... | collective-permute-start | bytes 393224 | tf_op jit(solution)/shard_map/while/body/eval_jaxpr/ppermute | solution.py:15
  448.1 13.3 %collective-permute-start.1 = (f32[2,32,8]{1,2,0:T(8,128)S(1)}, f32[2,32,8]{1,2,0:T(8,128)S(1)}, u32[]{:S(2)}, u32[]{:S(2)}) collective-permute-start(f32[2,32,8]{1,2,0:T(8,128)S(1)} %get-tuple-element.193), channel_id=1, source_target_pairs={{120,0},{0,8},{8,16},{16,24},{24,32},{32,40},{40,48},{48,56},{56,6... | collective-permute-start | bytes 6152 | tf_op jit(solution)/shard_map/while/body/eval_jaxpr/ppermute | solution.py:15
  463.4 12.7 %collective-permute-start = (bf16[2,32,1024]{2,1,0:T(8,128)(2,1)S(1)}, bf16[2,32,1024]{2,1,0:T(8,128)(2,1)S(1)}, u32[]{:S(2)}, u32[]{:S(2)}) collective-permute-start(bf16[2,32,1024]{2,1,0:T(8,128)(2,1)S(1)} %get-tuple-element.190), channel_id=1, source_target_pairs={{120,0},{0,8},{8,16},{16,24},{24,32},{32,40},{40,48},{48,56},{56,6... | collective-permute-start | bytes 393224 | tf_op jit(solution)/shard_map/while/body/eval_jaxpr/ppermute | solution.py:15
  482.1 5.8 collective-permute-done.3
  488.0 13.3 %collective-permute-start.1 = (f32[2,32,8]{1,2,0:T(8,128)S(1)}, f32[2,32,8]{1,2,0:T(8,128)S(1)}, u32[]{:S(2)}, u32[]{:S(2)}) collective-permute-start(f32[2,32,8]{1,2,0:T(8,128)S(1)} %get-tuple-element.193), channel_id=1, source_target_pairs={{120,0},{0,8},{8,16},{16,24},{24,32},{32,40},{40,48},{48,56},{56,6... | collective-permute-start | bytes 6152 | tf_op jit(solution)/shard_map/while/body/eval_jaxpr/ppermute | solution.py:15
  503.2 5.7 collective-permute-start
  510.9 8.8 %collective-permute-done = bf16[2,32,1024]{2,1,0:T(8,128)(2,1)S(1)} collective-permute-done((bf16[2,32,1024]{2,1,0:T(8,128)(2,1)S(1)}, bf16[2,32,1024]{2,1,0:T(8,128)(2,1)S(1)}, u32[]{:S(2)}, u32[]{:S(2)}) %collective-permute-start) | collective-permute-done | bytes 131104 | tf_op jit(solution)/shard_map/while/body/eval_jaxpr/ppermute | solution.py:15
  523.8 13.2 %collective-permute-start.5 = (f32[2,32,8]{1,2,0:T(8,128)S(1)}, f32[2,32,8]{1,2,0:T(8,128)S(1)}, u32[]{:S(2)}, u32[]{:S(2)}) collective-permute-start(f32[2,32,8]{1,2,0:T(8,128)S(1)} %get-tuple-element.50), channel_id=1, source_target_pairs={{120,0},{0,8},{8,16},{16,24},{24,32},{32,40},{40,48},{48,56},{56,6... | collective-permute-start | bytes 6152 | tf_op jit(solution)/shard_map/ppermute | solution.py:15
  538.9 3.4 collective-permute-start.4
  542.4 43.6 %all-gather = s32[16,32,2]{1,2,0:T(2,128)S(1)} all-gather(s32[1,32,2]{1,2,0:T(2,128)S(1)} %bitcast.194), channel_id=1, replica_groups=mesh['rep'=4,'ctx'=16,'tp'=8] {'ctx'}, dimensions={0}, use_global_device_ids=true | all-gather | bytes 4352 | tf_op jit(solution)/shard_map/all_gather | solution.py:79
  586.2 39.3 %all_gather.10 = bf16[2,512,128]{2,1,0:T(8,128)(2,1)S(1)} all-gather(bf16[2,32,128]{2,1,0:T(8,128)(2,1)S(1)} %copy-done.4), channel_id=1, replica_groups=mesh['rep'=4,'ctx'=16,'tp'=8] {'ctx'}, dimensions={1}, use_global_device_ids=true | all-gather | bytes 278528 | tf_op jit(solution)/shard_map/all_gather | solution.py:77
  625.5 41.8 %all_gather.11 = bf16[2,512,128]{2,1,0:T(8,128)(2,1)S(1)} all-gather(bf16[2,32,128]{2,1,0:T(8,128)(2,1)S(1)} %copy-done.5), channel_id=1, replica_groups=mesh['rep'=4,'ctx'=16,'tp'=8] {'ctx'}, dimensions={1}, use_global_device_ids=true | all-gather | bytes 278528 | tf_op jit(solution)/shard_map/all_gather | solution.py:78
  (354 shorter events, 112.6 us)
Async XLA Ops:
  4.1 21.9 %collective-permute-start.1 = (f32[2,32,8]{1,2,0:T(8,128)S(1)}, f32[2,32,8]{1,2,0:T(8,128)S(1)}, u32[]{:S(2)}, u32[]{:S(2)}) collective-permute-start(f32[2,32,8]{1,2,0:T(8,128)S(1)} %get-tuple-element.193), channel_id=1, source_target_pairs={{120,0},{0,8},{8,16},{16,24},{24,32},{32,40},{40,48},{48,56},{56,6... | collective-permute-start | bytes 6152 | tf_op jit(solution)/shard_map/while/body/eval_jaxpr/ppermute | solution.py:15
  14.5 11.5 %collective-permute-start.2 = (f32[2,32,8]{1,2,0:T(8,128)S(1)}, f32[2,32,8]{1,2,0:T(8,128)S(1)}, u32[]{:S(2)}, u32[]{:S(2)}) collective-permute-start(f32[2,32,8]{1,2,0:T(8,128)S(1)} %get-tuple-element.192), channel_id=1, source_target_pairs={{120,0},{0,8},{8,16},{16,24},{24,32},{32,40},{40,48},{48,56},{56,6... | collective-permute-start | bytes 6152 | tf_op jit(solution)/shard_map/while/body/eval_jaxpr/ppermute | solution.py:15
  22.0 11.9 %collective-permute-start.3 = (f32[2,32,1024]{2,1,0:T(8,128)S(1)}, f32[2,32,1024]{2,1,0:T(8,128)S(1)}, u32[]{:S(2)}, u32[]{:S(2)}) collective-permute-start(f32[2,32,1024]{2,1,0:T(8,128)S(1)} %get-tuple-element.191), channel_id=1, source_target_pairs={{120,0},{0,8},{8,16},{16,24},{24,32},{32,40},{40,48},{48,56},{56,6... | collective-permute-start | bytes 786440 | tf_op jit(solution)/shard_map/while/body/eval_jaxpr/ppermute | solution.py:15
  34.0 32.3 %collective-permute-start.1 = (f32[2,32,8]{1,2,0:T(8,128)S(1)}, f32[2,32,8]{1,2,0:T(8,128)S(1)}, u32[]{:S(2)}, u32[]{:S(2)}) collective-permute-start(f32[2,32,8]{1,2,0:T(8,128)S(1)} %get-tuple-element.193), channel_id=1, source_target_pairs={{120,0},{0,8},{8,16},{16,24},{24,32},{32,40},{40,48},{48,56},{56,6... | collective-permute-start | bytes 6152 | tf_op jit(solution)/shard_map/while/body/eval_jaxpr/ppermute | solution.py:15
  47.2 19.1 %collective-permute-start.2 = (f32[2,32,8]{1,2,0:T(8,128)S(1)}, f32[2,32,8]{1,2,0:T(8,128)S(1)}, u32[]{:S(2)}, u32[]{:S(2)}) collective-permute-start(f32[2,32,8]{1,2,0:T(8,128)S(1)} %get-tuple-element.192), channel_id=1, source_target_pairs={{120,0},{0,8},{8,16},{16,24},{24,32},{32,40},{40,48},{48,56},{56,6... | collective-permute-start | bytes 6152 | tf_op jit(solution)/shard_map/while/body/eval_jaxpr/ppermute | solution.py:15
  49.2 15.2 %collective-permute-start = (bf16[2,32,1024]{2,1,0:T(8,128)(2,1)S(1)}, bf16[2,32,1024]{2,1,0:T(8,128)(2,1)S(1)}, u32[]{:S(2)}, u32[]{:S(2)}) collective-permute-start(bf16[2,32,1024]{2,1,0:T(8,128)(2,1)S(1)} %get-tuple-element.190), channel_id=1, source_target_pairs={{120,0},{0,8},{8,16},{16,24},{24,32},{32,40},{40,48},{48,56},{56,6... | collective-permute-start | bytes 393224 | tf_op jit(solution)/shard_map/while/body/eval_jaxpr/ppermute | solution.py:15
  71.9 25.8 %collective-permute-start.1 = (f32[2,32,8]{1,2,0:T(8,128)S(1)}, f32[2,32,8]{1,2,0:T(8,128)S(1)}, u32[]{:S(2)}, u32[]{:S(2)}) collective-permute-start(f32[2,32,8]{1,2,0:T(8,128)S(1)} %get-tuple-element.193), channel_id=1, source_target_pairs={{120,0},{0,8},{8,16},{16,24},{24,32},{32,40},{40,48},{48,56},{56,6... | collective-permute-start | bytes 6152 | tf_op jit(solution)/shard_map/while/body/eval_jaxpr/ppermute | solution.py:15
  85.1 12.6 %collective-permute-start.2 = (f32[2,32,8]{1,2,0:T(8,128)S(1)}, f32[2,32,8]{1,2,0:T(8,128)S(1)}, u32[]{:S(2)}, u32[]{:S(2)}) collective-permute-start(f32[2,32,8]{1,2,0:T(8,128)S(1)} %get-tuple-element.192), channel_id=1, source_target_pairs={{120,0},{0,8},{8,16},{16,24},{24,32},{32,40},{40,48},{48,56},{56,6... | collective-permute-start | bytes 6152 | tf_op jit(solution)/shard_map/while/body/eval_jaxpr/ppermute | solution.py:15
  98.7 33.0 %collective-permute-start.1 = (f32[2,32,8]{1,2,0:T(8,128)S(1)}, f32[2,32,8]{1,2,0:T(8,128)S(1)}, u32[]{:S(2)}, u32[]{:S(2)}) collective-permute-start(f32[2,32,8]{1,2,0:T(8,128)S(1)} %get-tuple-element.193), channel_id=1, source_target_pairs={{120,0},{0,8},{8,16},{16,24},{24,32},{32,40},{40,48},{48,56},{56,6... | collective-permute-start | bytes 6152 | tf_op jit(solution)/shard_map/while/body/eval_jaxpr/ppermute | solution.py:15
  111.8 19.9 %collective-permute-start.2 = (f32[2,32,8]{1,2,0:T(8,128)S(1)}, f32[2,32,8]{1,2,0:T(8,128)S(1)}, u32[]{:S(2)}, u32[]{:S(2)}) collective-permute-start(f32[2,32,8]{1,2,0:T(8,128)S(1)} %get-tuple-element.192), channel_id=1, source_target_pairs={{120,0},{0,8},{8,16},{16,24},{24,32},{32,40},{40,48},{48,56},{56,6... | collective-permute-start | bytes 6152 | tf_op jit(solution)/shard_map/while/body/eval_jaxpr/ppermute | solution.py:15
  113.8 16.0 %collective-permute-start = (bf16[2,32,1024]{2,1,0:T(8,128)(2,1)S(1)}, bf16[2,32,1024]{2,1,0:T(8,128)(2,1)S(1)}, u32[]{:S(2)}, u32[]{:S(2)}) collective-permute-start(bf16[2,32,1024]{2,1,0:T(8,128)(2,1)S(1)} %get-tuple-element.190), channel_id=1, source_target_pairs={{120,0},{0,8},{8,16},{16,24},{24,32},{32,40},{40,48},{48,56},{56,6... | collective-permute-start | bytes 393224 | tf_op jit(solution)/shard_map/while/body/eval_jaxpr/ppermute | solution.py:15
  132.9 32.0 %collective-permute-start.1 = (f32[2,32,8]{1,2,0:T(8,128)S(1)}, f32[2,32,8]{1,2,0:T(8,128)S(1)}, u32[]{:S(2)}, u32[]{:S(2)}) collective-permute-start(f32[2,32,8]{1,2,0:T(8,128)S(1)} %get-tuple-element.193), channel_id=1, source_target_pairs={{120,0},{0,8},{8,16},{16,24},{24,32},{32,40},{40,48},{48,56},{56,6... | collective-permute-start | bytes 6152 | tf_op jit(solution)/shard_map/while/body/eval_jaxpr/ppermute | solution.py:15
  147.5 17.4 %collective-permute-start.2 = (f32[2,32,8]{1,2,0:T(8,128)S(1)}, f32[2,32,8]{1,2,0:T(8,128)S(1)}, u32[]{:S(2)}, u32[]{:S(2)}) collective-permute-start(f32[2,32,8]{1,2,0:T(8,128)S(1)} %get-tuple-element.192), channel_id=1, source_target_pairs={{120,0},{0,8},{8,16},{16,24},{24,32},{32,40},{40,48},{48,56},{56,6... | collective-permute-start | bytes 6152 | tf_op jit(solution)/shard_map/while/body/eval_jaxpr/ppermute | solution.py:15
  149.4 13.5 %collective-permute-start = (bf16[2,32,1024]{2,1,0:T(8,128)(2,1)S(1)}, bf16[2,32,1024]{2,1,0:T(8,128)(2,1)S(1)}, u32[]{:S(2)}, u32[]{:S(2)}) collective-permute-start(bf16[2,32,1024]{2,1,0:T(8,128)(2,1)S(1)} %get-tuple-element.190), channel_id=1, source_target_pairs={{120,0},{0,8},{8,16},{16,24},{24,32},{32,40},{40,48},{48,56},{56,6... | collective-permute-start | bytes 393224 | tf_op jit(solution)/shard_map/while/body/eval_jaxpr/ppermute | solution.py:15
  166.3 38.9 %collective-permute-start.1 = (f32[2,32,8]{1,2,0:T(8,128)S(1)}, f32[2,32,8]{1,2,0:T(8,128)S(1)}, u32[]{:S(2)}, u32[]{:S(2)}) collective-permute-start(f32[2,32,8]{1,2,0:T(8,128)S(1)} %get-tuple-element.193), channel_id=1, source_target_pairs={{120,0},{0,8},{8,16},{16,24},{24,32},{32,40},{40,48},{48,56},{56,6... | collective-permute-start | bytes 6152 | tf_op jit(solution)/shard_map/while/body/eval_jaxpr/ppermute | solution.py:15
  179.6 25.6 %collective-permute-start.2 = (f32[2,32,8]{1,2,0:T(8,128)S(1)}, f32[2,32,8]{1,2,0:T(8,128)S(1)}, u32[]{:S(2)}, u32[]{:S(2)}) collective-permute-start(f32[2,32,8]{1,2,0:T(8,128)S(1)} %get-tuple-element.192), channel_id=1, source_target_pairs={{120,0},{0,8},{8,16},{16,24},{24,32},{32,40},{40,48},{48,56},{56,6... | collective-permute-start | bytes 6152 | tf_op jit(solution)/shard_map/while/body/eval_jaxpr/ppermute | solution.py:15
  187.2 16.1 %collective-permute-start = (bf16[2,32,1024]{2,1,0:T(8,128)(2,1)S(1)}, bf16[2,32,1024]{2,1,0:T(8,128)(2,1)S(1)}, u32[]{:S(2)}, u32[]{:S(2)}) collective-permute-start(bf16[2,32,1024]{2,1,0:T(8,128)(2,1)S(1)} %get-tuple-element.190), channel_id=1, source_target_pairs={{120,0},{0,8},{8,16},{16,24},{24,32},{32,40},{40,48},{48,56},{56,6... | collective-permute-start | bytes 393224 | tf_op jit(solution)/shard_map/while/body/eval_jaxpr/ppermute | solution.py:15
  206.7 30.8 %collective-permute-start.1 = (f32[2,32,8]{1,2,0:T(8,128)S(1)}, f32[2,32,8]{1,2,0:T(8,128)S(1)}, u32[]{:S(2)}, u32[]{:S(2)}) collective-permute-start(f32[2,32,8]{1,2,0:T(8,128)S(1)} %get-tuple-element.193), channel_id=1, source_target_pairs={{120,0},{0,8},{8,16},{16,24},{24,32},{32,40},{40,48},{48,56},{56,6... | collective-permute-start | bytes 6152 | tf_op jit(solution)/shard_map/while/body/eval_jaxpr/ppermute | solution.py:15
  220.4 17.0 %collective-permute-start.2 = (f32[2,32,8]{1,2,0:T(8,128)S(1)}, f32[2,32,8]{1,2,0:T(8,128)S(1)}, u32[]{:S(2)}, u32[]{:S(2)}) collective-permute-start(f32[2,32,8]{1,2,0:T(8,128)S(1)} %get-tuple-element.192), channel_id=1, source_target_pairs={{120,0},{0,8},{8,16},{16,24},{24,32},{32,40},{40,48},{48,56},{56,6... | collective-permute-start | bytes 6152 | tf_op jit(solution)/shard_map/while/body/eval_jaxpr/ppermute | solution.py:15
  222.4 13.1 %collective-permute-start = (bf16[2,32,1024]{2,1,0:T(8,128)(2,1)S(1)}, bf16[2,32,1024]{2,1,0:T(8,128)(2,1)S(1)}, u32[]{:S(2)}, u32[]{:S(2)}) collective-permute-start(bf16[2,32,1024]{2,1,0:T(8,128)(2,1)S(1)} %get-tuple-element.190), channel_id=1, source_target_pairs={{120,0},{0,8},{8,16},{16,24},{24,32},{32,40},{40,48},{48,56},{56,6... | collective-permute-start | bytes 393224 | tf_op jit(solution)/shard_map/while/body/eval_jaxpr/ppermute | solution.py:15
  239.0 41.1 %collective-permute-start.1 = (f32[2,32,8]{1,2,0:T(8,128)S(1)}, f32[2,32,8]{1,2,0:T(8,128)S(1)}, u32[]{:S(2)}, u32[]{:S(2)}) collective-permute-start(f32[2,32,8]{1,2,0:T(8,128)S(1)} %get-tuple-element.193), channel_id=1, source_target_pairs={{120,0},{0,8},{8,16},{16,24},{24,32},{32,40},{40,48},{48,56},{56,6... | collective-permute-start | bytes 6152 | tf_op jit(solution)/shard_map/while/body/eval_jaxpr/ppermute | solution.py:15
  252.1 28.0 %collective-permute-start.2 = (f32[2,32,8]{1,2,0:T(8,128)S(1)}, f32[2,32,8]{1,2,0:T(8,128)S(1)}, u32[]{:S(2)}, u32[]{:S(2)}) collective-permute-start(f32[2,32,8]{1,2,0:T(8,128)S(1)} %get-tuple-element.192), channel_id=1, source_target_pairs={{120,0},{0,8},{8,16},{16,24},{24,32},{32,40},{40,48},{48,56},{56,6... | collective-permute-start | bytes 6152 | tf_op jit(solution)/shard_map/while/body/eval_jaxpr/ppermute | solution.py:15
  262.1 16.0 %collective-permute-start = (bf16[2,32,1024]{2,1,0:T(8,128)(2,1)S(1)}, bf16[2,32,1024]{2,1,0:T(8,128)(2,1)S(1)}, u32[]{:S(2)}, u32[]{:S(2)}) collective-permute-start(bf16[2,32,1024]{2,1,0:T(8,128)(2,1)S(1)} %get-tuple-element.190), channel_id=1, source_target_pairs={{120,0},{0,8},{8,16},{16,24},{24,32},{32,40},{40,48},{48,56},{56,6... | collective-permute-start | bytes 393224 | tf_op jit(solution)/shard_map/while/body/eval_jaxpr/ppermute | solution.py:15
  287.5 28.5 %collective-permute-start.1 = (f32[2,32,8]{1,2,0:T(8,128)S(1)}, f32[2,32,8]{1,2,0:T(8,128)S(1)}, u32[]{:S(2)}, u32[]{:S(2)}) collective-permute-start(f32[2,32,8]{1,2,0:T(8,128)S(1)} %get-tuple-element.193), channel_id=1, source_target_pairs={{120,0},{0,8},{8,16},{16,24},{24,32},{32,40},{40,48},{48,56},{56,6... | collective-permute-start | bytes 6152 | tf_op jit(solution)/shard_map/while/body/eval_jaxpr/ppermute | solution.py:15
  300.6 15.4 %collective-permute-start.2 = (f32[2,32,8]{1,2,0:T(8,128)S(1)}, f32[2,32,8]{1,2,0:T(8,128)S(1)}, u32[]{:S(2)}, u32[]{:S(2)}) collective-permute-start(f32[2,32,8]{1,2,0:T(8,128)S(1)} %get-tuple-element.192), channel_id=1, source_target_pairs={{120,0},{0,8},{8,16},{16,24},{24,32},{32,40},{40,48},{48,56},{56,6... | collective-permute-start | bytes 6152 | tf_op jit(solution)/shard_map/while/body/eval_jaxpr/ppermute | solution.py:15
  302.6 11.5 %collective-permute-start = (bf16[2,32,1024]{2,1,0:T(8,128)(2,1)S(1)}, bf16[2,32,1024]{2,1,0:T(8,128)(2,1)S(1)}, u32[]{:S(2)}, u32[]{:S(2)}) collective-permute-start(bf16[2,32,1024]{2,1,0:T(8,128)(2,1)S(1)} %get-tuple-element.190), channel_id=1, source_target_pairs={{120,0},{0,8},{8,16},{16,24},{24,32},{32,40},{40,48},{48,56},{56,6... | collective-permute-start | bytes 393224 | tf_op jit(solution)/shard_map/while/body/eval_jaxpr/ppermute | solution.py:15
  317.1 32.0 %collective-permute-start.1 = (f32[2,32,8]{1,2,0:T(8,128)S(1)}, f32[2,32,8]{1,2,0:T(8,128)S(1)}, u32[]{:S(2)}, u32[]{:S(2)}) collective-permute-start(f32[2,32,8]{1,2,0:T(8,128)S(1)} %get-tuple-element.193), channel_id=1, source_target_pairs={{120,0},{0,8},{8,16},{16,24},{24,32},{32,40},{40,48},{48,56},{56,6... | collective-permute-start | bytes 6152 | tf_op jit(solution)/shard_map/while/body/eval_jaxpr/ppermute | solution.py:15
  330.3 18.8 %collective-permute-start.2 = (f32[2,32,8]{1,2,0:T(8,128)S(1)}, f32[2,32,8]{1,2,0:T(8,128)S(1)}, u32[]{:S(2)}, u32[]{:S(2)}) collective-permute-start(f32[2,32,8]{1,2,0:T(8,128)S(1)} %get-tuple-element.192), channel_id=1, source_target_pairs={{120,0},{0,8},{8,16},{16,24},{24,32},{32,40},{40,48},{48,56},{56,6... | collective-permute-start | bytes 6152 | tf_op jit(solution)/shard_map/while/body/eval_jaxpr/ppermute | solution.py:15
  332.2 14.9 %collective-permute-start = (bf16[2,32,1024]{2,1,0:T(8,128)(2,1)S(1)}, bf16[2,32,1024]{2,1,0:T(8,128)(2,1)S(1)}, u32[]{:S(2)}, u32[]{:S(2)}) collective-permute-start(bf16[2,32,1024]{2,1,0:T(8,128)(2,1)S(1)} %get-tuple-element.190), channel_id=1, source_target_pairs={{120,0},{0,8},{8,16},{16,24},{24,32},{32,40},{40,48},{48,56},{56,6... | collective-permute-start | bytes 393224 | tf_op jit(solution)/shard_map/while/body/eval_jaxpr/ppermute | solution.py:15
  352.9 24.5 %collective-permute-start.1 = (f32[2,32,8]{1,2,0:T(8,128)S(1)}, f32[2,32,8]{1,2,0:T(8,128)S(1)}, u32[]{:S(2)}, u32[]{:S(2)}) collective-permute-start(f32[2,32,8]{1,2,0:T(8,128)S(1)} %get-tuple-element.193), channel_id=1, source_target_pairs={{120,0},{0,8},{8,16},{16,24},{24,32},{32,40},{40,48},{48,56},{56,6... | collective-permute-start | bytes 6152 | tf_op jit(solution)/shard_map/while/body/eval_jaxpr/ppermute | solution.py:15
  366.1 11.4 %collective-permute-start.2 = (f32[2,32,8]{1,2,0:T(8,128)S(1)}, f32[2,32,8]{1,2,0:T(8,128)S(1)}, u32[]{:S(2)}, u32[]{:S(2)}) collective-permute-start(f32[2,32,8]{1,2,0:T(8,128)S(1)} %get-tuple-element.192), channel_id=1, source_target_pairs={{120,0},{0,8},{8,16},{16,24},{24,32},{32,40},{40,48},{48,56},{56,6... | collective-permute-start | bytes 6152 | tf_op jit(solution)/shard_map/while/body/eval_jaxpr/ppermute | solution.py:15
  378.4 29.4 %collective-permute-start.1 = (f32[2,32,8]{1,2,0:T(8,128)S(1)}, f32[2,32,8]{1,2,0:T(8,128)S(1)}, u32[]{:S(2)}, u32[]{:S(2)}) collective-permute-start(f32[2,32,8]{1,2,0:T(8,128)S(1)} %get-tuple-element.193), channel_id=1, source_target_pairs={{120,0},{0,8},{8,16},{16,24},{24,32},{32,40},{40,48},{48,56},{56,6... | collective-permute-start | bytes 6152 | tf_op jit(solution)/shard_map/while/body/eval_jaxpr/ppermute | solution.py:15
  391.8 16.1 %collective-permute-start.2 = (f32[2,32,8]{1,2,0:T(8,128)S(1)}, f32[2,32,8]{1,2,0:T(8,128)S(1)}, u32[]{:S(2)}, u32[]{:S(2)}) collective-permute-start(f32[2,32,8]{1,2,0:T(8,128)S(1)} %get-tuple-element.192), channel_id=1, source_target_pairs={{120,0},{0,8},{8,16},{16,24},{24,32},{32,40},{40,48},{48,56},{56,6... | collective-permute-start | bytes 6152 | tf_op jit(solution)/shard_map/while/body/eval_jaxpr/ppermute | solution.py:15
  393.7 12.2 %collective-permute-start = (bf16[2,32,1024]{2,1,0:T(8,128)(2,1)S(1)}, bf16[2,32,1024]{2,1,0:T(8,128)(2,1)S(1)}, u32[]{:S(2)}, u32[]{:S(2)}) collective-permute-start(bf16[2,32,1024]{2,1,0:T(8,128)(2,1)S(1)} %get-tuple-element.190), channel_id=1, source_target_pairs={{120,0},{0,8},{8,16},{16,24},{24,32},{32,40},{40,48},{48,56},{56,6... | collective-permute-start | bytes 393224 | tf_op jit(solution)/shard_map/while/body/eval_jaxpr/ppermute | solution.py:15
  412.8 34.4 %collective-permute-start.1 = (f32[2,32,8]{1,2,0:T(8,128)S(1)}, f32[2,32,8]{1,2,0:T(8,128)S(1)}, u32[]{:S(2)}, u32[]{:S(2)}) collective-permute-start(f32[2,32,8]{1,2,0:T(8,128)S(1)} %get-tuple-element.193), channel_id=1, source_target_pairs={{120,0},{0,8},{8,16},{16,24},{24,32},{32,40},{40,48},{48,56},{56,6... | collective-permute-start | bytes 6152 | tf_op jit(solution)/shard_map/while/body/eval_jaxpr/ppermute | solution.py:15
  426.1 21.1 %collective-permute-start.2 = (f32[2,32,8]{1,2,0:T(8,128)S(1)}, f32[2,32,8]{1,2,0:T(8,128)S(1)}, u32[]{:S(2)}, u32[]{:S(2)}) collective-permute-start(f32[2,32,8]{1,2,0:T(8,128)S(1)} %get-tuple-element.192), channel_id=1, source_target_pairs={{120,0},{0,8},{8,16},{16,24},{24,32},{32,40},{40,48},{48,56},{56,6... | collective-permute-start | bytes 6152 | tf_op jit(solution)/shard_map/while/body/eval_jaxpr/ppermute | solution.py:15
  428.0 17.2 %collective-permute-start = (bf16[2,32,1024]{2,1,0:T(8,128)(2,1)S(1)}, bf16[2,32,1024]{2,1,0:T(8,128)(2,1)S(1)}, u32[]{:S(2)}, u32[]{:S(2)}) collective-permute-start(bf16[2,32,1024]{2,1,0:T(8,128)(2,1)S(1)} %get-tuple-element.190), channel_id=1, source_target_pairs={{120,0},{0,8},{8,16},{16,24},{24,32},{32,40},{40,48},{48,56},{56,6... | collective-permute-start | bytes 393224 | tf_op jit(solution)/shard_map/while/body/eval_jaxpr/ppermute | solution.py:15
  448.1 33.4 %collective-permute-start.1 = (f32[2,32,8]{1,2,0:T(8,128)S(1)}, f32[2,32,8]{1,2,0:T(8,128)S(1)}, u32[]{:S(2)}, u32[]{:S(2)}) collective-permute-start(f32[2,32,8]{1,2,0:T(8,128)S(1)} %get-tuple-element.193), channel_id=1, source_target_pairs={{120,0},{0,8},{8,16},{16,24},{24,32},{32,40},{40,48},{48,56},{56,6... | collective-permute-start | bytes 6152 | tf_op jit(solution)/shard_map/while/body/eval_jaxpr/ppermute | solution.py:15
  461.4 20.1 %collective-permute-start.2 = (f32[2,32,8]{1,2,0:T(8,128)S(1)}, f32[2,32,8]{1,2,0:T(8,128)S(1)}, u32[]{:S(2)}, u32[]{:S(2)}) collective-permute-start(f32[2,32,8]{1,2,0:T(8,128)S(1)} %get-tuple-element.192), channel_id=1, source_target_pairs={{120,0},{0,8},{8,16},{16,24},{24,32},{32,40},{40,48},{48,56},{56,6... | collective-permute-start | bytes 6152 | tf_op jit(solution)/shard_map/while/body/eval_jaxpr/ppermute | solution.py:15
  463.4 16.2 %collective-permute-start = (bf16[2,32,1024]{2,1,0:T(8,128)(2,1)S(1)}, bf16[2,32,1024]{2,1,0:T(8,128)(2,1)S(1)}, u32[]{:S(2)}, u32[]{:S(2)}) collective-permute-start(bf16[2,32,1024]{2,1,0:T(8,128)(2,1)S(1)} %get-tuple-element.190), channel_id=1, source_target_pairs={{120,0},{0,8},{8,16},{16,24},{24,32},{32,40},{40,48},{48,56},{56,6... | collective-permute-start | bytes 393224 | tf_op jit(solution)/shard_map/while/body/eval_jaxpr/ppermute | solution.py:15
  476.0 11.9 %collective-permute-start.3 = (f32[2,32,1024]{2,1,0:T(8,128)S(1)}, f32[2,32,1024]{2,1,0:T(8,128)S(1)}, u32[]{:S(2)}, u32[]{:S(2)}) collective-permute-start(f32[2,32,1024]{2,1,0:T(8,128)S(1)} %get-tuple-element.191), channel_id=1, source_target_pairs={{120,0},{0,8},{8,16},{16,24},{24,32},{32,40},{40,48},{48,56},{56,6... | collective-permute-start | bytes 786440 | tf_op jit(solution)/shard_map/while/body/eval_jaxpr/ppermute | solution.py:15
  488.0 33.6 %collective-permute-start.1 = (f32[2,32,8]{1,2,0:T(8,128)S(1)}, f32[2,32,8]{1,2,0:T(8,128)S(1)}, u32[]{:S(2)}, u32[]{:S(2)}) collective-permute-start(f32[2,32,8]{1,2,0:T(8,128)S(1)} %get-tuple-element.193), channel_id=1, source_target_pairs={{120,0},{0,8},{8,16},{16,24},{24,32},{32,40},{40,48},{48,56},{56,6... | collective-permute-start | bytes 6152 | tf_op jit(solution)/shard_map/while/body/eval_jaxpr/ppermute | solution.py:15
  501.3 20.3 %collective-permute-start.2 = (f32[2,32,8]{1,2,0:T(8,128)S(1)}, f32[2,32,8]{1,2,0:T(8,128)S(1)}, u32[]{:S(2)}, u32[]{:S(2)}) collective-permute-start(f32[2,32,8]{1,2,0:T(8,128)S(1)} %get-tuple-element.192), channel_id=1, source_target_pairs={{120,0},{0,8},{8,16},{16,24},{24,32},{32,40},{40,48},{48,56},{56,6... | collective-permute-start | bytes 6152 | tf_op jit(solution)/shard_map/while/body/eval_jaxpr/ppermute | solution.py:15
  503.2 16.4 %collective-permute-start = (bf16[2,32,1024]{2,1,0:T(8,128)(2,1)S(1)}, bf16[2,32,1024]{2,1,0:T(8,128)(2,1)S(1)}, u32[]{:S(2)}, u32[]{:S(2)}) collective-permute-start(bf16[2,32,1024]{2,1,0:T(8,128)(2,1)S(1)} %get-tuple-element.190), channel_id=1, source_target_pairs={{120,0},{0,8},{8,16},{16,24},{24,32},{32,40},{40,48},{48,56},{56,6... | collective-permute-start | bytes 393224 | tf_op jit(solution)/shard_map/while/body/eval_jaxpr/ppermute | solution.py:15
  508.9 14.8 %collective-permute-start.3 = (f32[2,32,1024]{2,1,0:T(8,128)S(1)}, f32[2,32,1024]{2,1,0:T(8,128)S(1)}, u32[]{:S(2)}, u32[]{:S(2)}) collective-permute-start(f32[2,32,1024]{2,1,0:T(8,128)S(1)} %get-tuple-element.191), channel_id=1, source_target_pairs={{120,0},{0,8},{8,16},{16,24},{24,32},{32,40},{40,48},{48,56},{56,6... | collective-permute-start | bytes 786440 | tf_op jit(solution)/shard_map/while/body/eval_jaxpr/ppermute | solution.py:15
  523.8 144.7 %collective-permute-start.5 = (f32[2,32,8]{1,2,0:T(8,128)S(1)}, f32[2,32,8]{1,2,0:T(8,128)S(1)}, u32[]{:S(2)}, u32[]{:S(2)}) collective-permute-start(f32[2,32,8]{1,2,0:T(8,128)S(1)} %get-tuple-element.50), channel_id=1, source_target_pairs={{120,0},{0,8},{8,16},{16,24},{24,32},{32,40},{40,48},{48,56},{56,6... | collective-permute-start | bytes 6152 | tf_op jit(solution)/shard_map/ppermute | solution.py:15
  537.0 131.5 %collective-permute-start.6 = (f32[2,32,8]{1,2,0:T(8,128)S(1)}, f32[2,32,8]{1,2,0:T(8,128)S(1)}, u32[]{:S(2)}, u32[]{:S(2)}) collective-permute-start(f32[2,32,8]{1,2,0:T(8,128)S(1)} %get-tuple-element.51), channel_id=1, source_target_pairs={{120,0},{0,8},{8,16},{16,24},{24,32},{32,40},{40,48},{48,56},{56,6... | collective-permute-start | bytes 6152 | tf_op jit(solution)/shard_map/ppermute | solution.py:15
  538.9 131.0 %collective-permute-start.4 = (f32[2,32,1024]{2,1,0:T(8,128)S(1)}, f32[2,32,1024]{2,1,0:T(8,128)S(1)}, u32[]{:S(2)}, u32[]{:S(2)}) collective-permute-start(f32[2,32,1024]{2,1,0:T(8,128)S(1)} %get-tuple-element.49), channel_id=1, source_target_pairs={{120,0},{0,8},{8,16},{16,24},{24,32},{32,40},{40,48},{48,56},{56,6... | collective-permute-start | bytes 786440 | tf_op jit(solution)/shard_map/ppermute | solution.py:15
  (23 other events, 2526.1 us)
where the time goes:
time: 673 us; the launch traced here: 671 us
  starting transfers between devices  437 us (65%)
  blocking collectives  125 us (19%)
  waiting for transfers between devices  60.2 us (9%)
  matrix products  19.7 us (3%)
  other arithmetic  13.8 us (2%)
  local copies, waits for them, and re-layouts  12.7 us (2%)
    ppermute x63, starting transfers between devices, shifted(): return lax.ppermute(block, axis, route)  437 us
    ppermute x63, waiting for transfers between devices, shifted(): return lax.ppermute(block, axis, route)  60.2 us
    all_gather x1, blocking collectives, per_device(): piece_pos = lax.all_gather(positions, 'ctx', axis=1, tiled=True)  43.6 us
    all_gather x1, blocking collectives, per_device(): piece_values = lax.all_gather(incoming_values, 'ctx', axis=1, tiled=True)  41.8 us
    all_gather x1, blocking collectives, per_device(): piece_keys = lax.all_gather(rotated_new_keys, 'ctx', axis=1, tiled=True)  39.3 us
  transfers between devices with their start and end apart: 63, of which 23 were waited for; matrix products, arithmetic and copies ran while one was open for 6% of the time, Pallas kernels for 0%

commit v1 on v0

v1 whole, which is shorter than its diff:
```python
import functools

import jax
import jax.numpy as jnp
from jax import lax
from jax.experimental import pallas as pl
from jax.experimental.pallas import tpu as pltpu
from jax.sharding import PartitionSpec as P

HEAD = 128
NEG = -1e30
VMEM = pl.BlockSpec(memory_space=pltpu.VMEM)
SMEM = pl.BlockSpec(memory_space=pltpu.SMEM)
LIMIT = 48 * 1024 * 1024
PACK = 48 * 1024 * 1024
SCALE = 1.0 / HEAD**0.5


def swap(block, mask):
    count = lax.axis_size("ctx")
    return lax.ppermute(block, "ctx", [(i, i ^ mask) for i in range(count)])


def column(row, rows, period):
    r = lax.broadcasted_iota(jnp.int32, (rows, 128), 0) % period
    c = lax.broadcasted_iota(jnp.int32, (rows, 128), 1)
    spread = jnp.broadcast_to(row, (rows, 128))
    return jnp.sum(jnp.where(r == c, spread, 0.0), axis=1, keepdims=True)


def lane_row(spread):
    r = lax.broadcasted_iota(jnp.int32, (128, 128), 0)
    c = lax.broadcasted_iota(jnp.int32, (128, 128), 1)
    return jnp.sum(jnp.where(r == c, jnp.broadcast_to(spread, (128, 128)), 0.0), axis=0, keepdims=True)


def stat_block(lse):
    halves = jnp.concatenate([lane_row(lse[:128]), lane_row(lse[128:])], axis=0)
    hi = halves.astype(jnp.bfloat16).astype(jnp.float32)
    rest = halves - hi
    mid = rest.astype(jnp.bfloat16).astype(jnp.float32)
    low = rest - mid
    blank = jnp.zeros((10, 128), jnp.float32)
    return jnp.concatenate([hi, mid, low, blank], axis=0).astype(jnp.bfloat16)


def read_stats(block):
    block = block.astype(jnp.float32)
    halves = block[0:2] + block[2:4] + block[4:6]
    return jnp.concatenate([column(halves[0:1], 128, 128), column(halves[1:2], 128, 128)], axis=0)


def place_block(row):
    line = lax.broadcasted_iota(jnp.int32, (16, 128), 0)
    spread = jnp.broadcast_to(row, (16, 128))
    pieces = jnp.where(line == 0, spread >> 7, jnp.where(line == 1, spread & 127, 0))
    return pieces.astype(jnp.float32).astype(jnp.bfloat16)


def read_places(block):
    block = block.astype(jnp.float32)
    return block[0:1] * 128.0 + block[1:2]


def pack_queries_kernel(tokens, queries, places, out):
    sessions, size, _ = out.shape
    for s in range(sessions):
        for h in range((size - 16) // tokens):
            out[s, h * tokens : (h + 1) * tokens, :] = queries[s, :, h * HEAD : (h + 1) * HEAD]
        out[s, size - 16 : size, :] = place_block(places[s : s + 1, :])


def pack_queries(queries, places):
    sessions, tokens, width = queries.shape
    return pl.pallas_call(
        functools.partial(pack_queries_kernel, tokens),
        out_shape=jax.ShapeDtypeStruct((sessions, width // HEAD * tokens + 16, HEAD), jnp.bfloat16),
        in_specs=[VMEM] * 2,
        out_specs=VMEM,
        compiler_params=pltpu.CompilerParams(vmem_limit_bytes=LIMIT),
    )(queries, places)


def pack_keys_kernel(slots, fresh, places, k, v, nk, nv, out, keys, sems):
    nk_at = 2 * slots
    copies = [pltpu.make_async_copy(k, keys, sems.at[0])]
    for i, (ref, at, size) in enumerate(((v, slots, slots), (nk, nk_at, fresh), (nv, nk_at + fresh, fresh))):
        copies.append(pltpu.make_async_copy(ref, out.at[:, pl.ds(at, size)], sems.at[i + 1]))
    for copy in copies:
        copy.start()
    for s in range(out.shape[0]):
        out[s, nk_at + 2 * fresh : nk_at + 2 * fresh + 16, :] = place_block(places[s : s + 1, :])
    copies[0].wait()
    for s in range(out.shape[0]):
        for at in range(0, slots, HEAD):
            tile = keys[s, at : at + HEAD, :].astype(jnp.float32)
            out[s, at : at + HEAD, :] = tile.T.astype(jnp.bfloat16)
    for copy in copies[1:]:
        copy.wait()


def pack_keys(places, k, v, nk, nv):
    sessions, slots, _ = k.shape
    fresh = nk.shape[1]
    return pl.pallas_call(
        functools.partial(pack_keys_kernel, slots, fresh),
        out_shape=jax.ShapeDtypeStruct((sessions, 2 * (slots + fresh) + 16, HEAD), jnp.bfloat16),
        in_specs=[VMEM] + [pl.BlockSpec(memory_space=pltpu.HBM)] * 4,
        out_specs=VMEM,
        scratch_shapes=[pltpu.VMEM(k.shape, k.dtype), pltpu.SemaphoreType.DMA((4,))],
        compiler_params=pltpu.CompilerParams(vmem_limit_bytes=PACK),
    )(places, k, v, nk, nv)


def attend_kernel(scal, q, s0, s1, s2, s3, out, points, weights):
    blocks = (s0, s1, s2, s3)
    sessions, size, _ = q.shape
    rows = size - 16
    fresh = 128 // len(blocks)
    slots = (s0.shape[1] - 16) // 2 - fresh
    nk = 2 * slots
    keys = len(blocks) * slots + 128
    wide, tall = 256, 32
    lane = lax.broadcasted_iota(jnp.int32, (1, 128), 1)
    cells = lax.broadcasted_iota(jnp.int32, (1, wide), 1)
    nt = (((1,), (1,)), ((), ()))

    def score(s):
        mine = q[s, 0:rows, :]
        top = jnp.full((rows, 128), NEG, jnp.float32)
        for b, blk in enumerate(blocks):
            left = scal[s] - scal[sessions + b]
            for at in range(0, slots, wide):
                tiles = [blk[s, j : j + HEAD, :] for j in range(at, at + wide, HEAD)]
                got = jnp.dot(mine, jnp.concatenate(tiles, axis=1), preferred_element_type=jnp.float32)
                got = jnp.where(cells < left - at, got, NEG)
                points[s, :, b * slots + at : b * slots + at + wide] = got
                for j in range(0, wide, 128):
                    top = jnp.maximum(top, got[:, j : j + 128])
        qpos = column(read_places(q[s, rows:size, :]), rows, fresh)
        kpos = jnp.zeros((1, 128), jnp.float32)
        for b, blk in enumerate(blocks):
            places = read_places(blk[s, nk + 2 * fresh : nk + 2 * fresh + 16, :])
            kpos = jnp.where(lane // fresh == b, places, kpos)
        new_keys = jnp.concatenate([blk[s, nk : nk + fresh, :] for blk in blocks], axis=0)
        got = lax.dot_general(mine, new_keys, nt, preferred_element_type=jnp.float32)
        got = jnp.where(kpos <= qpos, got, NEG)
        points[s, :, keys - 128 : keys] = got
        return jnp.maximum(top, got)

    def weigh(s, top):
        shifts, totals = [], []
        for r in range(0, rows, tall):
            shift = jnp.max(top[r : r + tall, :], axis=1, keepdims=True) * SCALE
            total = jnp.zeros((tall, 128), jnp.float32)
            for at in range(0, keys, 512):
                end = min(at + 512, keys)
                w = jnp.exp(points[s, r : r + tall, at:end] * SCALE - shift)
                for j in range(0, end - at, 128):
                    total += w[:, j : j + 128]
                weights[s, r : r + tall, at:end] = w.astype(jnp.bfloat16)
            shifts.append(shift)
            totals.append(jnp.sum(total, axis=1, keepdims=True))
        return jnp.concatenate(shifts, axis=0), jnp.concatenate(totals, axis=0)

    def gather(s, shift, total):
        summed = jnp.zeros((rows, HEAD), jnp.float32)
        for b, blk in enumerate(blocks):
            w = weights[s, :, b * slots : (b + 1) * slots]
            summed += jnp.dot(w, blk[s, slots:nk, :], preferred_element_type=jnp.float32)
        new_values = jnp.concatenate([blk[s, nk + fresh : nk + 2 * fresh, :] for blk in blocks], axis=0)
        summed += jnp.dot(weights[s, :, keys - 128 : keys], new_values, preferred_element_type=jnp.float32)
        out[s, 0:rows, :] = (summed / total).astype(jnp.bfloat16)
        out[s, rows:size, :] = stat_block(shift + jnp.log(total))

    tops = [score(s) for s in range(sessions)]
    for s in range(sessions):
        gather(s, *weigh(s, tops[s]))


def attend(scal, q, blocks):
    sessions, size, _ = q.shape
    keys = len(blocks) * ((blocks[0].shape[1] - 16) // 2)
    return pl.pallas_call(
        attend_kernel,
        out_shape=jax.ShapeDtypeStruct(q.shape, jnp.bfloat16),
        in_specs=[SMEM] + [VMEM] * (1 + len(blocks)),
        out_specs=VMEM,
        scratch_shapes=[
            pltpu.VMEM((sessions, size - 16, keys), jnp.float32),
            pltpu.VMEM((sessions, size - 16, keys), jnp.bfloat16),
        ],
        compiler_params=pltpu.CompilerParams(vmem_limit_bytes=LIMIT),
        cost_estimate=pl.CostEstimate(flops=q.size, bytes_accessed=0, transcendentals=0),
    )(scal, q, *blocks)


def merged(rows, messages):
    logs = [read_stats(m[rows : rows + 16, :]) for m in messages]
    top = functools.reduce(jnp.maximum, logs)
    shares = [jnp.exp(x - top) for x in logs]
    total = sum(shares)
    value = sum(m[:rows, :].astype(jnp.float32) * (x / total) for m, x in zip(messages, shares))
    return value, top + jnp.log(total)


def merge_kernel(own, came, out):
    sessions, size, _ = own.shape
    rows = size - 16
    for s in range(sessions):
        value, lse = merged(rows, [own[s], came[s]])
        out[s, 0:rows, :] = value.astype(jnp.bfloat16)
        out[s, rows:size, :] = stat_block(lse)


def merge(own, came):
    return pl.pallas_call(
        merge_kernel,
        out_shape=jax.ShapeDtypeStruct(own.shape, jnp.bfloat16),
        in_specs=[VMEM, VMEM],
        out_specs=VMEM,
        compiler_params=pltpu.CompilerParams(vmem_limit_bytes=LIMIT),
    )(own, came)


def finish_kernel(one, two, three, out):
    sessions, tokens, width = out.shape
    rows = one.shape[1] - 16
    for s in range(sessions):
        value, _ = merged(rows, [one[s], two[s], three[s]])
        value = value.astype(jnp.bfloat16)
        for h in range(width // HEAD):
            out[s, :, h * HEAD : (h + 1) * HEAD] = value[h * tokens : (h + 1) * tokens, :]


def finish(one, two, three, tokens):
    sessions, size, _ = one.shape
    return pl.pallas_call(
        finish_kernel,
        out_shape=jax.ShapeDtypeStruct((sessions, tokens, (size - 16) // tokens * HEAD), jnp.bfloat16),
        in_specs=[VMEM] * 3,
        out_specs=VMEM,
        compiler_params=pltpu.CompilerParams(vmem_limit_bytes=LIMIT),
    )(one, two, three)


def per_device(queries, cache_keys, stored_values, new_keys, new_values, lengths, positions):
    member = lax.axis_index("ctx")
    tokens = queries.shape[1]
    slots = cache_keys.shape[1]
    places = jnp.tile(positions, (1, 128 // tokens))
    bases = jnp.stack([member, member ^ 1, member ^ 4, member ^ 5]) * slots
    scal = jnp.concatenate([lengths, bases]).astype(jnp.int32)

    near_q = pack_queries(queries, places)
    near_x = swap(near_q, 12)
    far_q = swap(near_q, 2)
    own = pack_keys(places, cache_keys, stored_values, new_keys, new_values)
    x_own = swap(own, 4)

    far_x = swap(far_q, 12)
    x_own, far_q, near_x = lax.optimization_barrier((x_own, far_q, near_x))
    blocks = (own, swap(own, 1), x_own, swap(x_own, 1))
    far_a = attend(scal, far_q, blocks)
    far_x, far_a = lax.optimization_barrier((far_x, far_a))
    far_b = attend(scal, far_x, blocks)
    far_came = swap(far_b, 12)
    far_b, near_x = lax.optimization_barrier((far_b, near_x))
    near_b = attend(scal, near_x, blocks)
    near_came = swap(near_b, 12)
    far_came, near_b, near_q = lax.optimization_barrier((far_came, near_b, near_q))
    far = merge(far_a, far_came)
    back = swap(far, 2)
    far, near_q = lax.optimization_barrier((far, near_q))
    near_a = attend(scal, near_q, blocks)
    return finish(near_a, near_came, back, tokens)


def solution(mesh):
    spec = P("rep", "ctx", "tp")
    return jax.shard_map(
        per_device,
        mesh=mesh,
        in_specs=(spec, spec, spec, spec, spec, P("rep"), P("rep", "ctx")),
        out_specs=spec,
        check_vma=False,
    )
```

time: 673 us -> 93.7 us (0.14)
  the two profiles are of different devices: /device:TPU:169 before, /device:TPU:40 now
where the time goes in v1:
time: 93.7 us; the launch traced here: 93 us
  starting transfers between devices  49.4 us (53%)
  Pallas kernels  23.4 us (25%)
  waiting for transfers between devices  13.9 us (15%)
  local copies, waits for them, and re-layouts  5.86 us (6%)
    ppermute x9, starting transfers between devices, swap(): return lax.ppermute(block, 'ctx', [(i, i ^ mask) for i in range(count)])  49.4 us
    pallas_call x4, Pallas kernels, attend(): pl.pallas_call(attend_kernel, out_shape=jax.ShapeDtypeStruct(q.shape, jnp...  21.4 us
    ppermute x9, waiting for transfers between devices, swap(): return lax.ppermute(block, 'ctx', [(i, i ^ mask) for i in range(count)])  13.9 us
    unnamed x16, local copies, waits for them, and re-layouts  5.09 us
  transfers between devices with their start and end apart: 9, of which 2 were waited for; matrix products, arithmetic and copies ran while one was open for 0% of the time, Pallas kernels for 18%

profile of v1, /device:TPU:40, one launch (start us, length us, event | category | flops | bytes accessed | tf_op | source)
XLA Modules:
  0.0 93.0 jit_solution(13887703091144171571)
XLA Ops:
  0.0 0.7 tile.4
  0.7 0.1 tile.10.places
  0.8 0.0 copy-start
  0.8 1.0 %copy-done = bf16[2,1024,128]{2,1,0:T(8,128)(2,1)S(1)} copy-done((bf16[2,1024,128]{2,1,0:T(8,128)(2,1)S(1)}, bf16[2,1024,128]{2,1,0:T(8,128)(2,1)}, u32[]{:S(2)}) %copy-start) | copy-done | bytes 524312
  1.8 0.0 copy-start.1
  1.8 1.0 %copy-done.1 = bf16[2,1024,128]{2,1,0:T(8,128)(2,1)S(1)} copy-done((bf16[2,1024,128]{2,1,0:T(8,128)(2,1)S(1)}, bf16[2,1024,128]{2,1,0:T(8,128)(2,1)}, u32[]{:S(2)}) %copy-start.1) | copy-done | bytes 524312
  2.9 0.0 copy-start.5
  2.9 0.7 copy-done.5
  3.6 0.0 copy-start.6
  3.6 0.7 copy-done.6
  4.3 0.0 copy-start.4
  4.3 0.0 copy-start.7
  4.3 0.3 shard_map.74.s0
  4.6 3.4 %collective-permute-start.2 = (bf16[2,2128,128]{2,1,0:T(8,128)(2,1)S(1)}, bf16[2,2128,128]{2,1,0:T(8,128)(2,1)S(1)}, u32[]{:S(2)}, u32[]{:S(2)}) collective-permute-start(bf16[2,2128,128]{2,1,0:T(8,128)(2,1)S(1)} %shard_map.74.s0), channel_id=1, source_target_pairs={{0,32},{8,40},{16,48},{24,56},{32,0},{40,8},{48,16},{56,24},{64,96... | collective-permute-start | bytes 3268616 | tf_op jit(solution)/shard_map/ppermute | solution.py:21
  8.1 0.0 copy-done.4
  8.1 14.8 %collective-permute-start = (bf16[2,272,128]{2,1,0:T(8,128)(2,1)S(1)}, bf16[2,272,128]{2,1,0:T(8,128)(2,1)S(1)}, u32[]{:S(2)}, u32[]{:S(2)}) collective-permute-start(bf16[2,272,128]{2,1,0:T(8,128)(2,1)S(1)} %shard_map.73.q), channel_id=1, source_target_pairs={{0,16},{8,24},{16,0},{24,8},{32,48},{40,56},{48,32},{56,40},{64,80... | collective-permute-start | bytes 417800 | tf_op jit(solution)/shard_map/ppermute | solution.py:21
  22.9 4.0 %collective-permute-start.3 = (bf16[2,272,128]{2,1,0:T(8,128)(2,1)S(1)}, bf16[2,272,128]{2,1,0:T(8,128)(2,1)S(1)}, u32[]{:S(2)}, u32[]{:S(2)}) collective-permute-start(bf16[2,272,128]{2,1,0:T(8,128)(2,1)S(1)} %shard_map.73.q), channel_id=1, source_target_pairs={{0,96},{8,104},{16,112},{24,120},{32,64},{40,72},{48,80},{56,88},{... | collective-permute-start | bytes 417800 | tf_op jit(solution)/shard_map/ppermute | solution.py:21
  26.9 1.9 %collective-permute-start.4 = (bf16[2,2128,128]{2,1,0:T(8,128)(2,1)S(1)}, bf16[2,2128,128]{2,1,0:T(8,128)(2,1)S(1)}, u32[]{:S(2)}, u32[]{:S(2)}) collective-permute-start(bf16[2,2128,128]{2,1,0:T(8,128)(2,1)S(1)} %shard_map.74.s0), channel_id=1, source_target_pairs={{0,8},{8,0},{16,24},{24,16},{32,40},{40,32},{48,56},{56,48},{64,72... | collective-permute-start | bytes 3268616 | tf_op jit(solution)/shard_map/ppermute | solution.py:21
  28.9 6.5 %collective-permute-done.q = bf16[2,272,128]{2,1,0:T(8,128)(2,1)S(1)} collective-permute-done((bf16[2,272,128]{2,1,0:T(8,128)(2,1)S(1)}, bf16[2,272,128]{2,1,0:T(8,128)(2,1)S(1)}, u32[]{:S(2)}, u32[]{:S(2)}) %collective-permute-start) | collective-permute-done | bytes 139296 | tf_op jit(solution)/shard_map/ppermute | solution.py:21
  35.3 0.0 copy-start.2
  35.3 0.0 collective-permute-done.3.q
  35.3 0.0 collective-permute-done.2.s2
  35.3 0.7 copy-done.2
  36.0 1.9 %collective-permute-start.5 = (bf16[2,2128,128]{2,1,0:T(8,128)(2,1)S(1)}, bf16[2,2128,128]{2,1,0:T(8,128)(2,1)}, u32[]{:S(2)}, u32[]{:S(2)}) collective-permute-start(bf16[2,2128,128]{2,1,0:T(8,128)(2,1)S(1)} %collective-permute-done.2.s2), channel_id=1, source_target_pairs={{0,8},{8,0},{16,24},{24,16},{32,40},{40,32},{48,56},{56,48},{64,72... | collective-permute-start | bytes 3268616 | tf_op jit(solution)/shard_map/ppermute | solution.py:21
  37.9 4.0 %collective-permute-start.1 = (bf16[2,272,128]{2,1,0:T(8,128)(2,1)}, bf16[2,272,128]{2,1,0:T(8,128)(2,1)S(1)}, u32[]{:S(2)}, u32[]{:S(2)}) collective-permute-start(bf16[2,272,128]{2,1,0:T(8,128)(2,1)} %copy-done.2), channel_id=1, source_target_pairs={{0,96},{8,104},{16,112},{24,120},{32,64},{40,72},{48,80},{56,88},{... | collective-permute-start | bytes 417800 | tf_op jit(solution)/shard_map/ppermute | solution.py:21
  41.9 0.1 add_multiply_fusion
  42.0 0.0 copy-done.7
  42.0 0.1 pad_add_fusion.scal
  42.1 0.0 collective-permute-done.4.s1
  42.1 0.0 collective-permute-done.5.s3
  42.1 0.0 copy-start.3
  42.1 0.9 copy-done.3
  43.0 5.3 %shard_map.75.own = bf16[2,272,128]{2,1,0:T(8,128)(2,1)S(1)} custom-call(s32[6]{0:T(128)S(1)} %pad_add_fusion.scal, bf16[2,272,128]{2,1,0:T(8,128)(2,1)S(1)} %copy-done.3, bf16[2,2128,128]{2,1,0:T(8,128)(2,1)S(1)} %shard_map.74.s0, bf16[2,2128,128]{2,1,0:T(8,128)(2,1)S(1)} %collective-permute-done.4.s1, bf16[2,2128,128]{2,1,0:T(8,128)(2,1)S(1)} %collective-permute-done.2.s2, ...), custom_call_target="tpu_custom_call" | custom-call | flops 69632 | tf_op jit(solution)/shard_map/pallas_call | solution.py:184
  48.4 0.0 collective-permute-done.1.q
  48.4 5.4 %shard_map.76 = bf16[2,272,128]{2,1,0:T(8,128)(2,1)S(1)} custom-call(s32[6]{0:T(128)S(1)} %pad_add_fusion.scal, bf16[2,272,128]{2,1,0:T(8,128)(2,1)S(1)} %collective-permute-done.1.q, bf16[2,2128,128]{2,1,0:T(8,128)(2,1)S(1)} %shard_map.74.s0, bf16[2,2128,128]{2,1,0:T(8,128)(2,1)S(1)} %collective-permute-done.4.s1, ...), custom_call_target="tpu_custom_call" | custom-call | flops 69632 | tf_op jit(solution)/shard_map/pallas_call | solution.py:184
  53.7 3.2 %collective-permute-start.6 = (bf16[2,272,128]{2,1,0:T(8,128)(2,1)S(1)}, bf16[2,272,128]{2,1,0:T(8,128)(2,1)S(1)}, u32[]{:S(2)}, u32[]{:S(2)}) collective-permute-start(bf16[2,272,128]{2,1,0:T(8,128)(2,1)S(1)} %shard_map.76), channel_id=1, source_target_pairs={{0,96},{8,104},{16,112},{24,120},{32,64},{40,72},{48,80},{56,88},{... | collective-permute-start | bytes 417800 | tf_op jit(solution)/shard_map/ppermute | solution.py:21
  57.0 5.3 %shard_map.77 = bf16[2,272,128]{2,1,0:T(8,128)(2,1)S(1)} custom-call(s32[6]{0:T(128)S(1)} %pad_add_fusion.scal, bf16[2,272,128]{2,1,0:T(8,128)(2,1)S(1)} %collective-permute-done.3.q, bf16[2,2128,128]{2,1,0:T(8,128)(2,1)S(1)} %shard_map.74.s0, bf16[2,2128,128]{2,1,0:T(8,128)(2,1)S(1)} %collective-permute-done.4.s1, ...), custom_call_target="tpu_custom_call" | custom-call | flops 69632 | tf_op jit(solution)/shard_map/pallas_call | solution.py:184
  62.3 4.0 %collective-permute-start.7 = (bf16[2,272,128]{2,1,0:T(8,128)(2,1)S(1)}, bf16[2,272,128]{2,1,0:T(8,128)(2,1)S(1)}, u32[]{:S(2)}, u32[]{:S(2)}) collective-permute-start(bf16[2,272,128]{2,1,0:T(8,128)(2,1)S(1)} %shard_map.77), channel_id=1, source_target_pairs={{0,96},{8,104},{16,112},{24,120},{32,64},{40,72},{48,80},{56,88},{... | collective-permute-start | bytes 417800 | tf_op jit(solution)/shard_map/ppermute | solution.py:21
  66.3 0.0 collective-permute-done.6.came
  66.3 0.5 shard_map.78
  66.8 12.1 %collective-permute-start.8 = (bf16[2,272,128]{2,1,0:T(8,128)(2,1)S(1)}, bf16[2,272,128]{2,1,0:T(8,128)(2,1)S(1)}, u32[]{:S(2)}, u32[]{:S(2)}) collective-permute-start(bf16[2,272,128]{2,1,0:T(8,128)(2,1)S(1)} %shard_map.78), channel_id=1, source_target_pairs={{0,16},{8,24},{16,0},{24,8},{32,48},{40,56},{48,32},{56,40},{64,80... | collective-permute-start | bytes 417800 | tf_op jit(solution)/shard_map/ppermute | solution.py:21
  79.0 5.3 %shard_map.79.one = bf16[2,272,128]{2,1,0:T(8,128)(2,1)S(1)} custom-call(s32[6]{0:T(128)S(1)} %pad_add_fusion.scal, bf16[2,272,128]{2,1,0:T(8,128)(2,1)S(1)} %shard_map.73.q, bf16[2,2128,128]{2,1,0:T(8,128)(2,1)S(1)} %shard_map.74.s0, bf16[2,2128,128]{2,1,0:T(8,128)(2,1)S(1)} %collective-permute-done.4.s1, ...), custom_call_target="tpu_custom_call" | custom-call | flops 69632 | tf_op jit(solution)/shard_map/pallas_call | solution.py:184
  84.3 0.0 collective-permute-done.7.two
  84.3 7.4 %collective-permute-done.8.three = bf16[2,272,128]{2,1,0:T(8,128)(2,1)S(1)} collective-permute-done((bf16[2,272,128]{2,1,0:T(8,128)(2,1)S(1)}, bf16[2,272,128]{2,1,0:T(8,128)(2,1)S(1)}, u32[]{:S(2)}, u32[]{:S(2)}) %collective-permute-start.8) | collective-permute-done | bytes 139296 | tf_op jit(solution)/shard_map/ppermute | solution.py:21
  91.8 1.2 %shard_map.80 = bf16[2,32,1024]{2,1,0:T(8,128)(2,1)} custom-call(bf16[2,272,128]{2,1,0:T(8,128)(2,1)S(1)} %shard_map.79.one, bf16[2,272,128]{2,1,0:T(8,128)(2,1)S(1)} %collective-permute-done.7.two, bf16[2,272,128]{2,1,0:T(8,128)(2,1)S(1)} %collective-permute-done.8.three), custom_call_target="tpu_custom_call" | custom-call | tf_op jit(solution)/shard_map/pallas_call | solution.py:238
  (1 shorter events, 0.0 us)
Async XLA Ops:
  0.8 1.0 %copy-start = (bf16[2,1024,128]{2,1,0:T(8,128)(2,1)S(1)}, bf16[2,1024,128]{2,1,0:T(8,128)(2,1)}, u32[]{:S(2)}) copy-start(bf16[2,1024,128]{2,1,0:T(8,128)(2,1)} %k.1) | copy-start | bytes 1572868
  1.8 1.0 %copy-start.1 = (bf16[2,1024,128]{2,1,0:T(8,128)(2,1)S(1)}, bf16[2,1024,128]{2,1,0:T(8,128)(2,1)}, u32[]{:S(2)}) copy-start(bf16[2,1024,128]{2,1,0:T(8,128)(2,1)} %v.1) | copy-start | bytes 1572868
  2.9 0.7 copy-start.5
  3.6 0.7 copy-start.6
  4.3 3.8 %copy-start.4 = (bf16[2,32,1024]{2,1,0:T(8,128)(2,1)S(1)}, bf16[2,32,1024]{2,1,0:T(8,128)(2,1)}, u32[]{:S(2)}) copy-start(bf16[2,32,1024]{2,1,0:T(8,128)(2,1)} %queries.1) | copy-start | bytes 393220
  4.3 37.7 %copy-start.7 = (s32[2]{0:T(128)S(1)}, s32[2]{0:T(128)}, u32[]{:S(2)}) copy-start(s32[2]{0:T(128)} %param.12) | copy-start | bytes 28
  4.6 30.7 %collective-permute-start.2 = (bf16[2,2128,128]{2,1,0:T(8,128)(2,1)S(1)}, bf16[2,2128,128]{2,1,0:T(8,128)(2,1)S(1)}, u32[]{:S(2)}, u32[]{:S(2)}) collective-permute-start(bf16[2,2128,128]{2,1,0:T(8,128)(2,1)S(1)} %shard_map.74.s0), channel_id=1, source_target_pairs={{0,32},{8,40},{16,48},{24,56},{32,0},{40,8},{48,16},{56,24},{64,96... | collective-permute-start | bytes 3268616 | tf_op jit(solution)/shard_map/ppermute | solution.py:21
  8.1 27.2 %collective-permute-start = (bf16[2,272,128]{2,1,0:T(8,128)(2,1)S(1)}, bf16[2,272,128]{2,1,0:T(8,128)(2,1)S(1)}, u32[]{:S(2)}, u32[]{:S(2)}) collective-permute-start(bf16[2,272,128]{2,1,0:T(8,128)(2,1)S(1)} %shard_map.73.q), channel_id=1, source_target_pairs={{0,16},{8,24},{16,0},{24,8},{32,48},{40,56},{48,32},{56,40},{64,80... | collective-permute-start | bytes 417800 | tf_op jit(solution)/shard_map/ppermute | solution.py:21
  22.9 12.4 %collective-permute-start.3 = (bf16[2,272,128]{2,1,0:T(8,128)(2,1)S(1)}, bf16[2,272,128]{2,1,0:T(8,128)(2,1)S(1)}, u32[]{:S(2)}, u32[]{:S(2)}) collective-permute-start(bf16[2,272,128]{2,1,0:T(8,128)(2,1)S(1)} %shard_map.73.q), channel_id=1, source_target_pairs={{0,96},{8,104},{16,112},{24,120},{32,64},{40,72},{48,80},{56,88},{... | collective-permute-start | bytes 417800 | tf_op jit(solution)/shard_map/ppermute | solution.py:21
  26.9 15.2 %collective-permute-start.4 = (bf16[2,2128,128]{2,1,0:T(8,128)(2,1)S(1)}, bf16[2,2128,128]{2,1,0:T(8,128)(2,1)S(1)}, u32[]{:S(2)}, u32[]{:S(2)}) collective-permute-start(bf16[2,2128,128]{2,1,0:T(8,128)(2,1)S(1)} %shard_map.74.s0), channel_id=1, source_target_pairs={{0,8},{8,0},{16,24},{24,16},{32,40},{40,32},{48,56},{56,48},{64,72... | collective-permute-start | bytes 3268616 | tf_op jit(solution)/shard_map/ppermute | solution.py:21
  35.3 0.7 copy-start.2
  36.0 6.1 %collective-permute-start.5 = (bf16[2,2128,128]{2,1,0:T(8,128)(2,1)S(1)}, bf16[2,2128,128]{2,1,0:T(8,128)(2,1)}, u32[]{:S(2)}, u32[]{:S(2)}) collective-permute-start(bf16[2,2128,128]{2,1,0:T(8,128)(2,1)S(1)} %collective-permute-done.2.s2), channel_id=1, source_target_pairs={{0,8},{8,0},{16,24},{24,16},{32,40},{40,32},{48,56},{56,48},{64,72... | collective-permute-start | bytes 3268616 | tf_op jit(solution)/shard_map/ppermute | solution.py:21
  37.9 10.4 %collective-permute-start.1 = (bf16[2,272,128]{2,1,0:T(8,128)(2,1)}, bf16[2,272,128]{2,1,0:T(8,128)(2,1)S(1)}, u32[]{:S(2)}, u32[]{:S(2)}) collective-permute-start(bf16[2,272,128]{2,1,0:T(8,128)(2,1)} %copy-done.2), channel_id=1, source_target_pairs={{0,96},{8,104},{16,112},{24,120},{32,64},{40,72},{48,80},{56,88},{... | collective-permute-start | bytes 417800 | tf_op jit(solution)/shard_map/ppermute | solution.py:21
  42.1 0.9 copy-start.3
  53.7 12.6 %collective-permute-start.6 = (bf16[2,272,128]{2,1,0:T(8,128)(2,1)S(1)}, bf16[2,272,128]{2,1,0:T(8,128)(2,1)S(1)}, u32[]{:S(2)}, u32[]{:S(2)}) collective-permute-start(bf16[2,272,128]{2,1,0:T(8,128)(2,1)S(1)} %shard_map.76), channel_id=1, source_target_pairs={{0,96},{8,104},{16,112},{24,120},{32,64},{40,72},{48,80},{56,88},{... | collective-permute-start | bytes 417800 | tf_op jit(solution)/shard_map/ppermute | solution.py:21
  62.3 22.0 %collective-permute-start.7 = (bf16[2,272,128]{2,1,0:T(8,128)(2,1)S(1)}, bf16[2,272,128]{2,1,0:T(8,128)(2,1)S(1)}, u32[]{:S(2)}, u32[]{:S(2)}) collective-permute-start(bf16[2,272,128]{2,1,0:T(8,128)(2,1)S(1)} %shard_map.77), channel_id=1, source_target_pairs={{0,96},{8,104},{16,112},{24,120},{32,64},{40,72},{48,80},{56,88},{... | collective-permute-start | bytes 417800 | tf_op jit(solution)/shard_map/ppermute | solution.py:21
  66.8 24.9 %collective-permute-start.8 = (bf16[2,272,128]{2,1,0:T(8,128)(2,1)S(1)}, bf16[2,272,128]{2,1,0:T(8,128)(2,1)S(1)}, u32[]{:S(2)}, u32[]{:S(2)}) collective-permute-start(bf16[2,272,128]{2,1,0:T(8,128)(2,1)S(1)} %shard_map.78), channel_id=1, source_target_pairs={{0,16},{8,24},{16,0},{24,8},{32,48},{40,56},{48,32},{56,40},{64,80... | collective-permute-start | bytes 417800 | tf_op jit(solution)/shard_map/ppermute | solution.py:21

commit v2 on v1

v2 whole, which is shorter than its diff:
```python
import functools

import jax
import jax.numpy as jnp
from jax import lax
from jax.experimental import pallas as pl
from jax.experimental.pallas import tpu as pltpu
from jax.sharding import PartitionSpec as P

HEAD = 128
NEG = -1e30
VMEM = pl.BlockSpec(memory_space=pltpu.VMEM)
SMEM = pl.BlockSpec(memory_space=pltpu.SMEM)
LIMIT = 48 * 1024 * 1024
PACK = 48 * 1024 * 1024
SCALE = 1.0 / HEAD**0.5


def swap(block, mask):
    count = lax.axis_size("ctx")
    return lax.ppermute(block, "ctx", [(i, i ^ mask) for i in range(count)])


def column(row, rows, period):
    r = lax.broadcasted_iota(jnp.int32, (rows, 128), 0) % period
    c = lax.broadcasted_iota(jnp.int32, (rows, 128), 1)
    spread = jnp.broadcast_to(row, (rows, 128))
    return jnp.sum(jnp.where(r == c, spread, 0.0), axis=1, keepdims=True)


def lane_row(spread):
    r = lax.broadcasted_iota(jnp.int32, (128, 128), 0)
    c = lax.broadcasted_iota(jnp.int32, (128, 128), 1)
    return jnp.sum(jnp.where(r == c, jnp.broadcast_to(spread, (128, 128)), 0.0), axis=0, keepdims=True)


def stat_block(lse):
    halves = jnp.concatenate([lane_row(lse[:128]), lane_row(lse[128:])], axis=0)
    hi = halves.astype(jnp.bfloat16).astype(jnp.float32)
    rest = halves - hi
    mid = rest.astype(jnp.bfloat16).astype(jnp.float32)
    low = rest - mid
    blank = jnp.zeros((10, 128), jnp.float32)
    return jnp.concatenate([hi, mid, low, blank], axis=0).astype(jnp.bfloat16)


def read_stats(block):
    block = block.astype(jnp.float32)
    halves = block[0:2] + block[2:4] + block[4:6]
    return jnp.concatenate([column(halves[0:1], 128, 128), column(halves[1:2], 128, 128)], axis=0)


def place_block(row):
    shape = (16, row.shape[1])
    line = lax.broadcasted_iota(jnp.int32, shape, 0)
    spread = jnp.broadcast_to(row, shape)
    pieces = jnp.where(line == 0, spread >> 7, jnp.where(line == 1, spread & 127, 0))
    return pieces.astype(jnp.float32).astype(jnp.bfloat16)


def put_places(out, s, at, places):
    out[s, at : at + 16, :] = jnp.zeros((16, HEAD), jnp.bfloat16)
    out[s, at : at + 16, 0 : places.shape[1]] = place_block(places[s : s + 1, :])


def read_places(block):
    block = block.astype(jnp.float32)
    return block[0:1] * 128.0 + block[1:2]


def pack_queries_kernel(tokens, queries, places, out):
    sessions, size, _ = out.shape
    for s in range(sessions):
        for h in range((size - 16) // tokens):
            out[s, h * tokens : (h + 1) * tokens, :] = queries[s, :, h * HEAD : (h + 1) * HEAD]
        put_places(out, s, size - 16, places)


def pack_queries(queries, places):
    sessions, tokens, width = queries.shape
    return pl.pallas_call(
        functools.partial(pack_queries_kernel, tokens),
        out_shape=jax.ShapeDtypeStruct((sessions, width // HEAD * tokens + 16, HEAD), jnp.bfloat16),
        in_specs=[VMEM] * 2,
        out_specs=VMEM,
        compiler_params=pltpu.CompilerParams(vmem_limit_bytes=LIMIT),
    )(queries, places)


def pack_keys_kernel(slots, fresh, places, k, v, nk, nv, out, spots, sems):
    copies = [pltpu.make_async_copy(places, spots, sems.at[4])]
    at = 0
    for i, (ref, size) in enumerate(((k, slots), (v, slots), (nk, fresh), (nv, fresh))):
        copies.append(pltpu.make_async_copy(ref, out.at[:, pl.ds(at, size)], sems.at[i]))
        at += size
    for copy in copies:
        copy.start()
    copies[0].wait()
    for s in range(out.shape[0]):
        put_places(out, s, at, spots)
    for copy in copies[1:]:
        copy.wait()


def pack_keys(places, k, v, nk, nv):
    sessions, slots, _ = k.shape
    fresh = nk.shape[1]
    shape = (sessions, 2 * (slots + fresh) + 16, HEAD)
    return pl.pallas_call(
        functools.partial(pack_keys_kernel, slots, fresh),
        out_shape=pltpu.VMEM(shape, jnp.bfloat16),
        in_specs=[pl.BlockSpec(memory_space=pltpu.HBM)] * 5,
        out_specs=VMEM,
        scratch_shapes=[pltpu.VMEM(places.shape, places.dtype), pltpu.SemaphoreType.DMA((5,))],
        compiler_params=pltpu.CompilerParams(vmem_limit_bytes=PACK),
    )(*(pltpu.with_memory_space_constraint(x, pltpu.HBM) for x in (places, k, v, nk, nv)))


def attend_kernel(scal, q, s0, s1, s2, s3, out):
    blocks = (s0, s1, s2, s3)
    sessions, size, _ = q.shape
    rows = size - 16
    fresh = 128 // len(blocks)
    slots = (s0.shape[1] - 16) // 2 - fresh
    nk = 2 * slots
    cells = lax.broadcasted_iota(jnp.int32, (1, slots), 1)
    nt = (((1,), (1,)), ((), ()))
    for s in range(sessions):
        mine = q[s, 0:rows, :]
        qpos = column(read_places(q[s, rows:size, :]), rows, fresh)
        kpos = [read_places(blk[s, nk + 2 * fresh : nk + 2 * fresh + 16, :])[:, 0:fresh] for blk in blocks]
        scores = []
        for b, blk in enumerate(blocks):
            got = lax.dot_general(mine, blk[s, 0:slots, :], nt, preferred_element_type=jnp.float32)
            scores.append(jnp.where(cells < scal[s] - scal[sessions + b], got, NEG))
        new_keys = jnp.concatenate([blk[s, nk : nk + fresh, :] for blk in blocks], axis=0)
        got = lax.dot_general(mine, new_keys, nt, preferred_element_type=jnp.float32)
        scores.append(jnp.where(jnp.concatenate(kpos, axis=1) <= qpos, got, NEG))
        values = [blk[s, slots:nk, :] for blk in blocks]
        values.append(jnp.concatenate([blk[s, nk + fresh : nk + 2 * fresh, :] for blk in blocks], axis=0))
        shift = SCALE * functools.reduce(jnp.maximum, [jnp.max(x, axis=1, keepdims=True) for x in scores])
        total = jnp.zeros((rows, 1), jnp.float32)
        summed = jnp.zeros((rows, HEAD), jnp.float32)
        for x, v in zip(scores, values):
            w = jnp.exp(x * SCALE - shift)
            total += jnp.sum(w, axis=1, keepdims=True)
            summed += jnp.dot(w.astype(jnp.bfloat16), v, preferred_element_type=jnp.float32)
        out[s, 0:rows, :] = (summed / total).astype(jnp.bfloat16)
        out[s, rows:size, :] = stat_block(shift + jnp.log(total))


def attend(scal, q, blocks):
    return pl.pallas_call(
        attend_kernel,
        out_shape=jax.ShapeDtypeStruct(q.shape, jnp.bfloat16),
        in_specs=[SMEM] + [VMEM] * (1 + len(blocks)),
        out_specs=VMEM,
        compiler_params=pltpu.CompilerParams(vmem_limit_bytes=LIMIT),
        cost_estimate=pl.CostEstimate(flops=q.size, bytes_accessed=0, transcendentals=0),
    )(scal, q, *blocks)


def merged(rows, messages):
    logs = [read_stats(m[rows : rows + 16, :]) for m in messages]
    top = functools.reduce(jnp.maximum, logs)
    shares = [jnp.exp(x - top) for x in logs]
    total = sum(shares)
    value = sum(m[:rows, :].astype(jnp.float32) * (x / total) for m, x in zip(messages, shares))
    return value, top + jnp.log(total)


def merge_kernel(own, came, out):
    sessions, size, _ = own.shape
    rows = size - 16
    for s in range(sessions):
        value, lse = merged(rows, [own[s], came[s]])
        out[s, 0:rows, :] = value.astype(jnp.bfloat16)
        out[s, rows:size, :] = stat_block(lse)
        out[s, size:, :] = jnp.zeros((out.shape[1] - size, HEAD), jnp.bfloat16)


def merge(own, came):
    sessions, size, _ = own.shape
    return pl.pallas_call(
        merge_kernel,
        out_shape=jax.ShapeDtypeStruct((sessions, size + 16, HEAD), jnp.bfloat16),
        in_specs=[VMEM, VMEM],
        out_specs=VMEM,
        compiler_params=pltpu.CompilerParams(vmem_limit_bytes=LIMIT),
    )(own, came)


def finish_kernel(one, two, three, out):
    sessions, tokens, width = out.shape
    rows = one.shape[1] - 16
    for s in range(sessions):
        value, _ = merged(rows, [one[s], two[s], three[s]])
        value = value.astype(jnp.bfloat16)
        for h in range(width // HEAD):
            out[s, :, h * HEAD : (h + 1) * HEAD] = value[h * tokens : (h + 1) * tokens, :]


def finish(one, two, three, tokens):
    sessions, size, _ = one.shape
    return pl.pallas_call(
        finish_kernel,
        out_shape=jax.ShapeDtypeStruct((sessions, tokens, (size - 16) // tokens * HEAD), jnp.bfloat16),
        in_specs=[VMEM] * 3,
        out_specs=VMEM,
        compiler_params=pltpu.CompilerParams(vmem_limit_bytes=LIMIT),
    )(one, two, three)


def per_device(queries, cache_keys, stored_values, new_keys, new_values, lengths, positions):
    member = lax.axis_index("ctx")
    tokens = queries.shape[1]
    slots = cache_keys.shape[1]
    bases = jnp.stack([member, member ^ 1, member ^ 4, member ^ 5]) * slots
    scal = jnp.concatenate([lengths, bases]).astype(jnp.int32)

    near_q = pack_queries(queries, positions)
    near_x = [swap(near_q[s], 12) for s in range(near_q.shape[0])]
    far_q = swap(near_q, 2)
    own = pack_keys(positions, cache_keys, stored_values, new_keys, new_values)
    x_own = swap(own, 4)
    pair = swap(own, 1)
    far_q, scal, *near_x = lax.optimization_barrier((far_q, scal, *near_x))
    far_x = swap(far_q, 12)
    x_own, far_x = lax.optimization_barrier((x_own, far_x))
    blocks = (own, pair, x_own, swap(x_own, 1))

    far_b = attend(scal, far_x, blocks)
    far_came = swap(far_b, 12)
    far_b, far_q = lax.optimization_barrier((far_b, far_q))
    far_a = attend(scal, far_q, blocks)
    far_came, far_a = lax.optimization_barrier((far_came, far_a))
    far = merge(far_a, far_came)
    back = swap(far, 2)

    far, near_q, *near_x = lax.optimization_barrier((far, near_q, *near_x))
    near_b = attend(scal, jnp.stack(near_x), blocks)
    near_came = swap(near_b, 12)
    near_b, near_q = lax.optimization_barrier((near_b, near_q))
    near_a = attend(scal, near_q, blocks)
    return finish(near_a, near_came, back, tokens)


def solution(mesh):
    spec = P("rep", "ctx", "tp")
    return jax.shard_map(
        per_device,
        mesh=mesh,
        in_specs=(spec, spec, spec, spec, spec, P("rep"), P("rep", "ctx")),
        out_specs=spec,
        check_vma=False,
    )
```

time: 93.7 us -> 86.9 us (0.927)
  the two profiles are of different devices: /device:TPU:40 before, /device:TPU:48 now
where the time goes in v2:
time: 86.9 us; the launch traced here: 86.5 us
  starting transfers between devices  53.3 us (61%)
  Pallas kernels  22.8 us (26%)
  waiting for transfers between devices  10.1 us (12%)
    ppermute x10, starting transfers between devices, swap(): return lax.ppermute(block, 'ctx', [(i, i ^ mask) for i in range(count)])  53.3 us
    pallas_call x4, Pallas kernels, attend(): pl.pallas_call(attend_kernel, out_shape=jax.ShapeDtypeStruct(q.shape, jnp...  19.8 us
    ppermute x10, waiting for transfers between devices, swap(): return lax.ppermute(block, 'ctx', [(i, i ^ mask) for i in range(count)])  10.1 us
  transfers between devices with their start and end apart: 10, of which 5 were waited for; matrix products, arithmetic and copies ran while one was open for 0% of the time, Pallas kernels for 17%

profile of v2, /device:TPU:48, one launch (start us, length us, event | category | flops | bytes accessed | tf_op | source)
XLA Modules:
  0.0 86.5 jit_solution(800633061740229514)
XLA Ops:
  0.0 0.0 copy-start.1
  0.0 0.0 copy-start
  0.0 0.0 copy-start.2
  0.0 1.3 %shard_map.74.s0 = bf16[2,2128,128]{2,1,0:T(8,128)(2,1)S(1)} custom-call(s32[2,32]{1,0:T(2,128)} %places.3, bf16[2,1024,128]{2,1,0:T(8,128)(2,1)} %k.1, bf16[2,1024,128]{2,1,0:T(8,128)(2,1)} %v.1, bf16[2,32,128]{2,1,0:T(8,128)(2,1)} %nk.1, bf16[2,32,128]{2,1,0:T(8,128)(2,1)} %nv.1), custom_call_target="tpu_custom_call" | custom-call | tf_op jit(solution)/shard_map/pallas_call | solution.py:109
  1.3 3.4 %collective-permute-start.3 = (bf16[2,2128,128]{2,1,0:T(8,128)(2,1)S(1)}, bf16[2,2128,128]{2,1,0:T(8,128)(2,1)S(1)}, u32[]{:S(2)}, u32[]{:S(2)}) collective-permute-start(bf16[2,2128,128]{2,1,0:T(8,128)(2,1)S(1)} %shard_map.74.s0), channel_id=1, source_target_pairs={{0,32},{8,40},{16,48},{24,56},{32,0},{40,8},{48,16},{56,24},{64,96... | collective-permute-start | bytes 3268616 | tf_op jit(solution)/shard_map/ppermute | solution.py:21
  4.7 0.0 copy-done.1
  4.7 0.0 copy-done
  4.8 14.8 %collective-permute-start = (bf16[2,272,128]{2,1,0:T(8,128)(2,1)S(1)}, bf16[2,272,128]{2,1,0:T(8,128)(2,1)S(1)}, u32[]{:S(2)}, u32[]{:S(2)}) collective-permute-start(bf16[2,272,128]{2,1,0:T(8,128)(2,1)S(1)} %shard_map.73.q), channel_id=1, source_target_pairs={{0,16},{8,24},{16,0},{24,8},{32,48},{40,56},{48,32},{56,40},{64,80... | collective-permute-start | bytes 417800 | tf_op jit(solution)/shard_map/ppermute | solution.py:21
  19.6 4.0 %collective-permute-start.2 = (bf16[272,128]{1,0:T(8,128)(2,1)S(1)}, bf16[272,128]{1,0:T(8,128)(2,1)S(1)}, u32[]{:S(2)}, u32[]{:S(2)}) collective-permute-start(bf16[272,128]{1,0:T(8,128)(2,1)S(1)} %get-tuple-element.31), channel_id=1, source_target_pairs={{0,96},{8,104},{16,112},{24,120},{32,64},{40,72},{48,80},{56,88},{... | collective-permute-start | bytes 208904 | tf_op jit(solution)/shard_map/ppermute | solution.py:21
  23.6 3.0 %collective-permute-start.1 = (bf16[272,128]{1,0:T(8,128)(2,1)S(1)}, bf16[272,128]{1,0:T(8,128)(2,1)S(1)}, u32[]{:S(2)}, u32[]{:S(2)}) collective-permute-start(bf16[272,128]{1,0:T(8,128)(2,1)S(1)} %get-tuple-element.32), channel_id=1, source_target_pairs={{0,96},{8,104},{16,112},{24,120},{32,64},{40,72},{48,80},{56,88},{... | collective-permute-start | bytes 208904 | tf_op jit(solution)/shard_map/ppermute | solution.py:21
  26.7 0.1 add_multiply_fusion
  26.8 0.0 copy-done.2
  26.8 0.1 pad_add_fusion.scal
  26.9 0.2 collective-permute-done.2
  27.0 4.0 %collective-permute-done.1 = bf16[272,128]{1,0:T(8,128)(2,1)S(1)} collective-permute-done((bf16[272,128]{1,0:T(8,128)(2,1)S(1)}, bf16[272,128]{1,0:T(8,128)(2,1)S(1)}, u32[]{:S(2)}, u32[]{:S(2)}) %collective-permute-start.1) | collective-permute-done | bytes 69664 | tf_op jit(solution)/shard_map/ppermute | solution.py:21
  31.1 1.0 %collective-permute-done.q = bf16[2,272,128]{2,1,0:T(8,128)(2,1)S(1)} collective-permute-done((bf16[2,272,128]{2,1,0:T(8,128)(2,1)S(1)}, bf16[2,272,128]{2,1,0:T(8,128)(2,1)S(1)}, u32[]{:S(2)}, u32[]{:S(2)}) %collective-permute-start) | collective-permute-done | bytes 139296 | tf_op jit(solution)/shard_map/ppermute | solution.py:21
  32.0 4.0 %collective-permute-start.4 = (bf16[2,272,128]{2,1,0:T(8,128)(2,1)S(1)}, bf16[2,272,128]{2,1,0:T(8,128)(2,1)S(1)}, u32[]{:S(2)}, u32[]{:S(2)}) collective-permute-start(bf16[2,272,128]{2,1,0:T(8,128)(2,1)S(1)} %collective-permute-done.q), channel_id=1, source_target_pairs={{0,96},{8,104},{16,112},{24,120},{32,64},{40,72},{48,80},{56,88},{... | collective-permute-start | bytes 417800 | tf_op jit(solution)/shard_map/ppermute | solution.py:21
  36.0 1.9 %collective-permute-start.5 = (bf16[2,2128,128]{2,1,0:T(8,128)(2,1)S(1)}, bf16[2,2128,128]{2,1,0:T(8,128)(2,1)S(1)}, u32[]{:S(2)}, u32[]{:S(2)}) collective-permute-start(bf16[2,2128,128]{2,1,0:T(8,128)(2,1)S(1)} %shard_map.74.s0), channel_id=1, source_target_pairs={{0,8},{8,0},{16,24},{24,16},{32,40},{40,32},{48,56},{56,48},{64,72... | collective-permute-start | bytes 3268616 | tf_op jit(solution)/shard_map/ppermute | solution.py:21
  37.9 2.2 %collective-permute-done.4.q = bf16[2,272,128]{2,1,0:T(8,128)(2,1)S(1)} collective-permute-done((bf16[2,272,128]{2,1,0:T(8,128)(2,1)S(1)}, bf16[2,272,128]{2,1,0:T(8,128)(2,1)S(1)}, u32[]{:S(2)}, u32[]{:S(2)}) %collective-permute-start.4) | collective-permute-done | bytes 139296 | tf_op jit(solution)/shard_map/ppermute | solution.py:21
  40.2 0.0 collective-permute-done.3.s2
  40.2 1.9 %collective-permute-start.6 = (bf16[2,2128,128]{2,1,0:T(8,128)(2,1)S(1)}, bf16[2,2128,128]{2,1,0:T(8,128)(2,1)S(1)}, u32[]{:S(2)}, u32[]{:S(2)}) collective-permute-start(bf16[2,2128,128]{2,1,0:T(8,128)(2,1)S(1)} %collective-permute-done.3.s2), channel_id=1, source_target_pairs={{0,8},{8,0},{16,24},{24,16},{32,40},{40,32},{48,56},{56,48},{64,72... | collective-permute-start | bytes 3268616 | tf_op jit(solution)/shard_map/ppermute | solution.py:21
  42.1 0.0 collective-permute-done.5.s1
  42.1 2.7 %collective-permute-done.6.s3 = bf16[2,2128,128]{2,1,0:T(8,128)(2,1)S(1)} collective-permute-done((bf16[2,2128,128]{2,1,0:T(8,128)(2,1)S(1)}, bf16[2,2128,128]{2,1,0:T(8,128)(2,1)S(1)}, u32[]{:S(2)}, u32[]{:S(2)}) %collective-permute-start.6) | collective-permute-done | bytes 1089568 | tf_op jit(solution)/shard_map/ppermute | solution.py:21
  44.8 5.0 %shard_map.75 = bf16[2,272,128]{2,1,0:T(8,128)(2,1)S(1)} custom-call(s32[6]{0:T(128)S(1)} %pad_add_fusion.scal, bf16[2,272,128]{2,1,0:T(8,128)(2,1)S(1)} %collective-permute-done.4.q, bf16[2,2128,128]{2,1,0:T(8,128)(2,1)S(1)} %shard_map.74.s0, bf16[2,2128,128]{2,1,0:T(8,128)(2,1)S(1)} %collective-permute-done.5.s1, ...), custom_call_target="tpu_custom_call" | custom-call | flops 69632 | tf_op jit(solution)/shard_map/pallas_call | solution.py:153
  49.7 4.0 %collective-permute-start.7 = (bf16[2,272,128]{2,1,0:T(8,128)(2,1)S(1)}, bf16[2,272,128]{2,1,0:T(8,128)(2,1)S(1)}, u32[]{:S(2)}, u32[]{:S(2)}) collective-permute-start(bf16[2,272,128]{2,1,0:T(8,128)(2,1)S(1)} %shard_map.75), channel_id=1, source_target_pairs={{0,96},{8,104},{16,112},{24,120},{32,64},{40,72},{48,80},{56,88},{... | collective-permute-start | bytes 417800 | tf_op jit(solution)/shard_map/ppermute | solution.py:21
  53.7 5.0 %shard_map.76.own = bf16[2,272,128]{2,1,0:T(8,128)(2,1)S(1)} custom-call(s32[6]{0:T(128)S(1)} %pad_add_fusion.scal, bf16[2,272,128]{2,1,0:T(8,128)(2,1)S(1)} %collective-permute-done.q, bf16[2,2128,128]{2,1,0:T(8,128)(2,1)S(1)} %shard_map.74.s0, bf16[2,2128,128]{2,1,0:T(8,128)(2,1)S(1)} %collective-permute-done.5.s1, ...), custom_call_target="tpu_custom_call" | custom-call | flops 69632 | tf_op jit(solution)/shard_map/pallas_call | solution.py:153
  58.7 0.0 collective-permute-done.7.came
  58.7 0.5 shard_map.77
  59.2 12.3 %collective-permute-start.9 = (bf16[2,288,128]{2,1,0:T(8,128)(2,1)S(1)}, bf16[2,288,128]{2,1,0:T(8,128)(2,1)S(1)}, u32[]{:S(2)}, u32[]{:S(2)}) collective-permute-start(bf16[2,288,128]{2,1,0:T(8,128)(2,1)S(1)} %shard_map.77), channel_id=1, source_target_pairs={{0,16},{8,24},{16,0},{24,8},{32,48},{40,56},{48,32},{56,40},{64,80... | collective-permute-start | bytes 442376 | tf_op jit(solution)/shard_map/ppermute | solution.py:21
  71.6 5.0 %shard_map.78 = bf16[2,272,128]{2,1,0:T(8,128)(2,1)S(1)} custom-call(s32[6]{0:T(128)S(1)} %pad_add_fusion.scal, bf16[2,272,128]{2,1,0:T(8,128)(2,1)S(1)} %pad_maximum_fusion.q, bf16[2,2128,128]{2,1,0:T(8,128)(2,1)S(1)} %shard_map.74.s0, bf16[2,2128,128]{2,1,0:T(8,128)(2,1)S(1)} %collective-permute-done.5.s1, ...), custom_call_target="tpu_custom_call" | custom-call | flops 69632 | tf_op jit(solution)/shard_map/pallas_call | solution.py:153
  76.5 3.8 %collective-permute-start.8 = (bf16[2,272,128]{2,1,0:T(8,128)(2,1)S(1)}, bf16[2,272,128]{2,1,0:T(8,128)(2,1)S(1)}, u32[]{:S(2)}, u32[]{:S(2)}) collective-permute-start(bf16[2,272,128]{2,1,0:T(8,128)(2,1)S(1)} %shard_map.78), channel_id=1, source_target_pairs={{0,96},{8,104},{16,112},{24,120},{32,64},{40,72},{48,80},{56,88},{... | collective-permute-start | bytes 417800 | tf_op jit(solution)/shard_map/ppermute | solution.py:21
  80.4 4.9 %shard_map.79.one = bf16[2,272,128]{2,1,0:T(8,128)(2,1)S(1)} custom-call(s32[6]{0:T(128)S(1)} %pad_add_fusion.scal, bf16[2,272,128]{2,1,0:T(8,128)(2,1)S(1)} %shard_map.73.q, bf16[2,2128,128]{2,1,0:T(8,128)(2,1)S(1)} %shard_map.74.s0, bf16[2,2128,128]{2,1,0:T(8,128)(2,1)S(1)} %collective-permute-done.5.s1, ...), custom_call_target="tpu_custom_call" | custom-call | flops 69632 | tf_op jit(solution)/shard_map/pallas_call | solution.py:153
  85.3 0.0 collective-permute-done.8.two
  85.3 0.0 collective-permute-done.9.three
  85.3 1.2 %shard_map.80 = bf16[2,32,1024]{2,1,0:T(8,128)(2,1)} custom-call(bf16[2,272,128]{2,1,0:T(8,128)(2,1)S(1)} %shard_map.79.one, bf16[2,272,128]{2,1,0:T(8,128)(2,1)S(1)} %collective-permute-done.8.two, bf16[2,288,128]{2,1,0:T(8,128)(2,1)S(1)} %collective-permute-done.9.three), custom_call_target="tpu_custom_call" | custom-call | tf_op jit(solution)/shard_map/pallas_call | solution.py:205
  (3 shorter events, 0.1 us)
Async XLA Ops:
  0.0 4.7 %copy-start.1 = (s32[2,32]{1,0:T(2,128)S(1)}, s32[2,32]{1,0:T(2,128)}, u32[]{:S(2)}) copy-start(s32[2,32]{1,0:T(2,128)} %places.3) | copy-start | bytes 772
  0.0 4.7 %copy-start = (bf16[2,32,1024]{2,1,0:T(8,128)(2,1)S(1)}, bf16[2,32,1024]{2,1,0:T(8,128)(2,1)}, u32[]{:S(2)}) copy-start(bf16[2,32,1024]{2,1,0:T(8,128)(2,1)} %queries.1) | copy-start | bytes 393220
  0.0 26.8 %copy-start.2 = (s32[2]{0:T(128)S(1)}, s32[2]{0:T(128)}, u32[]{:S(2)}) copy-start(s32[2]{0:T(128)} %param.12) | copy-start | bytes 28
  1.3 38.8 %collective-permute-start.3 = (bf16[2,2128,128]{2,1,0:T(8,128)(2,1)S(1)}, bf16[2,2128,128]{2,1,0:T(8,128)(2,1)S(1)}, u32[]{:S(2)}, u32[]{:S(2)}) collective-permute-start(bf16[2,2128,128]{2,1,0:T(8,128)(2,1)S(1)} %shard_map.74.s0), channel_id=1, source_target_pairs={{0,32},{8,40},{16,48},{24,56},{32,0},{40,8},{48,16},{56,24},{64,96... | collective-permute-start | bytes 3268616 | tf_op jit(solution)/shard_map/ppermute | solution.py:21
  4.8 27.2 %collective-permute-start = (bf16[2,272,128]{2,1,0:T(8,128)(2,1)S(1)}, bf16[2,272,128]{2,1,0:T(8,128)(2,1)S(1)}, u32[]{:S(2)}, u32[]{:S(2)}) collective-permute-start(bf16[2,272,128]{2,1,0:T(8,128)(2,1)S(1)} %shard_map.73.q), channel_id=1, source_target_pairs={{0,16},{8,24},{16,0},{24,8},{32,48},{40,56},{48,32},{56,40},{64,80... | collective-permute-start | bytes 417800 | tf_op jit(solution)/shard_map/ppermute | solution.py:21
  19.6 7.4 %collective-permute-start.2 = (bf16[272,128]{1,0:T(8,128)(2,1)S(1)}, bf16[272,128]{1,0:T(8,128)(2,1)S(1)}, u32[]{:S(2)}, u32[]{:S(2)}) collective-permute-start(bf16[272,128]{1,0:T(8,128)(2,1)S(1)} %get-tuple-element.31), channel_id=1, source_target_pairs={{0,96},{8,104},{16,112},{24,120},{32,64},{40,72},{48,80},{56,88},{... | collective-permute-start | bytes 208904 | tf_op jit(solution)/shard_map/ppermute | solution.py:21
  23.6 7.4 %collective-permute-start.1 = (bf16[272,128]{1,0:T(8,128)(2,1)S(1)}, bf16[272,128]{1,0:T(8,128)(2,1)S(1)}, u32[]{:S(2)}, u32[]{:S(2)}) collective-permute-start(bf16[272,128]{1,0:T(8,128)(2,1)S(1)} %get-tuple-element.32), channel_id=1, source_target_pairs={{0,96},{8,104},{16,112},{24,120},{32,64},{40,72},{48,80},{56,88},{... | collective-permute-start | bytes 208904 | tf_op jit(solution)/shard_map/ppermute | solution.py:21
  32.0 8.1 %collective-permute-start.4 = (bf16[2,272,128]{2,1,0:T(8,128)(2,1)S(1)}, bf16[2,272,128]{2,1,0:T(8,128)(2,1)S(1)}, u32[]{:S(2)}, u32[]{:S(2)}) collective-permute-start(bf16[2,272,128]{2,1,0:T(8,128)(2,1)S(1)} %collective-permute-done.q), channel_id=1, source_target_pairs={{0,96},{8,104},{16,112},{24,120},{32,64},{40,72},{48,80},{56,88},{... | collective-permute-start | bytes 417800 | tf_op jit(solution)/shard_map/ppermute | solution.py:21
  36.0 6.1 %collective-permute-start.5 = (bf16[2,2128,128]{2,1,0:T(8,128)(2,1)S(1)}, bf16[2,2128,128]{2,1,0:T(8,128)(2,1)S(1)}, u32[]{:S(2)}, u32[]{:S(2)}) collective-permute-start(bf16[2,2128,128]{2,1,0:T(8,128)(2,1)S(1)} %shard_map.74.s0), channel_id=1, source_target_pairs={{0,8},{8,0},{16,24},{24,16},{32,40},{40,32},{48,56},{56,48},{64,72... | collective-permute-start | bytes 3268616 | tf_op jit(solution)/shard_map/ppermute | solution.py:21
  40.2 4.6 %collective-permute-start.6 = (bf16[2,2128,128]{2,1,0:T(8,128)(2,1)S(1)}, bf16[2,2128,128]{2,1,0:T(8,128)(2,1)S(1)}, u32[]{:S(2)}, u32[]{:S(2)}) collective-permute-start(bf16[2,2128,128]{2,1,0:T(8,128)(2,1)S(1)} %collective-permute-done.3.s2), channel_id=1, source_target_pairs={{0,8},{8,0},{16,24},{24,16},{32,40},{40,32},{48,56},{56,48},{64,72... | collective-permute-start | bytes 3268616 | tf_op jit(solution)/shard_map/ppermute | solution.py:21
  49.7 9.0 %collective-permute-start.7 = (bf16[2,272,128]{2,1,0:T(8,128)(2,1)S(1)}, bf16[2,272,128]{2,1,0:T(8,128)(2,1)S(1)}, u32[]{:S(2)}, u32[]{:S(2)}) collective-permute-start(bf16[2,272,128]{2,1,0:T(8,128)(2,1)S(1)} %shard_map.75), channel_id=1, source_target_pairs={{0,96},{8,104},{16,112},{24,120},{32,64},{40,72},{48,80},{56,88},{... | collective-permute-start | bytes 417800 | tf_op jit(solution)/shard_map/ppermute | solution.py:21
  59.2 26.1 %collective-permute-start.9 = (bf16[2,288,128]{2,1,0:T(8,128)(2,1)S(1)}, bf16[2,288,128]{2,1,0:T(8,128)(2,1)S(1)}, u32[]{:S(2)}, u32[]{:S(2)}) collective-permute-start(bf16[2,288,128]{2,1,0:T(8,128)(2,1)S(1)} %shard_map.77), channel_id=1, source_target_pairs={{0,16},{8,24},{16,0},{24,8},{32,48},{40,56},{48,32},{56,40},{64,80... | collective-permute-start | bytes 442376 | tf_op jit(solution)/shard_map/ppermute | solution.py:21
  76.5 8.8 %collective-permute-start.8 = (bf16[2,272,128]{2,1,0:T(8,128)(2,1)S(1)}, bf16[2,272,128]{2,1,0:T(8,128)(2,1)S(1)}, u32[]{:S(2)}, u32[]{:S(2)}) collective-permute-start(bf16[2,272,128]{2,1,0:T(8,128)(2,1)S(1)} %shard_map.78), channel_id=1, source_target_pairs={{0,96},{8,104},{16,112},{24,120},{32,64},{40,72},{48,80},{56,88},{... | collective-permute-start | bytes 417800 | tf_op jit(solution)/shard_map/ppermute | solution.py:21

commit v3 on v2

--- a/solution.py
+++ b/solution.py
@@ -125,28 +125,52 @@
     nk = 2 * slots
     cells = lax.broadcasted_iota(jnp.int32, (1, slots), 1)
     nt = (((1,), (1,)), ((), ()))
-    for s in range(sessions):
+    left = [[scal[s] - scal[sessions + b] for b in range(len(blocks))] for s in range(sessions)]
+
+    def score(s, b, masked):
         mine = q[s, 0:rows, :]
+        if b < len(blocks):
+            got = lax.dot_general(mine, blocks[b][s, 0:slots, :], nt, preferred_element_type=jnp.float32)
+            return jnp.where(cells < left[s][b], got, NEG) if masked else got
         qpos = column(read_places(q[s, rows:size, :]), rows, fresh)
         kpos = [read_places(blk[s, nk + 2 * fresh : nk + 2 * fresh + 16, :])[:, 0:fresh] for blk in blocks]
-        scores = []
-        for b, blk in enumerate(blocks):
-            got = lax.dot_general(mine, blk[s, 0:slots, :], nt, preferred_element_type=jnp.float32)
-            scores.append(jnp.where(cells < scal[s] - scal[sessions + b], got, NEG))
         new_keys = jnp.concatenate([blk[s, nk : nk + fresh, :] for blk in blocks], axis=0)
         got = lax.dot_general(mine, new_keys, nt, preferred_element_type=jnp.float32)
-        scores.append(jnp.where(jnp.concatenate(kpos, axis=1) <= qpos, got, NEG))
-        values = [blk[s, slots:nk, :] for blk in blocks]
-        values.append(jnp.concatenate([blk[s, nk + fresh : nk + 2 * fresh, :] for blk in blocks], axis=0))
-        shift = SCALE * functools.reduce(jnp.maximum, [jnp.max(x, axis=1, keepdims=True) for x in scores])
-        total = jnp.zeros((rows, 1), jnp.float32)
-        summed = jnp.zeros((rows, HEAD), jnp.float32)
-        for x, v in zip(scores, values):
-            w = jnp.exp(x * SCALE - shift)
-            total += jnp.sum(w, axis=1, keepdims=True)
-            summed += jnp.dot(w.astype(jnp.bfloat16), v, preferred_element_type=jnp.float32)
-        out[s, 0:rows, :] = (summed / total).astype(jnp.bfloat16)
-        out[s, rows:size, :] = stat_block(shift + jnp.log(total))
+        return jnp.where(jnp.concatenate(kpos, axis=1) <= qpos, got, NEG)
+
+    def weigh(s, b, got, state):
+        shift = jnp.max(got, axis=1, keepdims=True) * SCALE
+        if state is not None:
+            shift = jnp.maximum(shift, state[0])
+        w = jnp.exp(got * SCALE - shift)
+        total = jnp.sum(w, axis=1, keepdims=True)
+        if b < len(blocks):
+            v = blocks[b][s, slots:nk, :]
+        else:
+            v = jnp.concatenate([blk[s, nk + fresh : nk + 2 * fresh, :] for blk in blocks], axis=0)
+        summed = jnp.dot(w.astype(jnp.bfloat16), v, preferred_element_type=jnp.float32)
+        if state is not None:
+            scale = jnp.exp(state[0] - shift)
+            total += scale * state[1]
+            summed += scale * state[2]
+        return shift, total, summed
+
+    def body(masked):
+        units = [(s, b) for b in (len(blocks), *range(len(blocks))) for s in range(sessions)]
+        states = [None] * sessions
+        ahead = score(*units[0], masked)
+        for n, (s, b) in enumerate(units):
+            got = ahead
+            if n + 1 < len(units):
+                ahead = score(*units[n + 1], masked)
+            states[s] = weigh(s, b, got, states[s])
+        for s, (shift, total, summed) in enumerate(states):
+            out[s, 0:rows, :] = (summed / total).astype(jnp.bfloat16)
+            out[s, rows:size, :] = stat_block(shift + jnp.log(total))
+
+    full = functools.reduce(jnp.logical_and, [x >= slots for row in left for x in row])
+    pl.when(full)(lambda: body(False))
+    pl.when(jnp.logical_not(full))(lambda: body(True))
 
 
 def attend(scal, q, blocks):

time: 86.9 us -> 85.8 us (0.987)
  Pallas kernels: 22.8 us -> 20 us
  starting transfers between devices: 53.3 us -> 54.9 us
    pallas_call x4, Pallas kernels: 19.8 us -> 17.1 us  [attend(): pl.pallas_call(attend_kernel, out_shape=jax.ShapeDtypeStruct(q.shape, jnp...]
    ppermute x10, starting transfers between devices: 53.3 us -> 54.9 us  [swap(): return lax.ppermute(block, 'ctx', [(i, i ^ mask) for i in range(count)])]
  transfers between devices with their start and end apart: 10 -> 10, of which waited for: 5 -> 5; matrix products, arithmetic and copies ran while one was open for 0% -> 0% of each run, Pallas kernels for 17% -> 15%
where the time goes in v3:
time: 85.8 us; the launch traced here: 85.3 us
  starting transfers between devices  54.9 us (64%)
  Pallas kernels  20 us (23%)
  waiting for transfers between devices  10.1 us (12%)
    ppermute x10, starting transfers between devices, swap(): return lax.ppermute(block, 'ctx', [(i, i ^ mask) for i in range(count)])  54.9 us
    pallas_call x4, Pallas kernels, attend(): pl.pallas_call(attend_kernel, out_shape=jax.ShapeDtypeStruct(q.shape, jnp...  17.1 us
    ppermute x10, waiting for transfers between devices, swap(): return lax.ppermute(block, 'ctx', [(i, i ^ mask) for i in range(count)])  10.1 us
  transfers between devices with their start and end apart: 10, of which 5 were waited for; matrix products, arithmetic and copies ran while one was open for 0% of the time, Pallas kernels for 15%

profile of v3, /device:TPU:48, one launch (start us, length us, event | category | flops | bytes accessed | tf_op | source)
XLA Modules:
  0.0 85.3 jit_solution(7948241867735637478)
XLA Ops:
  0.0 0.0 copy-start.1
  0.0 0.0 copy-start
  0.0 0.0 copy-start.2
  0.0 1.3 %shard_map.74.s0 = bf16[2,2128,128]{2,1,0:T(8,128)(2,1)S(1)} custom-call(s32[2,32]{1,0:T(2,128)} %places.3, bf16[2,1024,128]{2,1,0:T(8,128)(2,1)} %k.1, bf16[2,1024,128]{2,1,0:T(8,128)(2,1)} %v.1, bf16[2,32,128]{2,1,0:T(8,128)(2,1)} %nk.1, bf16[2,32,128]{2,1,0:T(8,128)(2,1)} %nv.1), custom_call_target="tpu_custom_call" | custom-call | tf_op jit(solution)/shard_map/pallas_call | solution.py:109
  1.3 3.4 %collective-permute-start.3 = (bf16[2,2128,128]{2,1,0:T(8,128)(2,1)S(1)}, bf16[2,2128,128]{2,1,0:T(8,128)(2,1)S(1)}, u32[]{:S(2)}, u32[]{:S(2)}) collective-permute-start(bf16[2,2128,128]{2,1,0:T(8,128)(2,1)S(1)} %shard_map.74.s0), channel_id=1, source_target_pairs={{0,32},{8,40},{16,48},{24,56},{32,0},{40,8},{48,16},{56,24},{64,96... | collective-permute-start | bytes 3268616 | tf_op jit(solution)/shard_map/ppermute | solution.py:21
  4.7 0.0 copy-done.1
  4.7 0.0 copy-done
  4.8 14.8 %collective-permute-start = (bf16[2,272,128]{2,1,0:T(8,128)(2,1)S(1)}, bf16[2,272,128]{2,1,0:T(8,128)(2,1)S(1)}, u32[]{:S(2)}, u32[]{:S(2)}) collective-permute-start(bf16[2,272,128]{2,1,0:T(8,128)(2,1)S(1)} %shard_map.73.q), channel_id=1, source_target_pairs={{0,16},{8,24},{16,0},{24,8},{32,48},{40,56},{48,32},{56,40},{64,80... | collective-permute-start | bytes 417800 | tf_op jit(solution)/shard_map/ppermute | solution.py:21
  19.6 4.0 %collective-permute-start.2 = (bf16[272,128]{1,0:T(8,128)(2,1)S(1)}, bf16[272,128]{1,0:T(8,128)(2,1)S(1)}, u32[]{:S(2)}, u32[]{:S(2)}) collective-permute-start(bf16[272,128]{1,0:T(8,128)(2,1)S(1)} %get-tuple-element.31), channel_id=1, source_target_pairs={{0,96},{8,104},{16,112},{24,120},{32,64},{40,72},{48,80},{56,88},{... | collective-permute-start | bytes 208904 | tf_op jit(solution)/shard_map/ppermute | solution.py:21
  23.6 3.0 %collective-permute-start.1 = (bf16[272,128]{1,0:T(8,128)(2,1)S(1)}, bf16[272,128]{1,0:T(8,128)(2,1)S(1)}, u32[]{:S(2)}, u32[]{:S(2)}) collective-permute-start(bf16[272,128]{1,0:T(8,128)(2,1)S(1)} %get-tuple-element.32), channel_id=1, source_target_pairs={{0,96},{8,104},{16,112},{24,120},{32,64},{40,72},{48,80},{56,88},{... | collective-permute-start | bytes 208904 | tf_op jit(solution)/shard_map/ppermute | solution.py:21
  26.7 0.1 add_multiply_fusion
  26.8 0.0 copy-done.2
  26.8 0.1 pad_add_fusion.scal
  26.9 0.2 collective-permute-done.2
  27.0 4.0 %collective-permute-done.1 = bf16[272,128]{1,0:T(8,128)(2,1)S(1)} collective-permute-done((bf16[272,128]{1,0:T(8,128)(2,1)S(1)}, bf16[272,128]{1,0:T(8,128)(2,1)S(1)}, u32[]{:S(2)}, u32[]{:S(2)}) %collective-permute-start.1) | collective-permute-done | bytes 69664 | tf_op jit(solution)/shard_map/ppermute | solution.py:21
  31.1 1.0 %collective-permute-done.q = bf16[2,272,128]{2,1,0:T(8,128)(2,1)S(1)} collective-permute-done((bf16[2,272,128]{2,1,0:T(8,128)(2,1)S(1)}, bf16[2,272,128]{2,1,0:T(8,128)(2,1)S(1)}, u32[]{:S(2)}, u32[]{:S(2)}) %collective-permute-start) | collective-permute-done | bytes 139296 | tf_op jit(solution)/shard_map/ppermute | solution.py:21
  32.0 4.0 %collective-permute-start.4 = (bf16[2,272,128]{2,1,0:T(8,128)(2,1)S(1)}, bf16[2,272,128]{2,1,0:T(8,128)(2,1)S(1)}, u32[]{:S(2)}, u32[]{:S(2)}) collective-permute-start(bf16[2,272,128]{2,1,0:T(8,128)(2,1)S(1)} %collective-permute-done.q), channel_id=1, source_target_pairs={{0,96},{8,104},{16,112},{24,120},{32,64},{40,72},{48,80},{56,88},{... | collective-permute-start | bytes 417800 | tf_op jit(solution)/shard_map/ppermute | solution.py:21
  36.0 1.9 %collective-permute-start.5 = (bf16[2,2128,128]{2,1,0:T(8,128)(2,1)S(1)}, bf16[2,2128,128]{2,1,0:T(8,128)(2,1)S(1)}, u32[]{:S(2)}, u32[]{:S(2)}) collective-permute-start(bf16[2,2128,128]{2,1,0:T(8,128)(2,1)S(1)} %shard_map.74.s0), channel_id=1, source_target_pairs={{0,8},{8,0},{16,24},{24,16},{32,40},{40,32},{48,56},{56,48},{64,72... | collective-permute-start | bytes 3268616 | tf_op jit(solution)/shard_map/ppermute | solution.py:21
  37.9 2.2 %collective-permute-done.4.q = bf16[2,272,128]{2,1,0:T(8,128)(2,1)S(1)} collective-permute-done((bf16[2,272,128]{2,1,0:T(8,128)(2,1)S(1)}, bf16[2,272,128]{2,1,0:T(8,128)(2,1)S(1)}, u32[]{:S(2)}, u32[]{:S(2)}) %collective-permute-start.4) | collective-permute-done | bytes 139296 | tf_op jit(solution)/shard_map/ppermute | solution.py:21
  40.2 0.0 collective-permute-done.3.s2
  40.2 1.9 %collective-permute-start.6 = (bf16[2,2128,128]{2,1,0:T(8,128)(2,1)S(1)}, bf16[2,2128,128]{2,1,0:T(8,128)(2,1)S(1)}, u32[]{:S(2)}, u32[]{:S(2)}) collective-permute-start(bf16[2,2128,128]{2,1,0:T(8,128)(2,1)S(1)} %collective-permute-done.3.s2), channel_id=1, source_target_pairs={{0,8},{8,0},{16,24},{24,16},{32,40},{40,32},{48,56},{56,48},{64,72... | collective-permute-start | bytes 3268616 | tf_op jit(solution)/shard_map/ppermute | solution.py:21
  42.1 0.0 collective-permute-done.5.s1
  42.1 2.7 %collective-permute-done.6.s3 = bf16[2,2128,128]{2,1,0:T(8,128)(2,1)S(1)} collective-permute-done((bf16[2,2128,128]{2,1,0:T(8,128)(2,1)S(1)}, bf16[2,2128,128]{2,1,0:T(8,128)(2,1)S(1)}, u32[]{:S(2)}, u32[]{:S(2)}) %collective-permute-start.6) | collective-permute-done | bytes 1089568 | tf_op jit(solution)/shard_map/ppermute | solution.py:21
  44.8 4.2 %shard_map.75 = bf16[2,272,128]{2,1,0:T(8,128)(2,1)S(1)} custom-call(s32[6]{0:T(128)S(1)} %pad_add_fusion.scal, bf16[2,272,128]{2,1,0:T(8,128)(2,1)S(1)} %collective-permute-done.4.q, bf16[2,2128,128]{2,1,0:T(8,128)(2,1)S(1)} %shard_map.74.s0, bf16[2,2128,128]{2,1,0:T(8,128)(2,1)S(1)} %collective-permute-done.5.s1, ...), custom_call_target="tpu_custom_call" | custom-call | flops 69632 | tf_op jit(solution)/shard_map/pallas_call | solution.py:177
  48.9 4.6 %collective-permute-start.7 = (bf16[2,272,128]{2,1,0:T(8,128)(2,1)S(1)}, bf16[2,272,128]{2,1,0:T(8,128)(2,1)S(1)}, u32[]{:S(2)}, u32[]{:S(2)}) collective-permute-start(bf16[2,272,128]{2,1,0:T(8,128)(2,1)S(1)} %shard_map.75), channel_id=1, source_target_pairs={{0,96},{8,104},{16,112},{24,120},{32,64},{40,72},{48,80},{56,88},{... | collective-permute-start | bytes 417800 | tf_op jit(solution)/shard_map/ppermute | solution.py:21
  53.5 4.4 %shard_map.76.own = bf16[2,272,128]{2,1,0:T(8,128)(2,1)S(1)} custom-call(s32[6]{0:T(128)S(1)} %pad_add_fusion.scal, bf16[2,272,128]{2,1,0:T(8,128)(2,1)S(1)} %collective-permute-done.q, bf16[2,2128,128]{2,1,0:T(8,128)(2,1)S(1)} %shard_map.74.s0, bf16[2,2128,128]{2,1,0:T(8,128)(2,1)S(1)} %collective-permute-done.5.s1, ...), custom_call_target="tpu_custom_call" | custom-call | flops 69632 | tf_op jit(solution)/shard_map/pallas_call | solution.py:177
  57.9 0.0 collective-permute-done.7.came
  57.9 0.5 shard_map.77
  58.4 12.1 %collective-permute-start.9 = (bf16[2,288,128]{2,1,0:T(8,128)(2,1)S(1)}, bf16[2,288,128]{2,1,0:T(8,128)(2,1)S(1)}, u32[]{:S(2)}, u32[]{:S(2)}) collective-permute-start(bf16[2,288,128]{2,1,0:T(8,128)(2,1)S(1)} %shard_map.77), channel_id=1, source_target_pairs={{0,16},{8,24},{16,0},{24,8},{32,48},{40,56},{48,32},{56,40},{64,80... | collective-permute-start | bytes 442376 | tf_op jit(solution)/shard_map/ppermute | solution.py:21
  70.6 4.4 %shard_map.78 = bf16[2,272,128]{2,1,0:T(8,128)(2,1)S(1)} custom-call(s32[6]{0:T(128)S(1)} %pad_add_fusion.scal, bf16[2,272,128]{2,1,0:T(8,128)(2,1)S(1)} %pad_maximum_fusion.q, bf16[2,2128,128]{2,1,0:T(8,128)(2,1)S(1)} %shard_map.74.s0, bf16[2,2128,128]{2,1,0:T(8,128)(2,1)S(1)} %collective-permute-done.5.s1, ...), custom_call_target="tpu_custom_call" | custom-call | flops 69632 | tf_op jit(solution)/shard_map/pallas_call | solution.py:177
  75.0 5.0 %collective-permute-start.8 = (bf16[2,272,128]{2,1,0:T(8,128)(2,1)S(1)}, bf16[2,272,128]{2,1,0:T(8,128)(2,1)S(1)}, u32[]{:S(2)}, u32[]{:S(2)}) collective-permute-start(bf16[2,272,128]{2,1,0:T(8,128)(2,1)S(1)} %shard_map.78), channel_id=1, source_target_pairs={{0,96},{8,104},{16,112},{24,120},{32,64},{40,72},{48,80},{56,88},{... | collective-permute-start | bytes 417800 | tf_op jit(solution)/shard_map/ppermute | solution.py:21
  80.0 4.1 %shard_map.79.one = bf16[2,272,128]{2,1,0:T(8,128)(2,1)S(1)} custom-call(s32[6]{0:T(128)S(1)} %pad_add_fusion.scal, bf16[2,272,128]{2,1,0:T(8,128)(2,1)S(1)} %shard_map.73.q, bf16[2,2128,128]{2,1,0:T(8,128)(2,1)S(1)} %shard_map.74.s0, bf16[2,2128,128]{2,1,0:T(8,128)(2,1)S(1)} %collective-permute-done.5.s1, ...), custom_call_target="tpu_custom_call" | custom-call | flops 69632 | tf_op jit(solution)/shard_map/pallas_call | solution.py:177
  84.1 0.0 collective-permute-done.8.two
  84.2 0.0 collective-permute-done.9.three
  84.2 1.2 %shard_map.80 = bf16[2,32,1024]{2,1,0:T(8,128)(2,1)} custom-call(bf16[2,272,128]{2,1,0:T(8,128)(2,1)S(1)} %shard_map.79.one, bf16[2,272,128]{2,1,0:T(8,128)(2,1)S(1)} %collective-permute-done.8.two, bf16[2,288,128]{2,1,0:T(8,128)(2,1)S(1)} %collective-permute-done.9.three), custom_call_target="tpu_custom_call" | custom-call | tf_op jit(solution)/shard_map/pallas_call | solution.py:229
  (3 shorter events, 0.1 us)
Async XLA Ops:
  0.0 4.7 %copy-start.1 = (s32[2,32]{1,0:T(2,128)S(1)}, s32[2,32]{1,0:T(2,128)}, u32[]{:S(2)}) copy-start(s32[2,32]{1,0:T(2,128)} %places.3) | copy-start | bytes 772
  0.0 4.7 %copy-start = (bf16[2,32,1024]{2,1,0:T(8,128)(2,1)S(1)}, bf16[2,32,1024]{2,1,0:T(8,128)(2,1)}, u32[]{:S(2)}) copy-start(bf16[2,32,1024]{2,1,0:T(8,128)(2,1)} %queries.1) | copy-start | bytes 393220
  0.0 26.8 %copy-start.2 = (s32[2]{0:T(128)S(1)}, s32[2]{0:T(128)}, u32[]{:S(2)}) copy-start(s32[2]{0:T(128)} %param.12) | copy-start | bytes 28
  1.3 38.8 %collective-permute-start.3 = (bf16[2,2128,128]{2,1,0:T(8,128)(2,1)S(1)}, bf16[2,2128,128]{2,1,0:T(8,128)(2,1)S(1)}, u32[]{:S(2)}, u32[]{:S(2)}) collective-permute-start(bf16[2,2128,128]{2,1,0:T(8,128)(2,1)S(1)} %shard_map.74.s0), channel_id=1, source_target_pairs={{0,32},{8,40},{16,48},{24,56},{32,0},{40,8},{48,16},{56,24},{64,96... | collective-permute-start | bytes 3268616 | tf_op jit(solution)/shard_map/ppermute | solution.py:21
  4.8 27.2 %collective-permute-start = (bf16[2,272,128]{2,1,0:T(8,128)(2,1)S(1)}, bf16[2,272,128]{2,1,0:T(8,128)(2,1)S(1)}, u32[]{:S(2)}, u32[]{:S(2)}) collective-permute-start(bf16[2,272,128]{2,1,0:T(8,128)(2,1)S(1)} %shard_map.73.q), channel_id=1, source_target_pairs={{0,16},{8,24},{16,0},{24,8},{32,48},{40,56},{48,32},{56,40},{64,80... | collective-permute-start | bytes 417800 | tf_op jit(solution)/shard_map/ppermute | solution.py:21
  19.6 7.4 %collective-permute-start.2 = (bf16[272,128]{1,0:T(8,128)(2,1)S(1)}, bf16[272,128]{1,0:T(8,128)(2,1)S(1)}, u32[]{:S(2)}, u32[]{:S(2)}) collective-permute-start(bf16[272,128]{1,0:T(8,128)(2,1)S(1)} %get-tuple-element.31), channel_id=1, source_target_pairs={{0,96},{8,104},{16,112},{24,120},{32,64},{40,72},{48,80},{56,88},{... | collective-permute-start | bytes 208904 | tf_op jit(solution)/shard_map/ppermute | solution.py:21
  23.6 7.4 %collective-permute-start.1 = (bf16[272,128]{1,0:T(8,128)(2,1)S(1)}, bf16[272,128]{1,0:T(8,128)(2,1)S(1)}, u32[]{:S(2)}, u32[]{:S(2)}) collective-permute-start(bf16[272,128]{1,0:T(8,128)(2,1)S(1)} %get-tuple-element.32), channel_id=1, source_target_pairs={{0,96},{8,104},{16,112},{24,120},{32,64},{40,72},{48,80},{56,88},{... | collective-permute-start | bytes 208904 | tf_op jit(solution)/shard_map/ppermute | solution.py:21
  32.0 8.1 %collective-permute-start.4 = (bf16[2,272,128]{2,1,0:T(8,128)(2,1)S(1)}, bf16[2,272,128]{2,1,0:T(8,128)(2,1)S(1)}, u32[]{:S(2)}, u32[]{:S(2)}) collective-permute-start(bf16[2,272,128]{2,1,0:T(8,128)(2,1)S(1)} %collective-permute-done.q), channel_id=1, source_target_pairs={{0,96},{8,104},{16,112},{24,120},{32,64},{40,72},{48,80},{56,88},{... | collective-permute-start | bytes 417800 | tf_op jit(solution)/shard_map/ppermute | solution.py:21
  36.0 6.1 %collective-permute-start.5 = (bf16[2,2128,128]{2,1,0:T(8,128)(2,1)S(1)}, bf16[2,2128,128]{2,1,0:T(8,128)(2,1)S(1)}, u32[]{:S(2)}, u32[]{:S(2)}) collective-permute-start(bf16[2,2128,128]{2,1,0:T(8,128)(2,1)S(1)} %shard_map.74.s0), channel_id=1, source_target_pairs={{0,8},{8,0},{16,24},{24,16},{32,40},{40,32},{48,56},{56,48},{64,72... | collective-permute-start | bytes 3268616 | tf_op jit(solution)/shard_map/ppermute | solution.py:21
  40.2 4.6 %collective-permute-start.6 = (bf16[2,2128,128]{2,1,0:T(8,128)(2,1)S(1)}, bf16[2,2128,128]{2,1,0:T(8,128)(2,1)S(1)}, u32[]{:S(2)}, u32[]{:S(2)}) collective-permute-start(bf16[2,2128,128]{2,1,0:T(8,128)(2,1)S(1)} %collective-permute-done.3.s2), channel_id=1, source_target_pairs={{0,8},{8,0},{16,24},{24,16},{32,40},{40,32},{48,56},{56,48},{64,72... | collective-permute-start | bytes 3268616 | tf_op jit(solution)/shard_map/ppermute | solution.py:21
  48.9 9.0 %collective-permute-start.7 = (bf16[2,272,128]{2,1,0:T(8,128)(2,1)S(1)}, bf16[2,272,128]{2,1,0:T(8,128)(2,1)S(1)}, u32[]{:S(2)}, u32[]{:S(2)}) collective-permute-start(bf16[2,272,128]{2,1,0:T(8,128)(2,1)S(1)} %shard_map.75), channel_id=1, source_target_pairs={{0,96},{8,104},{16,112},{24,120},{32,64},{40,72},{48,80},{56,88},{... | collective-permute-start | bytes 417800 | tf_op jit(solution)/shard_map/ppermute | solution.py:21
  58.4 25.8 %collective-permute-start.9 = (bf16[2,288,128]{2,1,0:T(8,128)(2,1)S(1)}, bf16[2,288,128]{2,1,0:T(8,128)(2,1)S(1)}, u32[]{:S(2)}, u32[]{:S(2)}) collective-permute-start(bf16[2,288,128]{2,1,0:T(8,128)(2,1)S(1)} %shard_map.77), channel_id=1, source_target_pairs={{0,16},{8,24},{16,0},{24,8},{32,48},{40,56},{48,32},{56,40},{64,80... | collective-permute-start | bytes 442376 | tf_op jit(solution)/shard_map/ppermute | solution.py:21
  75.0 9.2 %collective-permute-start.8 = (bf16[2,272,128]{2,1,0:T(8,128)(2,1)S(1)}, bf16[2,272,128]{2,1,0:T(8,128)(2,1)S(1)}, u32[]{:S(2)}, u32[]{:S(2)}) collective-permute-start(bf16[2,272,128]{2,1,0:T(8,128)(2,1)S(1)} %shard_map.78), channel_id=1, source_target_pairs={{0,96},{8,104},{16,112},{24,120},{32,64},{40,72},{48,80},{56,88},{... | collective-permute-start | bytes 417800 | tf_op jit(solution)/shard_map/ppermute | solution.py:21

commit v4 on v3

--- a/solution.py
+++ b/solution.py
@@ -12,6 +12,7 @@
 VMEM = pl.BlockSpec(memory_space=pltpu.VMEM)
 SMEM = pl.BlockSpec(memory_space=pltpu.SMEM)
 LIMIT = 48 * 1024 * 1024
+STEER = 16000000000
 PACK = 48 * 1024 * 1024
 SCALE = 1.0 / HEAD**0.5
 
@@ -184,6 +185,21 @@
     )(scal, q, *blocks)
 
 
+def pass_on_kernel(came, out):
+    out[...] = came[...]
+
+
+def pass_on(came):
+    return pl.pallas_call(
+        pass_on_kernel,
+        out_shape=jax.ShapeDtypeStruct(came.shape, came.dtype),
+        in_specs=[VMEM],
+        out_specs=VMEM,
+        compiler_params=pltpu.CompilerParams(vmem_limit_bytes=LIMIT),
+        cost_estimate=pl.CostEstimate(flops=STEER, bytes_accessed=0, transcendentals=0),
+    )(came)
+
+
 def merged(rows, messages):
     logs = [read_stats(m[rows : rows + 16, :]) for m in messages]
     top = functools.reduce(jnp.maximum, logs)
@@ -249,8 +265,8 @@
     x_own = swap(own, 4)
     pair = swap(own, 1)
     far_q, scal, *near_x = lax.optimization_barrier((far_q, scal, *near_x))
-    far_x = swap(far_q, 12)
-    x_own, far_x = lax.optimization_barrier((x_own, far_x))
+    far_x = pass_on(swap(far_q, 12))
+    x_own, far_q = lax.optimization_barrier((x_own, far_q))
     blocks = (own, pair, x_own, swap(x_own, 1))
 
     far_b = attend(scal, far_x, blocks)

time: 85.8 us -> 83.5 us (0.973)
  starting transfers between devices: 54.9 us -> 52.4 us
    ppermute x10, starting transfers between devices: 54.9 us -> 52.4 us  [swap(): return lax.ppermute(block, 'ctx', [(i, i ^ mask) for i in range(count)])]
  transfers between devices with their start and end apart: 10 -> 10, of which waited for: 5 -> 8; matrix products, arithmetic and copies ran while one was open for 0% -> 0% of each run, Pallas kernels for 15% -> 16%
where the time goes in v4:
time: 83.5 us; the launch traced here: 82.9 us
  starting transfers between devices  52.4 us (63%)
  Pallas kernels  20 us (24%)
  waiting for transfers between devices  10 us (12%)
    ppermute x10, starting transfers between devices, swap(): return lax.ppermute(block, 'ctx', [(i, i ^ mask) for i in range(count)])  52.4 us
    pallas_call x4, Pallas kernels, attend(): pl.pallas_call(attend_kernel, out_shape=jax.ShapeDtypeStruct(q.shape, jnp...  17.1 us
    ppermute x10, waiting for transfers between devices, swap(): return lax.ppermute(block, 'ctx', [(i, i ^ mask) for i in range(count)])  10 us
  transfers between devices with their start and end apart: 10, of which 8 were waited for; matrix products, arithmetic and copies ran while one was open for 0% of the time, Pallas kernels for 16%

profile of v4, /device:TPU:48, one launch (start us, length us, event | category | flops | bytes accessed | tf_op | source)
XLA Modules:
  0.0 82.9 jit_solution(3738100803670870257)
XLA Ops:
  0.0 0.0 copy-start.1
  0.0 0.0 copy-start
  0.0 0.0 copy-start.2
  0.0 1.3 %shard_map.75.s0 = bf16[2,2128,128]{2,1,0:T(8,128)(2,1)S(1)} custom-call(s32[2,32]{1,0:T(2,128)} %places.3, bf16[2,1024,128]{2,1,0:T(8,128)(2,1)} %k.1, bf16[2,1024,128]{2,1,0:T(8,128)(2,1)} %v.1, bf16[2,32,128]{2,1,0:T(8,128)(2,1)} %nk.1, bf16[2,32,128]{2,1,0:T(8,128)(2,1)} %nv.1), custom_call_target="tpu_custom_call" | custom-call | tf_op jit(solution)/shard_map/pallas_call | solution.py:110
  1.3 3.4 %collective-permute-start.5 = (bf16[2,2128,128]{2,1,0:T(8,128)(2,1)S(1)}, bf16[2,2128,128]{2,1,0:T(8,128)(2,1)S(1)}, u32[]{:S(2)}, u32[]{:S(2)}) collective-permute-start(bf16[2,2128,128]{2,1,0:T(8,128)(2,1)S(1)} %shard_map.75.s0), channel_id=1, source_target_pairs={{0,32},{8,40},{16,48},{24,56},{32,0},{40,8},{48,16},{56,24},{64,96... | collective-permute-start | bytes 3268616 | tf_op jit(solution)/shard_map/ppermute | solution.py:22
  4.7 0.0 copy-done.1
  4.7 0.0 copy-done
  4.8 14.8 %collective-permute-start = (bf16[2,272,128]{2,1,0:T(8,128)(2,1)S(1)}, bf16[2,272,128]{2,1,0:T(8,128)(2,1)S(1)}, u32[]{:S(2)}, u32[]{:S(2)}) collective-permute-start(bf16[2,272,128]{2,1,0:T(8,128)(2,1)S(1)} %shard_map.73.q), channel_id=1, source_target_pairs={{0,16},{8,24},{16,0},{24,8},{32,48},{40,56},{48,32},{56,40},{64,80... | collective-permute-start | bytes 417800 | tf_op jit(solution)/shard_map/ppermute | solution.py:22
  19.6 4.0 %collective-permute-start.2 = (bf16[272,128]{1,0:T(8,128)(2,1)S(1)}, bf16[272,128]{1,0:T(8,128)(2,1)S(1)}, u32[]{:S(2)}, u32[]{:S(2)}) collective-permute-start(bf16[272,128]{1,0:T(8,128)(2,1)S(1)} %get-tuple-element.31), channel_id=1, source_target_pairs={{0,96},{8,104},{16,112},{24,120},{32,64},{40,72},{48,80},{56,88},{... | collective-permute-start | bytes 208904 | tf_op jit(solution)/shard_map/ppermute | solution.py:22
  23.6 3.0 %collective-permute-start.1 = (bf16[272,128]{1,0:T(8,128)(2,1)S(1)}, bf16[272,128]{1,0:T(8,128)(2,1)S(1)}, u32[]{:S(2)}, u32[]{:S(2)}) collective-permute-start(bf16[272,128]{1,0:T(8,128)(2,1)S(1)} %get-tuple-element.32), channel_id=1, source_target_pairs={{0,96},{8,104},{16,112},{24,120},{32,64},{40,72},{48,80},{56,88},{... | collective-permute-start | bytes 208904 | tf_op jit(solution)/shard_map/ppermute | solution.py:22
  26.7 0.1 add_multiply_fusion
  26.8 0.0 copy-done.2
  26.8 0.1 pad_add_fusion.scal
  26.9 0.2 collective-permute-done.2
  27.0 4.0 %collective-permute-done.1 = bf16[272,128]{1,0:T(8,128)(2,1)S(1)} collective-permute-done((bf16[272,128]{1,0:T(8,128)(2,1)S(1)}, bf16[272,128]{1,0:T(8,128)(2,1)S(1)}, u32[]{:S(2)}, u32[]{:S(2)}) %collective-permute-start.1) | collective-permute-done | bytes 69664 | tf_op jit(solution)/shard_map/ppermute | solution.py:22
  31.1 1.0 %collective-permute-done.q = bf16[2,272,128]{2,1,0:T(8,128)(2,1)S(1)} collective-permute-done((bf16[2,272,128]{2,1,0:T(8,128)(2,1)S(1)}, bf16[2,272,128]{2,1,0:T(8,128)(2,1)S(1)}, u32[]{:S(2)}, u32[]{:S(2)}) %collective-permute-start) | collective-permute-done | bytes 139296 | tf_op jit(solution)/shard_map/ppermute | solution.py:22
  32.0 4.0 %collective-permute-start.3 = (bf16[2,272,128]{2,1,0:T(8,128)(2,1)S(1)}, bf16[2,272,128]{2,1,0:T(8,128)(2,1)S(1)}, u32[]{:S(2)}, u32[]{:S(2)}) collective-permute-start(bf16[2,272,128]{2,1,0:T(8,128)(2,1)S(1)} %collective-permute-done.q), channel_id=1, source_target_pairs={{0,96},{8,104},{16,112},{24,120},{32,64},{40,72},{48,80},{56,88},{... | collective-permute-start | bytes 417800 | tf_op jit(solution)/shard_map/ppermute | solution.py:22
  36.0 1.9 %collective-permute-start.4 = (bf16[2,2128,128]{2,1,0:T(8,128)(2,1)S(1)}, bf16[2,2128,128]{2,1,0:T(8,128)(2,1)S(1)}, u32[]{:S(2)}, u32[]{:S(2)}) collective-permute-start(bf16[2,2128,128]{2,1,0:T(8,128)(2,1)S(1)} %shard_map.75.s0), channel_id=1, source_target_pairs={{0,8},{8,0},{16,24},{24,16},{32,40},{40,32},{48,56},{56,48},{64,72... | collective-permute-start | bytes 3268616 | tf_op jit(solution)/shard_map/ppermute | solution.py:22
  37.9 0.0 collective-permute-done.5.s2
  38.0 2.4 %collective-permute-start.6 = (bf16[2,2128,128]{2,1,0:T(8,128)(2,1)S(1)}, bf16[2,2128,128]{2,1,0:T(8,128)(2,1)S(1)}, u32[]{:S(2)}, u32[]{:S(2)}) collective-permute-start(bf16[2,2128,128]{2,1,0:T(8,128)(2,1)S(1)} %collective-permute-done.5.s2), channel_id=1, source_target_pairs={{0,8},{8,0},{16,24},{24,16},{32,40},{40,32},{48,56},{56,48},{64,72... | collective-permute-start | bytes 3268616 | tf_op jit(solution)/shard_map/ppermute | solution.py:22
  40.4 0.0 collective-permute-done.3.came
  40.4 0.2 collective-permute-done.4.s1
  40.6 2.1 %collective-permute-done.6.s3 = bf16[2,2128,128]{2,1,0:T(8,128)(2,1)S(1)} collective-permute-done((bf16[2,2128,128]{2,1,0:T(8,128)(2,1)S(1)}, bf16[2,2128,128]{2,1,0:T(8,128)(2,1)S(1)}, u32[]{:S(2)}, u32[]{:S(2)}) %collective-permute-start.6) | collective-permute-done | bytes 1089568 | tf_op jit(solution)/shard_map/ppermute | solution.py:22
  42.7 4.2 %shard_map.76 = bf16[2,272,128]{2,1,0:T(8,128)(2,1)S(1)} custom-call(s32[6]{0:T(128)S(1)} %pad_add_fusion.scal, bf16[2,272,128]{2,1,0:T(8,128)(2,1)S(1)} %shard_map.74.q, bf16[2,2128,128]{2,1,0:T(8,128)(2,1)S(1)} %shard_map.75.s0, bf16[2,2128,128]{2,1,0:T(8,128)(2,1)S(1)} %collective-permute-done.4.s1, bf16[2,2128,128]{2,1,0:T(8,128)(2,1)S(1)} %collective-permute-done.5.s2, ...), custom_call_target="tpu_custom_call" | custom-call | flops 69632 | tf_op jit(solution)/shard_map/pallas_call | solution.py:178
  46.9 3.1 %collective-permute-start.7 = (bf16[2,272,128]{2,1,0:T(8,128)(2,1)S(1)}, bf16[2,272,128]{2,1,0:T(8,128)(2,1)S(1)}, u32[]{:S(2)}, u32[]{:S(2)}) collective-permute-start(bf16[2,272,128]{2,1,0:T(8,128)(2,1)S(1)} %shard_map.76), channel_id=1, source_target_pairs={{0,96},{8,104},{16,112},{24,120},{32,64},{40,72},{48,80},{56,88},{... | collective-permute-start | bytes 417800 | tf_op jit(solution)/shard_map/ppermute | solution.py:22
  49.9 4.3 %shard_map.77.own = bf16[2,272,128]{2,1,0:T(8,128)(2,1)S(1)} custom-call(s32[6]{0:T(128)S(1)} %pad_add_fusion.scal, bf16[2,272,128]{2,1,0:T(8,128)(2,1)S(1)} %collective-permute-done.q, bf16[2,2128,128]{2,1,0:T(8,128)(2,1)S(1)} %shard_map.75.s0, bf16[2,2128,128]{2,1,0:T(8,128)(2,1)S(1)} %collective-permute-done.4.s1, ...), custom_call_target="tpu_custom_call" | custom-call | flops 69632 | tf_op jit(solution)/shard_map/pallas_call | solution.py:178
  54.3 1.6 %collective-permute-done.7.came = bf16[2,272,128]{2,1,0:T(8,128)(2,1)S(1)} collective-permute-done((bf16[2,272,128]{2,1,0:T(8,128)(2,1)S(1)}, bf16[2,272,128]{2,1,0:T(8,128)(2,1)S(1)}, u32[]{:S(2)}, u32[]{:S(2)}) %collective-permute-start.7) | collective-permute-done | bytes 139296 | tf_op jit(solution)/shard_map/ppermute | solution.py:22
  55.9 0.5 shard_map.78
  56.4 12.2 %collective-permute-start.9 = (bf16[2,288,128]{2,1,0:T(8,128)(2,1)S(1)}, bf16[2,288,128]{2,1,0:T(8,128)(2,1)S(1)}, u32[]{:S(2)}, u32[]{:S(2)}) collective-permute-start(bf16[2,288,128]{2,1,0:T(8,128)(2,1)S(1)} %shard_map.78), channel_id=1, source_target_pairs={{0,16},{8,24},{16,0},{24,8},{32,48},{40,56},{48,32},{56,40},{64,80... | collective-permute-start | bytes 442376 | tf_op jit(solution)/shard_map/ppermute | solution.py:22
  68.6 4.4 %shard_map.79 = bf16[2,272,128]{2,1,0:T(8,128)(2,1)S(1)} custom-call(s32[6]{0:T(128)S(1)} %pad_add_fusion.scal, bf16[2,272,128]{2,1,0:T(8,128)(2,1)S(1)} %pad_maximum_fusion.q, bf16[2,2128,128]{2,1,0:T(8,128)(2,1)S(1)} %shard_map.75.s0, bf16[2,2128,128]{2,1,0:T(8,128)(2,1)S(1)} %collective-permute-done.4.s1, ...), custom_call_target="tpu_custom_call" | custom-call | flops 69632 | tf_op jit(solution)/shard_map/pallas_call | solution.py:178
  73.0 3.6 %collective-permute-start.8 = (bf16[2,272,128]{2,1,0:T(8,128)(2,1)S(1)}, bf16[2,272,128]{2,1,0:T(8,128)(2,1)S(1)}, u32[]{:S(2)}, u32[]{:S(2)}) collective-permute-start(bf16[2,272,128]{2,1,0:T(8,128)(2,1)S(1)} %shard_map.79), channel_id=1, source_target_pairs={{0,96},{8,104},{16,112},{24,120},{32,64},{40,72},{48,80},{56,88},{... | collective-permute-start | bytes 417800 | tf_op jit(solution)/shard_map/ppermute | solution.py:22
  76.6 4.1 %shard_map.80.one = bf16[2,272,128]{2,1,0:T(8,128)(2,1)S(1)} custom-call(s32[6]{0:T(128)S(1)} %pad_add_fusion.scal, bf16[2,272,128]{2,1,0:T(8,128)(2,1)S(1)} %shard_map.73.q, bf16[2,2128,128]{2,1,0:T(8,128)(2,1)S(1)} %shard_map.75.s0, bf16[2,2128,128]{2,1,0:T(8,128)(2,1)S(1)} %collective-permute-done.4.s1, ...), custom_call_target="tpu_custom_call" | custom-call | flops 69632 | tf_op jit(solution)/shard_map/pallas_call | solution.py:178
  80.8 0.4 collective-permute-done.8.two
  81.1 0.6 collective-permute-done.9.three
  81.7 1.2 %shard_map.81 = bf16[2,32,1024]{2,1,0:T(8,128)(2,1)} custom-call(bf16[2,272,128]{2,1,0:T(8,128)(2,1)S(1)} %shard_map.80.one, bf16[2,272,128]{2,1,0:T(8,128)(2,1)S(1)} %collective-permute-done.8.two, bf16[2,288,128]{2,1,0:T(8,128)(2,1)S(1)} %collective-permute-done.9.three), custom_call_target="tpu_custom_call" | custom-call | tf_op jit(solution)/shard_map/pallas_call | solution.py:245
  (4 shorter events, 0.1 us)
Async XLA Ops:
  0.0 4.7 %copy-start.1 = (s32[2,32]{1,0:T(2,128)S(1)}, s32[2,32]{1,0:T(2,128)}, u32[]{:S(2)}) copy-start(s32[2,32]{1,0:T(2,128)} %places.3) | copy-start | bytes 772
  0.0 4.7 %copy-start = (bf16[2,32,1024]{2,1,0:T(8,128)(2,1)S(1)}, bf16[2,32,1024]{2,1,0:T(8,128)(2,1)}, u32[]{:S(2)}) copy-start(bf16[2,32,1024]{2,1,0:T(8,128)(2,1)} %queries.1) | copy-start | bytes 393220
  0.0 26.8 %copy-start.2 = (s32[2]{0:T(128)S(1)}, s32[2]{0:T(128)}, u32[]{:S(2)}) copy-start(s32[2]{0:T(128)} %param.12) | copy-start | bytes 28
  1.3 36.6 %collective-permute-start.5 = (bf16[2,2128,128]{2,1,0:T(8,128)(2,1)S(1)}, bf16[2,2128,128]{2,1,0:T(8,128)(2,1)S(1)}, u32[]{:S(2)}, u32[]{:S(2)}) collective-permute-start(bf16[2,2128,128]{2,1,0:T(8,128)(2,1)S(1)} %shard_map.75.s0), channel_id=1, source_target_pairs={{0,32},{8,40},{16,48},{24,56},{32,0},{40,8},{48,16},{56,24},{64,96... | collective-permute-start | bytes 3268616 | tf_op jit(solution)/shard_map/ppermute | solution.py:22
  4.8 27.2 %collective-permute-start = (bf16[2,272,128]{2,1,0:T(8,128)(2,1)S(1)}, bf16[2,272,128]{2,1,0:T(8,128)(2,1)S(1)}, u32[]{:S(2)}, u32[]{:S(2)}) collective-permute-start(bf16[2,272,128]{2,1,0:T(8,128)(2,1)S(1)} %shard_map.73.q), channel_id=1, source_target_pairs={{0,16},{8,24},{16,0},{24,8},{32,48},{40,56},{48,32},{56,40},{64,80... | collective-permute-start | bytes 417800 | tf_op jit(solution)/shard_map/ppermute | solution.py:22
  19.6 7.4 %collective-permute-start.2 = (bf16[272,128]{1,0:T(8,128)(2,1)S(1)}, bf16[272,128]{1,0:T(8,128)(2,1)S(1)}, u32[]{:S(2)}, u32[]{:S(2)}) collective-permute-start(bf16[272,128]{1,0:T(8,128)(2,1)S(1)} %get-tuple-element.31), channel_id=1, source_target_pairs={{0,96},{8,104},{16,112},{24,120},{32,64},{40,72},{48,80},{56,88},{... | collective-permute-start | bytes 208904 | tf_op jit(solution)/shard_map/ppermute | solution.py:22
  23.6 7.4 %collective-permute-start.1 = (bf16[272,128]{1,0:T(8,128)(2,1)S(1)}, bf16[272,128]{1,0:T(8,128)(2,1)S(1)}, u32[]{:S(2)}, u32[]{:S(2)}) collective-permute-start(bf16[272,128]{1,0:T(8,128)(2,1)S(1)} %get-tuple-element.32), channel_id=1, source_target_pairs={{0,96},{8,104},{16,112},{24,120},{32,64},{40,72},{48,80},{56,88},{... | collective-permute-start | bytes 208904 | tf_op jit(solution)/shard_map/ppermute | solution.py:22
  32.0 8.4 %collective-permute-start.3 = (bf16[2,272,128]{2,1,0:T(8,128)(2,1)S(1)}, bf16[2,272,128]{2,1,0:T(8,128)(2,1)S(1)}, u32[]{:S(2)}, u32[]{:S(2)}) collective-permute-start(bf16[2,272,128]{2,1,0:T(8,128)(2,1)S(1)} %collective-permute-done.q), channel_id=1, source_target_pairs={{0,96},{8,104},{16,112},{24,120},{32,64},{40,72},{48,80},{56,88},{... | collective-permute-start | bytes 417800 | tf_op jit(solution)/shard_map/ppermute | solution.py:22
  36.0 4.6 %collective-permute-start.4 = (bf16[2,2128,128]{2,1,0:T(8,128)(2,1)S(1)}, bf16[2,2128,128]{2,1,0:T(8,128)(2,1)S(1)}, u32[]{:S(2)}, u32[]{:S(2)}) collective-permute-start(bf16[2,2128,128]{2,1,0:T(8,128)(2,1)S(1)} %shard_map.75.s0), channel_id=1, source_target_pairs={{0,8},{8,0},{16,24},{24,16},{32,40},{40,32},{48,56},{56,48},{64,72... | collective-permute-start | bytes 3268616 | tf_op jit(solution)/shard_map/ppermute | solution.py:22
  38.0 4.7 %collective-permute-start.6 = (bf16[2,2128,128]{2,1,0:T(8,128)(2,1)S(1)}, bf16[2,2128,128]{2,1,0:T(8,128)(2,1)S(1)}, u32[]{:S(2)}, u32[]{:S(2)}) collective-permute-start(bf16[2,2128,128]{2,1,0:T(8,128)(2,1)S(1)} %collective-permute-done.5.s2), channel_id=1, source_target_pairs={{0,8},{8,0},{16,24},{24,16},{32,40},{40,32},{48,56},{56,48},{64,72... | collective-permute-start | bytes 3268616 | tf_op jit(solution)/shard_map/ppermute | solution.py:22
  46.9 9.1 %collective-permute-start.7 = (bf16[2,272,128]{2,1,0:T(8,128)(2,1)S(1)}, bf16[2,272,128]{2,1,0:T(8,128)(2,1)S(1)}, u32[]{:S(2)}, u32[]{:S(2)}) collective-permute-start(bf16[2,272,128]{2,1,0:T(8,128)(2,1)S(1)} %shard_map.76), channel_id=1, source_target_pairs={{0,96},{8,104},{16,112},{24,120},{32,64},{40,72},{48,80},{56,88},{... | collective-permute-start | bytes 417800 | tf_op jit(solution)/shard_map/ppermute | solution.py:22
  56.4 25.3 %collective-permute-start.9 = (bf16[2,288,128]{2,1,0:T(8,128)(2,1)S(1)}, bf16[2,288,128]{2,1,0:T(8,128)(2,1)S(1)}, u32[]{:S(2)}, u32[]{:S(2)}) collective-permute-start(bf16[2,288,128]{2,1,0:T(8,128)(2,1)S(1)} %shard_map.78), channel_id=1, source_target_pairs={{0,16},{8,24},{16,0},{24,8},{32,48},{40,56},{48,32},{56,40},{64,80... | collective-permute-start | bytes 442376 | tf_op jit(solution)/shard_map/ppermute | solution.py:22
  73.0 8.2 %collective-permute-start.8 = (bf16[2,272,128]{2,1,0:T(8,128)(2,1)S(1)}, bf16[2,272,128]{2,1,0:T(8,128)(2,1)S(1)}, u32[]{:S(2)}, u32[]{:S(2)}) collective-permute-start(bf16[2,272,128]{2,1,0:T(8,128)(2,1)S(1)} %shard_map.79), channel_id=1, source_target_pairs={{0,96},{8,104},{16,112},{24,120},{32,64},{40,72},{48,80},{56,88},{... | collective-permute-start | bytes 417800 | tf_op jit(solution)/shard_map/ppermute | solution.py:22

commit v5 on v4

--- a/solution.py
+++ b/solution.py
@@ -144,7 +144,7 @@
         if state is not None:
             shift = jnp.maximum(shift, state[0])
         w = jnp.exp(got * SCALE - shift)
-        total = jnp.sum(w, axis=1, keepdims=True)
+        total = functools.reduce(jnp.add, [w[:, j : j + 128] for j in range(0, w.shape[1], 128)])
         if b < len(blocks):
             v = blocks[b][s, slots:nk, :]
         else:
@@ -166,6 +166,7 @@
                 ahead = score(*units[n + 1], masked)
             states[s] = weigh(s, b, got, states[s])
         for s, (shift, total, summed) in enumerate(states):
+            total = jnp.sum(total, axis=1, keepdims=True)
             out[s, 0:rows, :] = (summed / total).astype(jnp.bfloat16)
             out[s, rows:size, :] = stat_block(shift + jnp.log(total))
 
@@ -189,14 +190,14 @@
     out[...] = came[...]
 
 
-def pass_on(came):
+def pass_on(came, cost):
     return pl.pallas_call(
         pass_on_kernel,
         out_shape=jax.ShapeDtypeStruct(came.shape, came.dtype),
         in_specs=[VMEM],
         out_specs=VMEM,
         compiler_params=pltpu.CompilerParams(vmem_limit_bytes=LIMIT),
-        cost_estimate=pl.CostEstimate(flops=STEER, bytes_accessed=0, transcendentals=0),
+        cost_estimate=pl.CostEstimate(flops=cost, bytes_accessed=0, transcendentals=0),
     )(came)
 
 
@@ -216,14 +217,12 @@
         value, lse = merged(rows, [own[s], came[s]])
         out[s, 0:rows, :] = value.astype(jnp.bfloat16)
         out[s, rows:size, :] = stat_block(lse)
-        out[s, size:, :] = jnp.zeros((out.shape[1] - size, HEAD), jnp.bfloat16)
 
 
 def merge(own, came):
-    sessions, size, _ = own.shape
     return pl.pallas_call(
         merge_kernel,
-        out_shape=jax.ShapeDtypeStruct((sessions, size + 16, HEAD), jnp.bfloat16),
+        out_shape=jax.ShapeDtypeStruct(own.shape, jnp.bfloat16),
         in_specs=[VMEM, VMEM],
         out_specs=VMEM,
         compiler_params=pltpu.CompilerParams(vmem_limit_bytes=LIMIT),
@@ -265,7 +264,7 @@
     x_own = swap(own, 4)
     pair = swap(own, 1)
     far_q, scal, *near_x = lax.optimization_barrier((far_q, scal, *near_x))
-    far_x = pass_on(swap(far_q, 12))
+    far_x = pass_on(swap(far_q, 12), STEER)
     x_own, far_q = lax.optimization_barrier((x_own, far_q))
     blocks = (own, pair, x_own, swap(x_own, 1))
 
@@ -275,7 +274,7 @@
     far_a = attend(scal, far_q, blocks)
     far_came, far_a = lax.optimization_barrier((far_came, far_a))
     far = merge(far_a, far_came)
-    back = swap(far, 2)
+    back = pass_on(swap(far, 2), 10**9)
 
     far, near_q, *near_x = lax.optimization_barrier((far, near_q, *near_x))
     near_b = attend(scal, jnp.stack(near_x), blocks)

time: 83.5 us -> 83 us (level)
  waiting for transfers between devices: 10 us -> 8.5 us
  starting transfers between devices: 52.4 us -> 53.4 us
    ppermute x10, waiting for transfers between devices: 10 us -> 8.5 us  [swap(): return lax.ppermute(block, 'ctx', [(i, i ^ mask) for i in range(count)])]
    ppermute x10, starting transfers between devices: 52.4 us -> 53.4 us  [swap(): return lax.ppermute(block, 'ctx', [(i, i ^ mask) for i in range(count)])]
  transfers between devices with their start and end apart: 10 -> 10, of which waited for: 8 -> 6; matrix products, arithmetic and copies ran while one was open for 0% -> 0% of each run, Pallas kernels for 16% -> 16%
where the time goes in v5:
time: 83 us; the launch traced here: 82.6 us
  starting transfers between devices  53.4 us (64%)
  Pallas kernels  20.3 us (24%)
  waiting for transfers between devices  8.5 us (10%)
    ppermute x10, starting transfers between devices, swap(): return lax.ppermute(block, 'ctx', [(i, i ^ mask) for i in range(count)])  53.4 us
    pallas_call x4, Pallas kernels, attend(): pl.pallas_call(attend_kernel, out_shape=jax.ShapeDtypeStruct(q.shape, jnp...  17.3 us
    ppermute x10, waiting for transfers between devices, swap(): return lax.ppermute(block, 'ctx', [(i, i ^ mask) for i in range(count)])  8.5 us
  transfers between devices with their start and end apart: 10, of which 6 were waited for; matrix products, arithmetic and copies ran while one was open for 0% of the time, Pallas kernels for 16%

profile of v5, /device:TPU:48, one launch (start us, length us, event | category | flops | bytes accessed | tf_op | source)
XLA Modules:
  0.0 82.6 jit_solution(14012573984334047056)
XLA Ops:
  0.0 0.0 copy-start.1
  0.0 0.0 copy-start
  0.0 0.0 copy-start.2
  0.0 1.3 %shard_map.75.s0 = bf16[2,2128,128]{2,1,0:T(8,128)(2,1)S(1)} custom-call(s32[2,32]{1,0:T(2,128)} %places.3, bf16[2,1024,128]{2,1,0:T(8,128)(2,1)} %k.1, bf16[2,1024,128]{2,1,0:T(8,128)(2,1)} %v.1, bf16[2,32,128]{2,1,0:T(8,128)(2,1)} %nk.1, bf16[2,32,128]{2,1,0:T(8,128)(2,1)} %nv.1), custom_call_target="tpu_custom_call" | custom-call | tf_op jit(solution)/shard_map/pallas_call | solution.py:110
  1.3 3.4 %collective-permute-start.5 = (bf16[2,2128,128]{2,1,0:T(8,128)(2,1)S(1)}, bf16[2,2128,128]{2,1,0:T(8,128)(2,1)S(1)}, u32[]{:S(2)}, u32[]{:S(2)}) collective-permute-start(bf16[2,2128,128]{2,1,0:T(8,128)(2,1)S(1)} %shard_map.75.s0), channel_id=1, source_target_pairs={{0,32},{8,40},{16,48},{24,56},{32,0},{40,8},{48,16},{56,24},{64,96... | collective-permute-start | bytes 3268616 | tf_op jit(solution)/shard_map/ppermute | solution.py:22
  4.7 0.0 copy-done.1
  4.7 0.0 copy-done
  4.8 14.8 %collective-permute-start = (bf16[2,272,128]{2,1,0:T(8,128)(2,1)S(1)}, bf16[2,272,128]{2,1,0:T(8,128)(2,1)S(1)}, u32[]{:S(2)}, u32[]{:S(2)}) collective-permute-start(bf16[2,272,128]{2,1,0:T(8,128)(2,1)S(1)} %shard_map.73.q), channel_id=1, source_target_pairs={{0,16},{8,24},{16,0},{24,8},{32,48},{40,56},{48,32},{56,40},{64,80... | collective-permute-start | bytes 417800 | tf_op jit(solution)/shard_map/ppermute | solution.py:22
  19.6 4.0 %collective-permute-start.2 = (bf16[272,128]{1,0:T(8,128)(2,1)S(1)}, bf16[272,128]{1,0:T(8,128)(2,1)S(1)}, u32[]{:S(2)}, u32[]{:S(2)}) collective-permute-start(bf16[272,128]{1,0:T(8,128)(2,1)S(1)} %get-tuple-element.31), channel_id=1, source_target_pairs={{0,96},{8,104},{16,112},{24,120},{32,64},{40,72},{48,80},{56,88},{... | collective-permute-start | bytes 208904 | tf_op jit(solution)/shard_map/ppermute | solution.py:22
  23.6 3.0 %collective-permute-start.1 = (bf16[272,128]{1,0:T(8,128)(2,1)S(1)}, bf16[272,128]{1,0:T(8,128)(2,1)S(1)}, u32[]{:S(2)}, u32[]{:S(2)}) collective-permute-start(bf16[272,128]{1,0:T(8,128)(2,1)S(1)} %get-tuple-element.32), channel_id=1, source_target_pairs={{0,96},{8,104},{16,112},{24,120},{32,64},{40,72},{48,80},{56,88},{... | collective-permute-start | bytes 208904 | tf_op jit(solution)/shard_map/ppermute | solution.py:22
  26.7 0.1 add_multiply_fusion
  26.8 0.0 copy-done.2
  26.8 0.1 pad_add_fusion.scal
  26.9 0.2 collective-permute-done.2
  27.0 4.0 %collective-permute-done.1 = bf16[272,128]{1,0:T(8,128)(2,1)S(1)} collective-permute-done((bf16[272,128]{1,0:T(8,128)(2,1)S(1)}, bf16[272,128]{1,0:T(8,128)(2,1)S(1)}, u32[]{:S(2)}, u32[]{:S(2)}) %collective-permute-start.1) | collective-permute-done | bytes 69664 | tf_op jit(solution)/shard_map/ppermute | solution.py:22
  31.1 1.0 %collective-permute-done.q = bf16[2,272,128]{2,1,0:T(8,128)(2,1)S(1)} collective-permute-done((bf16[2,272,128]{2,1,0:T(8,128)(2,1)S(1)}, bf16[2,272,128]{2,1,0:T(8,128)(2,1)S(1)}, u32[]{:S(2)}, u32[]{:S(2)}) %collective-permute-start) | collective-permute-done | bytes 139296 | tf_op jit(solution)/shard_map/ppermute | solution.py:22
  32.0 4.0 %collective-permute-start.3 = (bf16[2,272,128]{2,1,0:T(8,128)(2,1)S(1)}, bf16[2,272,128]{2,1,0:T(8,128)(2,1)S(1)}, u32[]{:S(2)}, u32[]{:S(2)}) collective-permute-start(bf16[2,272,128]{2,1,0:T(8,128)(2,1)S(1)} %collective-permute-done.q), channel_id=1, source_target_pairs={{0,96},{8,104},{16,112},{24,120},{32,64},{40,72},{48,80},{56,88},{... | collective-permute-start | bytes 417800 | tf_op jit(solution)/shard_map/ppermute | solution.py:22
  36.0 1.9 %collective-permute-start.4 = (bf16[2,2128,128]{2,1,0:T(8,128)(2,1)S(1)}, bf16[2,2128,128]{2,1,0:T(8,128)(2,1)S(1)}, u32[]{:S(2)}, u32[]{:S(2)}) collective-permute-start(bf16[2,2128,128]{2,1,0:T(8,128)(2,1)S(1)} %shard_map.75.s0), channel_id=1, source_target_pairs={{0,8},{8,0},{16,24},{24,16},{32,40},{40,32},{48,56},{56,48},{64,72... | collective-permute-start | bytes 3268616 | tf_op jit(solution)/shard_map/ppermute | solution.py:22
  37.9 0.0 collective-permute-done.5.s2
  38.0 2.4 %collective-permute-start.6 = (bf16[2,2128,128]{2,1,0:T(8,128)(2,1)S(1)}, bf16[2,2128,128]{2,1,0:T(8,128)(2,1)S(1)}, u32[]{:S(2)}, u32[]{:S(2)}) collective-permute-start(bf16[2,2128,128]{2,1,0:T(8,128)(2,1)S(1)} %collective-permute-done.5.s2), channel_id=1, source_target_pairs={{0,8},{8,0},{16,24},{24,16},{32,40},{40,32},{48,56},{56,48},{64,72... | collective-permute-start | bytes 3268616 | tf_op jit(solution)/shard_map/ppermute | solution.py:22
  40.4 0.0 collective-permute-done.3.came
  40.4 0.2 collective-permute-done.4.s1
  40.6 2.1 %collective-permute-done.6.s3 = bf16[2,2128,128]{2,1,0:T(8,128)(2,1)S(1)} collective-permute-done((bf16[2,2128,128]{2,1,0:T(8,128)(2,1)S(1)}, bf16[2,2128,128]{2,1,0:T(8,128)(2,1)S(1)}, u32[]{:S(2)}, u32[]{:S(2)}) %collective-permute-start.6) | collective-permute-done | bytes 1089568 | tf_op jit(solution)/shard_map/ppermute | solution.py:22
  42.7 4.2 %shard_map.76 = bf16[2,272,128]{2,1,0:T(8,128)(2,1)S(1)} custom-call(s32[6]{0:T(128)S(1)} %pad_add_fusion.scal, bf16[2,272,128]{2,1,0:T(8,128)(2,1)S(1)} %shard_map.74.q, bf16[2,2128,128]{2,1,0:T(8,128)(2,1)S(1)} %shard_map.75.s0, bf16[2,2128,128]{2,1,0:T(8,128)(2,1)S(1)} %collective-permute-done.4.s1, bf16[2,2128,128]{2,1,0:T(8,128)(2,1)S(1)} %collective-permute-done.5.s2, ...), custom_call_target="tpu_custom_call" | custom-call | flops 69632 | tf_op jit(solution)/shard_map/pallas_call | solution.py:179
  46.9 3.6 %collective-permute-start.7 = (bf16[2,272,128]{2,1,0:T(8,128)(2,1)S(1)}, bf16[2,272,128]{2,1,0:T(8,128)(2,1)S(1)}, u32[]{:S(2)}, u32[]{:S(2)}) collective-permute-start(bf16[2,272,128]{2,1,0:T(8,128)(2,1)S(1)} %shard_map.76), channel_id=1, source_target_pairs={{0,96},{8,104},{16,112},{24,120},{32,64},{40,72},{48,80},{56,88},{... | collective-permute-start | bytes 417800 | tf_op jit(solution)/shard_map/ppermute | solution.py:22
  50.5 4.4 %shard_map.77.own = bf16[2,272,128]{2,1,0:T(8,128)(2,1)S(1)} custom-call(s32[6]{0:T(128)S(1)} %pad_add_fusion.scal, bf16[2,272,128]{2,1,0:T(8,128)(2,1)S(1)} %collective-permute-done.q, bf16[2,2128,128]{2,1,0:T(8,128)(2,1)S(1)} %shard_map.75.s0, bf16[2,2128,128]{2,1,0:T(8,128)(2,1)S(1)} %collective-permute-done.4.s1, ...), custom_call_target="tpu_custom_call" | custom-call | flops 69632 | tf_op jit(solution)/shard_map/pallas_call | solution.py:179
  54.9 1.1 %collective-permute-done.7.came = bf16[2,272,128]{2,1,0:T(8,128)(2,1)S(1)} collective-permute-done((bf16[2,272,128]{2,1,0:T(8,128)(2,1)S(1)}, bf16[2,272,128]{2,1,0:T(8,128)(2,1)S(1)}, u32[]{:S(2)}, u32[]{:S(2)}) %collective-permute-start.7) | collective-permute-done | bytes 139296 | tf_op jit(solution)/shard_map/ppermute | solution.py:22
  56.0 0.5 shard_map.78
  56.5 12.2 %collective-permute-start.9 = (bf16[2,272,128]{2,1,0:T(8,128)(2,1)S(1)}, bf16[2,272,128]{2,1,0:T(8,128)(2,1)S(1)}, u32[]{:S(2)}, u32[]{:S(2)}) collective-permute-start(bf16[2,272,128]{2,1,0:T(8,128)(2,1)S(1)} %shard_map.78), channel_id=1, source_target_pairs={{0,16},{8,24},{16,0},{24,8},{32,48},{40,56},{48,32},{56,40},{64,80... | collective-permute-start | bytes 417800 | tf_op jit(solution)/shard_map/ppermute | solution.py:22
  68.6 4.5 %shard_map.79 = bf16[2,272,128]{2,1,0:T(8,128)(2,1)S(1)} custom-call(s32[6]{0:T(128)S(1)} %pad_add_fusion.scal, bf16[2,272,128]{2,1,0:T(8,128)(2,1)S(1)} %pad_maximum_fusion.q, bf16[2,2128,128]{2,1,0:T(8,128)(2,1)S(1)} %shard_map.75.s0, bf16[2,2128,128]{2,1,0:T(8,128)(2,1)S(1)} %collective-permute-done.4.s1, ...), custom_call_target="tpu_custom_call" | custom-call | flops 69632 | tf_op jit(solution)/shard_map/pallas_call | solution.py:179
  73.1 4.1 %collective-permute-start.8 = (bf16[2,272,128]{2,1,0:T(8,128)(2,1)S(1)}, bf16[2,272,128]{2,1,0:T(8,128)(2,1)S(1)}, u32[]{:S(2)}, u32[]{:S(2)}) collective-permute-start(bf16[2,272,128]{2,1,0:T(8,128)(2,1)S(1)} %shard_map.79), channel_id=1, source_target_pairs={{0,96},{8,104},{16,112},{24,120},{32,64},{40,72},{48,80},{56,88},{... | collective-permute-start | bytes 417800 | tf_op jit(solution)/shard_map/ppermute | solution.py:22
  77.2 4.2 %shard_map.80.one = bf16[2,272,128]{2,1,0:T(8,128)(2,1)S(1)} custom-call(s32[6]{0:T(128)S(1)} %pad_add_fusion.scal, bf16[2,272,128]{2,1,0:T(8,128)(2,1)S(1)} %shard_map.73.q, bf16[2,2128,128]{2,1,0:T(8,128)(2,1)S(1)} %shard_map.75.s0, bf16[2,2128,128]{2,1,0:T(8,128)(2,1)S(1)} %collective-permute-done.4.s1, ...), custom_call_target="tpu_custom_call" | custom-call | flops 69632 | tf_op jit(solution)/shard_map/pallas_call | solution.py:179
  81.4 0.0 collective-permute-done.9.came
  81.4 0.0 collective-permute-done.8.two
  81.4 1.2 %shard_map.82 = bf16[2,32,1024]{2,1,0:T(8,128)(2,1)} custom-call(bf16[2,272,128]{2,1,0:T(8,128)(2,1)S(1)} %shard_map.80.one, bf16[2,272,128]{2,1,0:T(8,128)(2,1)S(1)} %collective-permute-done.8.two, bf16[2,272,128]{2,1,0:T(8,128)(2,1)S(1)} %shard_map.81.three), custom_call_target="tpu_custom_call" | custom-call | tf_op jit(solution)/shard_map/pallas_call | solution.py:244
  (5 shorter events, 0.1 us)
Async XLA Ops:
  0.0 4.7 %copy-start.1 = (s32[2,32]{1,0:T(2,128)S(1)}, s32[2,32]{1,0:T(2,128)}, u32[]{:S(2)}) copy-start(s32[2,32]{1,0:T(2,128)} %places.3) | copy-start | bytes 772
  0.0 4.7 %copy-start = (bf16[2,32,1024]{2,1,0:T(8,128)(2,1)S(1)}, bf16[2,32,1024]{2,1,0:T(8,128)(2,1)}, u32[]{:S(2)}) copy-start(bf16[2,32,1024]{2,1,0:T(8,128)(2,1)} %queries.1) | copy-start | bytes 393220
  0.0 26.8 %copy-start.2 = (s32[2]{0:T(128)S(1)}, s32[2]{0:T(128)}, u32[]{:S(2)}) copy-start(s32[2]{0:T(128)} %param.12) | copy-start | bytes 28
  1.3 36.6 %collective-permute-start.5 = (bf16[2,2128,128]{2,1,0:T(8,128)(2,1)S(1)}, bf16[2,2128,128]{2,1,0:T(8,128)(2,1)S(1)}, u32[]{:S(2)}, u32[]{:S(2)}) collective-permute-start(bf16[2,2128,128]{2,1,0:T(8,128)(2,1)S(1)} %shard_map.75.s0), channel_id=1, source_target_pairs={{0,32},{8,40},{16,48},{24,56},{32,0},{40,8},{48,16},{56,24},{64,96... | collective-permute-start | bytes 3268616 | tf_op jit(solution)/shard_map/ppermute | solution.py:22
  4.8 27.2 %collective-permute-start = (bf16[2,272,128]{2,1,0:T(8,128)(2,1)S(1)}, bf16[2,272,128]{2,1,0:T(8,128)(2,1)S(1)}, u32[]{:S(2)}, u32[]{:S(2)}) collective-permute-start(bf16[2,272,128]{2,1,0:T(8,128)(2,1)S(1)} %shard_map.73.q), channel_id=1, source_target_pairs={{0,16},{8,24},{16,0},{24,8},{32,48},{40,56},{48,32},{56,40},{64,80... | collective-permute-start | bytes 417800 | tf_op jit(solution)/shard_map/ppermute | solution.py:22
  19.6 7.4 %collective-permute-start.2 = (bf16[272,128]{1,0:T(8,128)(2,1)S(1)}, bf16[272,128]{1,0:T(8,128)(2,1)S(1)}, u32[]{:S(2)}, u32[]{:S(2)}) collective-permute-start(bf16[272,128]{1,0:T(8,128)(2,1)S(1)} %get-tuple-element.31), channel_id=1, source_target_pairs={{0,96},{8,104},{16,112},{24,120},{32,64},{40,72},{48,80},{56,88},{... | collective-permute-start | bytes 208904 | tf_op jit(solution)/shard_map/ppermute | solution.py:22
  23.6 7.4 %collective-permute-start.1 = (bf16[272,128]{1,0:T(8,128)(2,1)S(1)}, bf16[272,128]{1,0:T(8,128)(2,1)S(1)}, u32[]{:S(2)}, u32[]{:S(2)}) collective-permute-start(bf16[272,128]{1,0:T(8,128)(2,1)S(1)} %get-tuple-element.32), channel_id=1, source_target_pairs={{0,96},{8,104},{16,112},{24,120},{32,64},{40,72},{48,80},{56,88},{... | collective-permute-start | bytes 208904 | tf_op jit(solution)/shard_map/ppermute | solution.py:22
  32.0 8.4 %collective-permute-start.3 = (bf16[2,272,128]{2,1,0:T(8,128)(2,1)S(1)}, bf16[2,272,128]{2,1,0:T(8,128)(2,1)S(1)}, u32[]{:S(2)}, u32[]{:S(2)}) collective-permute-start(bf16[2,272,128]{2,1,0:T(8,128)(2,1)S(1)} %collective-permute-done.q), channel_id=1, source_target_pairs={{0,96},{8,104},{16,112},{24,120},{32,64},{40,72},{48,80},{56,88},{... | collective-permute-start | bytes 417800 | tf_op jit(solution)/shard_map/ppermute | solution.py:22
  36.0 4.6 %collective-permute-start.4 = (bf16[2,2128,128]{2,1,0:T(8,128)(2,1)S(1)}, bf16[2,2128,128]{2,1,0:T(8,128)(2,1)S(1)}, u32[]{:S(2)}, u32[]{:S(2)}) collective-permute-start(bf16[2,2128,128]{2,1,0:T(8,128)(2,1)S(1)} %shard_map.75.s0), channel_id=1, source_target_pairs={{0,8},{8,0},{16,24},{24,16},{32,40},{40,32},{48,56},{56,48},{64,72... | collective-permute-start | bytes 3268616 | tf_op jit(solution)/shard_map/ppermute | solution.py:22
  38.0 4.7 %collective-permute-start.6 = (bf16[2,2128,128]{2,1,0:T(8,128)(2,1)S(1)}, bf16[2,2128,128]{2,1,0:T(8,128)(2,1)S(1)}, u32[]{:S(2)}, u32[]{:S(2)}) collective-permute-start(bf16[2,2128,128]{2,1,0:T(8,128)(2,1)S(1)} %collective-permute-done.5.s2), channel_id=1, source_target_pairs={{0,8},{8,0},{16,24},{24,16},{32,40},{40,32},{48,56},{56,48},{64,72... | collective-permute-start | bytes 3268616 | tf_op jit(solution)/shard_map/ppermute | solution.py:22
  46.9 9.1 %collective-permute-start.7 = (bf16[2,272,128]{2,1,0:T(8,128)(2,1)S(1)}, bf16[2,272,128]{2,1,0:T(8,128)(2,1)S(1)}, u32[]{:S(2)}, u32[]{:S(2)}) collective-permute-start(bf16[2,272,128]{2,1,0:T(8,128)(2,1)S(1)} %shard_map.76), channel_id=1, source_target_pairs={{0,96},{8,104},{16,112},{24,120},{32,64},{40,72},{48,80},{56,88},{... | collective-permute-start | bytes 417800 | tf_op jit(solution)/shard_map/ppermute | solution.py:22
  56.5 24.9 %collective-permute-start.9 = (bf16[2,272,128]{2,1,0:T(8,128)(2,1)S(1)}, bf16[2,272,128]{2,1,0:T(8,128)(2,1)S(1)}, u32[]{:S(2)}, u32[]{:S(2)}) collective-permute-start(bf16[2,272,128]{2,1,0:T(8,128)(2,1)S(1)} %shard_map.78), channel_id=1, source_target_pairs={{0,16},{8,24},{16,0},{24,8},{32,48},{40,56},{48,32},{56,40},{64,80... | collective-permute-start | bytes 417800 | tf_op jit(solution)/shard_map/ppermute | solution.py:22
  73.1 8.3 %collective-permute-start.8 = (bf16[2,272,128]{2,1,0:T(8,128)(2,1)S(1)}, bf16[2,272,128]{2,1,0:T(8,128)(2,1)S(1)}, u32[]{:S(2)}, u32[]{:S(2)}) collective-permute-start(bf16[2,272,128]{2,1,0:T(8,128)(2,1)S(1)} %shard_map.79), channel_id=1, source_target_pairs={{0,96},{8,104},{16,112},{24,120},{32,64},{40,72},{48,80},{56,88},{... | collective-permute-start | bytes 417800 | tf_op jit(solution)/shard_map/ppermute | solution.py:22

commit v6 on v5

--- a/solution.py
+++ b/solution.py
@@ -159,11 +159,11 @@
     def body(masked):
         units = [(s, b) for b in (len(blocks), *range(len(blocks))) for s in range(sessions)]
         states = [None] * sessions
-        ahead = score(*units[0], masked)
+        ahead = [score(*u, masked) for u in units[:2]]
         for n, (s, b) in enumerate(units):
-            got = ahead
-            if n + 1 < len(units):
-                ahead = score(*units[n + 1], masked)
+            got = ahead.pop(0)
+            if n + 2 < len(units):
+                ahead.append(score(*units[n + 2], masked))
             states[s] = weigh(s, b, got, states[s])
         for s, (shift, total, summed) in enumerate(states):
             total = jnp.sum(total, axis=1, keepdims=True)

time: 83 us -> 82.8 us (level)
  transfers between devices with their start and end apart: 10 -> 10, of which waited for: 6 -> 6; matrix products, arithmetic and copies ran while one was open for 0% -> 0% of each run, Pallas kernels for 16% -> 15%
where the time goes in v6:
time: 82.8 us; the launch traced here: 82.3 us
  starting transfers between devices  53.6 us (65%)
  Pallas kernels  19.8 us (24%)
  waiting for transfers between devices  8.58 us (10%)
    ppermute x10, starting transfers between devices, swap(): return lax.ppermute(block, 'ctx', [(i, i ^ mask) for i in range(count)])  53.6 us
    pallas_call x4, Pallas kernels, attend(): pl.pallas_call(attend_kernel, out_shape=jax.ShapeDtypeStruct(q.shape, jnp...  16.8 us
    ppermute x10, waiting for transfers between devices, swap(): return lax.ppermute(block, 'ctx', [(i, i ^ mask) for i in range(count)])  8.58 us
  transfers between devices with their start and end apart: 10, of which 6 were waited for; matrix products, arithmetic and copies ran while one was open for 0% of the time, Pallas kernels for 15%

profile of v6, /device:TPU:48, one launch (start us, length us, event | category | flops | bytes accessed | tf_op | source)
XLA Modules:
  0.0 82.3 jit_solution(16132155656107362186)
XLA Ops:
  0.0 0.0 copy-start.1
  0.0 0.0 copy-start
  0.0 0.0 copy-start.2
  0.0 1.3 %shard_map.75.s0 = bf16[2,2128,128]{2,1,0:T(8,128)(2,1)S(1)} custom-call(s32[2,32]{1,0:T(2,128)} %places.3, bf16[2,1024,128]{2,1,0:T(8,128)(2,1)} %k.1, bf16[2,1024,128]{2,1,0:T(8,128)(2,1)} %v.1, bf16[2,32,128]{2,1,0:T(8,128)(2,1)} %nk.1, bf16[2,32,128]{2,1,0:T(8,128)(2,1)} %nv.1), custom_call_target="tpu_custom_call" | custom-call | tf_op jit(solution)/shard_map/pallas_call | solution.py:110
  1.3 3.4 %collective-permute-start.5 = (bf16[2,2128,128]{2,1,0:T(8,128)(2,1)S(1)}, bf16[2,2128,128]{2,1,0:T(8,128)(2,1)S(1)}, u32[]{:S(2)}, u32[]{:S(2)}) collective-permute-start(bf16[2,2128,128]{2,1,0:T(8,128)(2,1)S(1)} %shard_map.75.s0), channel_id=1, source_target_pairs={{0,32},{8,40},{16,48},{24,56},{32,0},{40,8},{48,16},{56,24},{64,96... | collective-permute-start | bytes 3268616 | tf_op jit(solution)/shard_map/ppermute | solution.py:22
  4.7 0.0 copy-done.1
  4.7 0.0 copy-done
  4.8 14.8 %collective-permute-start = (bf16[2,272,128]{2,1,0:T(8,128)(2,1)S(1)}, bf16[2,272,128]{2,1,0:T(8,128)(2,1)S(1)}, u32[]{:S(2)}, u32[]{:S(2)}) collective-permute-start(bf16[2,272,128]{2,1,0:T(8,128)(2,1)S(1)} %shard_map.73.q), channel_id=1, source_target_pairs={{0,16},{8,24},{16,0},{24,8},{32,48},{40,56},{48,32},{56,40},{64,80... | collective-permute-start | bytes 417800 | tf_op jit(solution)/shard_map/ppermute | solution.py:22
  19.6 4.0 %collective-permute-start.2 = (bf16[272,128]{1,0:T(8,128)(2,1)S(1)}, bf16[272,128]{1,0:T(8,128)(2,1)S(1)}, u32[]{:S(2)}, u32[]{:S(2)}) collective-permute-start(bf16[272,128]{1,0:T(8,128)(2,1)S(1)} %get-tuple-element.31), channel_id=1, source_target_pairs={{0,96},{8,104},{16,112},{24,120},{32,64},{40,72},{48,80},{56,88},{... | collective-permute-start | bytes 208904 | tf_op jit(solution)/shard_map/ppermute | solution.py:22
  23.6 3.0 %collective-permute-start.1 = (bf16[272,128]{1,0:T(8,128)(2,1)S(1)}, bf16[272,128]{1,0:T(8,128)(2,1)S(1)}, u32[]{:S(2)}, u32[]{:S(2)}) collective-permute-start(bf16[272,128]{1,0:T(8,128)(2,1)S(1)} %get-tuple-element.32), channel_id=1, source_target_pairs={{0,96},{8,104},{16,112},{24,120},{32,64},{40,72},{48,80},{56,88},{... | collective-permute-start | bytes 208904 | tf_op jit(solution)/shard_map/ppermute | solution.py:22
  26.7 0.1 add_multiply_fusion
  26.8 0.0 copy-done.2
  26.8 0.1 pad_add_fusion.scal
  26.9 0.2 collective-permute-done.2
  27.0 4.0 %collective-permute-done.1 = bf16[272,128]{1,0:T(8,128)(2,1)S(1)} collective-permute-done((bf16[272,128]{1,0:T(8,128)(2,1)S(1)}, bf16[272,128]{1,0:T(8,128)(2,1)S(1)}, u32[]{:S(2)}, u32[]{:S(2)}) %collective-permute-start.1) | collective-permute-done | bytes 69664 | tf_op jit(solution)/shard_map/ppermute | solution.py:22
  31.1 1.0 %collective-permute-done.q = bf16[2,272,128]{2,1,0:T(8,128)(2,1)S(1)} collective-permute-done((bf16[2,272,128]{2,1,0:T(8,128)(2,1)S(1)}, bf16[2,272,128]{2,1,0:T(8,128)(2,1)S(1)}, u32[]{:S(2)}, u32[]{:S(2)}) %collective-permute-start) | collective-permute-done | bytes 139296 | tf_op jit(solution)/shard_map/ppermute | solution.py:22
  32.0 4.0 %collective-permute-start.3 = (bf16[2,272,128]{2,1,0:T(8,128)(2,1)S(1)}, bf16[2,272,128]{2,1,0:T(8,128)(2,1)S(1)}, u32[]{:S(2)}, u32[]{:S(2)}) collective-permute-start(bf16[2,272,128]{2,1,0:T(8,128)(2,1)S(1)} %collective-permute-done.q), channel_id=1, source_target_pairs={{0,96},{8,104},{16,112},{24,120},{32,64},{40,72},{48,80},{56,88},{... | collective-permute-start | bytes 417800 | tf_op jit(solution)/shard_map/ppermute | solution.py:22
  36.0 1.9 %collective-permute-start.4 = (bf16[2,2128,128]{2,1,0:T(8,128)(2,1)S(1)}, bf16[2,2128,128]{2,1,0:T(8,128)(2,1)S(1)}, u32[]{:S(2)}, u32[]{:S(2)}) collective-permute-start(bf16[2,2128,128]{2,1,0:T(8,128)(2,1)S(1)} %shard_map.75.s0), channel_id=1, source_target_pairs={{0,8},{8,0},{16,24},{24,16},{32,40},{40,32},{48,56},{56,48},{64,72... | collective-permute-start | bytes 3268616 | tf_op jit(solution)/shard_map/ppermute | solution.py:22
  37.9 0.0 collective-permute-done.5.s2
  38.0 2.4 %collective-permute-start.6 = (bf16[2,2128,128]{2,1,0:T(8,128)(2,1)S(1)}, bf16[2,2128,128]{2,1,0:T(8,128)(2,1)S(1)}, u32[]{:S(2)}, u32[]{:S(2)}) collective-permute-start(bf16[2,2128,128]{2,1,0:T(8,128)(2,1)S(1)} %collective-permute-done.5.s2), channel_id=1, source_target_pairs={{0,8},{8,0},{16,24},{24,16},{32,40},{40,32},{48,56},{56,48},{64,72... | collective-permute-start | bytes 3268616 | tf_op jit(solution)/shard_map/ppermute | solution.py:22
  40.4 0.0 collective-permute-done.3.came
  40.4 0.2 collective-permute-done.4.s1
  40.6 2.1 %collective-permute-done.6.s3 = bf16[2,2128,128]{2,1,0:T(8,128)(2,1)S(1)} collective-permute-done((bf16[2,2128,128]{2,1,0:T(8,128)(2,1)S(1)}, bf16[2,2128,128]{2,1,0:T(8,128)(2,1)S(1)}, u32[]{:S(2)}, u32[]{:S(2)}) %collective-permute-start.6) | collective-permute-done | bytes 1089568 | tf_op jit(solution)/shard_map/ppermute | solution.py:22
  42.7 4.1 %shard_map.76 = bf16[2,272,128]{2,1,0:T(8,128)(2,1)S(1)} custom-call(s32[6]{0:T(128)S(1)} %pad_add_fusion.scal, bf16[2,272,128]{2,1,0:T(8,128)(2,1)S(1)} %shard_map.74.q, bf16[2,2128,128]{2,1,0:T(8,128)(2,1)S(1)} %shard_map.75.s0, bf16[2,2128,128]{2,1,0:T(8,128)(2,1)S(1)} %collective-permute-done.4.s1, bf16[2,2128,128]{2,1,0:T(8,128)(2,1)S(1)} %collective-permute-done.5.s2, ...), custom_call_target="tpu_custom_call" | custom-call | flops 69632 | tf_op jit(solution)/shard_map/pallas_call | solution.py:179
  46.8 3.6 %collective-permute-start.7 = (bf16[2,272,128]{2,1,0:T(8,128)(2,1)S(1)}, bf16[2,272,128]{2,1,0:T(8,128)(2,1)S(1)}, u32[]{:S(2)}, u32[]{:S(2)}) collective-permute-start(bf16[2,272,128]{2,1,0:T(8,128)(2,1)S(1)} %shard_map.76), channel_id=1, source_target_pairs={{0,96},{8,104},{16,112},{24,120},{32,64},{40,72},{48,80},{56,88},{... | collective-permute-start | bytes 417800 | tf_op jit(solution)/shard_map/ppermute | solution.py:22
  50.4 4.3 %shard_map.77.own = bf16[2,272,128]{2,1,0:T(8,128)(2,1)S(1)} custom-call(s32[6]{0:T(128)S(1)} %pad_add_fusion.scal, bf16[2,272,128]{2,1,0:T(8,128)(2,1)S(1)} %collective-permute-done.q, bf16[2,2128,128]{2,1,0:T(8,128)(2,1)S(1)} %shard_map.75.s0, bf16[2,2128,128]{2,1,0:T(8,128)(2,1)S(1)} %collective-permute-done.4.s1, ...), custom_call_target="tpu_custom_call" | custom-call | flops 69632 | tf_op jit(solution)/shard_map/pallas_call | solution.py:179
  54.7 1.1 %collective-permute-done.7.came = bf16[2,272,128]{2,1,0:T(8,128)(2,1)S(1)} collective-permute-done((bf16[2,272,128]{2,1,0:T(8,128)(2,1)S(1)}, bf16[2,272,128]{2,1,0:T(8,128)(2,1)S(1)}, u32[]{:S(2)}, u32[]{:S(2)}) %collective-permute-start.7) | collective-permute-done | bytes 139296 | tf_op jit(solution)/shard_map/ppermute | solution.py:22
  55.8 0.5 shard_map.78
  56.3 12.1 %collective-permute-start.9 = (bf16[2,272,128]{2,1,0:T(8,128)(2,1)S(1)}, bf16[2,272,128]{2,1,0:T(8,128)(2,1)S(1)}, u32[]{:S(2)}, u32[]{:S(2)}) collective-permute-start(bf16[2,272,128]{2,1,0:T(8,128)(2,1)S(1)} %shard_map.78), channel_id=1, source_target_pairs={{0,16},{8,24},{16,0},{24,8},{32,48},{40,56},{48,32},{56,40},{64,80... | collective-permute-start | bytes 417800 | tf_op jit(solution)/shard_map/ppermute | solution.py:22
  68.5 4.3 %shard_map.79 = bf16[2,272,128]{2,1,0:T(8,128)(2,1)S(1)} custom-call(s32[6]{0:T(128)S(1)} %pad_add_fusion.scal, bf16[2,272,128]{2,1,0:T(8,128)(2,1)S(1)} %pad_maximum_fusion.q, bf16[2,2128,128]{2,1,0:T(8,128)(2,1)S(1)} %shard_map.75.s0, bf16[2,2128,128]{2,1,0:T(8,128)(2,1)S(1)} %collective-permute-done.4.s1, ...), custom_call_target="tpu_custom_call" | custom-call | flops 69632 | tf_op jit(solution)/shard_map/pallas_call | solution.py:179
  72.8 4.2 %collective-permute-start.8 = (bf16[2,272,128]{2,1,0:T(8,128)(2,1)S(1)}, bf16[2,272,128]{2,1,0:T(8,128)(2,1)S(1)}, u32[]{:S(2)}, u32[]{:S(2)}) collective-permute-start(bf16[2,272,128]{2,1,0:T(8,128)(2,1)S(1)} %shard_map.79), channel_id=1, source_target_pairs={{0,96},{8,104},{16,112},{24,120},{32,64},{40,72},{48,80},{56,88},{... | collective-permute-start | bytes 417800 | tf_op jit(solution)/shard_map/ppermute | solution.py:22
  77.0 4.1 %shard_map.80.one = bf16[2,272,128]{2,1,0:T(8,128)(2,1)S(1)} custom-call(s32[6]{0:T(128)S(1)} %pad_add_fusion.scal, bf16[2,272,128]{2,1,0:T(8,128)(2,1)S(1)} %shard_map.73.q, bf16[2,2128,128]{2,1,0:T(8,128)(2,1)S(1)} %shard_map.75.s0, bf16[2,2128,128]{2,1,0:T(8,128)(2,1)S(1)} %collective-permute-done.4.s1, ...), custom_call_target="tpu_custom_call" | custom-call | flops 69632 | tf_op jit(solution)/shard_map/pallas_call | solution.py:179
  81.1 0.0 collective-permute-done.9.came
  81.1 0.0 collective-permute-done.8.two
  81.1 1.2 %shard_map.82 = bf16[2,32,1024]{2,1,0:T(8,128)(2,1)} custom-call(bf16[2,272,128]{2,1,0:T(8,128)(2,1)S(1)} %shard_map.80.one, bf16[2,272,128]{2,1,0:T(8,128)(2,1)S(1)} %collective-permute-done.8.two, bf16[2,272,128]{2,1,0:T(8,128)(2,1)S(1)} %shard_map.81.three), custom_call_target="tpu_custom_call" | custom-call | tf_op jit(solution)/shard_map/pallas_call | solution.py:244
  (5 shorter events, 0.1 us)
Async XLA Ops:
  0.0 4.7 %copy-start.1 = (s32[2,32]{1,0:T(2,128)S(1)}, s32[2,32]{1,0:T(2,128)}, u32[]{:S(2)}) copy-start(s32[2,32]{1,0:T(2,128)} %places.3) | copy-start | bytes 772
  0.0 4.7 %copy-start = (bf16[2,32,1024]{2,1,0:T(8,128)(2,1)S(1)}, bf16[2,32,1024]{2,1,0:T(8,128)(2,1)}, u32[]{:S(2)}) copy-start(bf16[2,32,1024]{2,1,0:T(8,128)(2,1)} %queries.1) | copy-start | bytes 393220
  0.0 26.8 %copy-start.2 = (s32[2]{0:T(128)S(1)}, s32[2]{0:T(128)}, u32[]{:S(2)}) copy-start(s32[2]{0:T(128)} %param.12) | copy-start | bytes 28
  1.3 36.6 %collective-permute-start.5 = (bf16[2,2128,128]{2,1,0:T(8,128)(2,1)S(1)}, bf16[2,2128,128]{2,1,0:T(8,128)(2,1)S(1)}, u32[]{:S(2)}, u32[]{:S(2)}) collective-permute-start(bf16[2,2128,128]{2,1,0:T(8,128)(2,1)S(1)} %shard_map.75.s0), channel_id=1, source_target_pairs={{0,32},{8,40},{16,48},{24,56},{32,0},{40,8},{48,16},{56,24},{64,96... | collective-permute-start | bytes 3268616 | tf_op jit(solution)/shard_map/ppermute | solution.py:22
  4.8 27.2 %collective-permute-start = (bf16[2,272,128]{2,1,0:T(8,128)(2,1)S(1)}, bf16[2,272,128]{2,1,0:T(8,128)(2,1)S(1)}, u32[]{:S(2)}, u32[]{:S(2)}) collective-permute-start(bf16[2,272,128]{2,1,0:T(8,128)(2,1)S(1)} %shard_map.73.q), channel_id=1, source_target_pairs={{0,16},{8,24},{16,0},{24,8},{32,48},{40,56},{48,32},{56,40},{64,80... | collective-permute-start | bytes 417800 | tf_op jit(solution)/shard_map/ppermute | solution.py:22
  19.6 7.4 %collective-permute-start.2 = (bf16[272,128]{1,0:T(8,128)(2,1)S(1)}, bf16[272,128]{1,0:T(8,128)(2,1)S(1)}, u32[]{:S(2)}, u32[]{:S(2)}) collective-permute-start(bf16[272,128]{1,0:T(8,128)(2,1)S(1)} %get-tuple-element.31), channel_id=1, source_target_pairs={{0,96},{8,104},{16,112},{24,120},{32,64},{40,72},{48,80},{56,88},{... | collective-permute-start | bytes 208904 | tf_op jit(solution)/shard_map/ppermute | solution.py:22
  23.6 7.4 %collective-permute-start.1 = (bf16[272,128]{1,0:T(8,128)(2,1)S(1)}, bf16[272,128]{1,0:T(8,128)(2,1)S(1)}, u32[]{:S(2)}, u32[]{:S(2)}) collective-permute-start(bf16[272,128]{1,0:T(8,128)(2,1)S(1)} %get-tuple-element.32), channel_id=1, source_target_pairs={{0,96},{8,104},{16,112},{24,120},{32,64},{40,72},{48,80},{56,88},{... | collective-permute-start | bytes 208904 | tf_op jit(solution)/shard_map/ppermute | solution.py:22
  32.0 8.4 %collective-permute-start.3 = (bf16[2,272,128]{2,1,0:T(8,128)(2,1)S(1)}, bf16[2,272,128]{2,1,0:T(8,128)(2,1)S(1)}, u32[]{:S(2)}, u32[]{:S(2)}) collective-permute-start(bf16[2,272,128]{2,1,0:T(8,128)(2,1)S(1)} %collective-permute-done.q), channel_id=1, source_target_pairs={{0,96},{8,104},{16,112},{24,120},{32,64},{40,72},{48,80},{56,88},{... | collective-permute-start | bytes 417800 | tf_op jit(solution)/shard_map/ppermute | solution.py:22
  36.0 4.6 %collective-permute-start.4 = (bf16[2,2128,128]{2,1,0:T(8,128)(2,1)S(1)}, bf16[2,2128,128]{2,1,0:T(8,128)(2,1)S(1)}, u32[]{:S(2)}, u32[]{:S(2)}) collective-permute-start(bf16[2,2128,128]{2,1,0:T(8,128)(2,1)S(1)} %shard_map.75.s0), channel_id=1, source_target_pairs={{0,8},{8,0},{16,24},{24,16},{32,40},{40,32},{48,56},{56,48},{64,72... | collective-permute-start | bytes 3268616 | tf_op jit(solution)/shard_map/ppermute | solution.py:22
  38.0 4.7 %collective-permute-start.6 = (bf16[2,2128,128]{2,1,0:T(8,128)(2,1)S(1)}, bf16[2,2128,128]{2,1,0:T(8,128)(2,1)S(1)}, u32[]{:S(2)}, u32[]{:S(2)}) collective-permute-start(bf16[2,2128,128]{2,1,0:T(8,128)(2,1)S(1)} %collective-permute-done.5.s2), channel_id=1, source_target_pairs={{0,8},{8,0},{16,24},{24,16},{32,40},{40,32},{48,56},{56,48},{64,72... | collective-permute-start | bytes 3268616 | tf_op jit(solution)/shard_map/ppermute | solution.py:22
  46.8 9.1 %collective-permute-start.7 = (bf16[2,272,128]{2,1,0:T(8,128)(2,1)S(1)}, bf16[2,272,128]{2,1,0:T(8,128)(2,1)S(1)}, u32[]{:S(2)}, u32[]{:S(2)}) collective-permute-start(bf16[2,272,128]{2,1,0:T(8,128)(2,1)S(1)} %shard_map.76), channel_id=1, source_target_pairs={{0,96},{8,104},{16,112},{24,120},{32,64},{40,72},{48,80},{56,88},{... | collective-permute-start | bytes 417800 | tf_op jit(solution)/shard_map/ppermute | solution.py:22
  56.3 24.8 %collective-permute-start.9 = (bf16[2,272,128]{2,1,0:T(8,128)(2,1)S(1)}, bf16[2,272,128]{2,1,0:T(8,128)(2,1)S(1)}, u32[]{:S(2)}, u32[]{:S(2)}) collective-permute-start(bf16[2,272,128]{2,1,0:T(8,128)(2,1)S(1)} %shard_map.78), channel_id=1, source_target_pairs={{0,16},{8,24},{16,0},{24,8},{32,48},{40,56},{48,32},{56,40},{64,80... | collective-permute-start | bytes 417800 | tf_op jit(solution)/shard_map/ppermute | solution.py:22
  72.8 8.3 %collective-permute-start.8 = (bf16[2,272,128]{2,1,0:T(8,128)(2,1)S(1)}, bf16[2,272,128]{2,1,0:T(8,128)(2,1)S(1)}, u32[]{:S(2)}, u32[]{:S(2)}) collective-permute-start(bf16[2,272,128]{2,1,0:T(8,128)(2,1)S(1)} %shard_map.79), channel_id=1, source_target_pairs={{0,96},{8,104},{16,112},{24,120},{32,64},{40,72},{48,80},{56,88},{... | collective-permute-start | bytes 417800 | tf_op jit(solution)/shard_map/ppermute | solution.py:22
